TPU v7x, 32 devices: a whole 2x2x4 slice. The times are simulated.
32 devices in a mesh: tm: 4 (over y, core), vert: 8 (over z, x).
Axes of the slice: x: 2, y: 2, z: 4, core: 2. Of those that a mesh axis runs over, the one named last changes fastest.
Arguments:
- features: bfloat16 [32, 4096, 128], P('tm', 'vert'), may hold values from -6 to 6
- tile_cols: int32 [32, 32, 8], P('tm', 'vert'), may hold values from 0 to 31, as said below
- tile_vals: bfloat16 [32, 32, 8, 128, 128], P('tm', 'vert'), may hold values from -0.1875 to 0.1875
- space_weight: bfloat16 [128, 128], replicated, may hold values from -0.5 to 0.5
- positions: bfloat16 [32, 128], replicated, may hold values from -6 to 6
- attn_proj: bfloat16 [128, 384], replicated, may hold values from -0.5 to 0.5
- attn_out: bfloat16 [128, 128], replicated, may hold values from -0.5 to 0.5
- norm_gain: float32 [128], replicated, may hold values from 0.1 to 1.9
- mlp_up: bfloat16 [128, 512], replicated, may hold values from -0.5 to 0.5
- mlp_down: bfloat16 [512, 128], replicated, may hold values from -0.25 to 0.25
Outputs:
- embedded: bfloat16 [32, 4096, 128], P('tm', 'vert')
Inputs may be any that keep to these rules, and one draw needn't show every extreme that they name: `tile_cols`: for each snapshot and each group of 4 consecutive row blocks, the listed column blocks name at most two distinct blocks among those of any one group (blocks c with the same c // 4), and exactly two for some group.
All inputs are finite; a program needn't handle non-finite values.
Results may differ from a plain program's by a relative error of at most 0.0064.
Values may be sent and summed in bfloat16 or wider, within the bound.
No kernel may reach another device: no remote copies, remote signals or barrier semaphores. Data moves between devices by JAX's collectives and lax.ppermute only.
A program may use at most 128 MiB of HBM per device.

v0:
```python
import math

import jax
import jax.numpy as jnp
from jax import lax
from jax.sharding import PartitionSpec as P

HEADS = 16


cap_value = 4.0
norm_eps = 1e-05


def temporal(hidden, positions, attn_proj, attn_out, norm_gain, mlp_up, mlp_down):
    snap_total = hidden.shape[0]
    feature_dim = hidden.shape[2]
    head_count = HEADS
    head_dim = feature_dim // head_count
    mixed_in = (hidden.astype(jnp.float32) + positions.astype(jnp.float32)[:, None, :]).astype(
        jnp.bfloat16
    )
    flat_in = mixed_in.reshape(-1, feature_dim)
    projected = jnp.dot(flat_in, attn_proj, preferred_element_type=jnp.float32).astype(jnp.bfloat16)
    projected = projected.reshape(snap_total, -1, 3, head_count, head_dim)
    query_part = projected[:, :, 0]
    key_part = projected[:, :, 1]
    value_part = projected[:, :, 2]
    scores = jnp.einsum(
        "tvhd,uvhd->vhtu", query_part, key_part, preferred_element_type=jnp.float32
    ) / math.sqrt(head_dim)
    capped = cap_value * jnp.tanh(scores / cap_value)
    causal = jnp.arange(snap_total)[:, None] >= jnp.arange(snap_total)[None, :]
    raised = jnp.where(causal, jnp.exp(capped), 0.0)
    weights = (raised / jnp.sum(raised, axis=-1, keepdims=True)).astype(jnp.bfloat16)
    attended = jnp.einsum(
        "vhtu,uvhd->tvhd", weights, value_part, preferred_element_type=jnp.float32
    ).astype(jnp.bfloat16)
    stream = flat_in.astype(jnp.float32) + jnp.dot(
        attended.reshape(-1, feature_dim), attn_out, preferred_element_type=jnp.float32
    )
    centre = jnp.mean(stream, axis=-1, keepdims=True)
    spread = jnp.mean((stream - centre) ** 2, axis=-1, keepdims=True)
    normed = ((stream - centre) * lax.rsqrt(spread + norm_eps) * norm_gain).astype(jnp.bfloat16)
    expanded = jax.nn.relu(jnp.dot(normed, mlp_up, preferred_element_type=jnp.float32)).astype(
        jnp.bfloat16
    )
    output = stream + jnp.dot(expanded, mlp_down, preferred_element_type=jnp.float32)
    return output.astype(jnp.bfloat16).reshape(snap_total, -1, feature_dim)


def spatial(features, tile_cols, tile_vals, space_weight):
    snap_count, row_count, feature_dim = features.shape
    tile_size = tile_vals.shape[-1]
    block_count = row_count // tile_size
    tile_count = tile_cols.shape[2]
    flat_cols = tile_cols.reshape(snap_count, block_count * tile_count)
    vert_count = lax.axis_size("vert")
    owners = flat_cols // block_count
    local_blk = flat_cols % block_count
    matched = owners[:, :, None] == jnp.arange(vert_count, dtype=jnp.int32)[None, None, :]
    lowest = jnp.min(jnp.where(matched, local_blk[:, :, None], block_count - 1), axis=1)
    highest = jnp.max(jnp.where(matched, local_blk[:, :, None], 0), axis=1)
    wanted = jnp.stack([lowest, highest], axis=2)
    asked_for = lax.all_to_all(wanted, "vert", split_axis=1, concat_axis=1, tiled=True)
    own_blocks = features.reshape(snap_count, block_count, tile_size, feature_dim)
    chosen = jnp.take_along_axis(
        own_blocks, asked_for.reshape(snap_count, vert_count * 2)[:, :, None, None], axis=1
    )
    chosen = chosen.reshape(snap_count, vert_count, 2, tile_size, feature_dim)
    arrived = lax.all_to_all(chosen, "vert", split_axis=1, concat_axis=1, tiled=True)
    arrived = arrived.reshape(snap_count, vert_count * 2, tile_size, feature_dim)
    slot_low = jnp.take_along_axis(lowest, owners, axis=1)
    position = owners * 2 + jnp.where(local_blk == slot_low, 0, 1)
    blocks = jnp.take_along_axis(arrived, position[:, :, None, None], axis=1)
    blocks = blocks.reshape(snap_count, block_count, tile_count, tile_size, feature_dim)
    summed = jnp.einsum(
        "srkij,srkjd->srid", tile_vals, blocks, preferred_element_type=jnp.float32
    ).astype(jnp.bfloat16)
    hidden = jax.nn.relu(
        jnp.dot(summed.reshape(-1, feature_dim), space_weight, preferred_element_type=jnp.float32)
    )
    return hidden.astype(jnp.bfloat16).reshape(snap_count, row_count, feature_dim)


def local(
    features,
    tile_cols,
    tile_vals,
    space_weight,
    positions,
    attn_proj,
    attn_out,
    norm_gain,
    mlp_up,
    mlp_down,
):
    snap_count, row_count, feature_dim = features.shape
    time_count = lax.axis_size("tm")
    hidden = spatial(features, tile_cols, tile_vals, space_weight)
    grouped = hidden.reshape(snap_count, time_count, row_count // time_count, feature_dim)
    arrived = lax.all_to_all(grouped, "tm", split_axis=1, concat_axis=0, tiled=True)
    snap_total = arrived.shape[0]
    timeline = arrived.reshape(snap_total, -1, feature_dim)
    result = temporal(timeline, positions, attn_proj, attn_out, norm_gain, mlp_up, mlp_down)
    result = result.reshape(snap_total, 1, -1, feature_dim)
    embedded = lax.all_to_all(result, "tm", split_axis=0, concat_axis=1, tiled=True)
    return embedded.reshape(snap_count, row_count, feature_dim)


def solution(mesh):
    placed = (
        P("tm", "vert", None),
        P("tm", "vert", None),
        P("tm", "vert", None, None, None),
        P(),
        P(),
        P(),
        P(),
        P(),
        P(),
        P(),
    )
    return jax.shard_map(
        local, mesh=mesh, in_specs=placed, out_specs=P("tm", "vert", None), check_vma=False
    )
```

profile of v0, /device:TPU:5, one launch (start us, length us, event | category | flops | bytes accessed | tf_op | source)
XLA Modules:
  0.0 317.3 jit_solution(16043806983787452429)
XLA Ops:
  1.3 10.7 %all_to_all.34 = s32[8,8,2]{0,2,1:T(2,128)S(1)} all-to-all(s32[8,8,2]{0,2,1:T(2,128)S(1)} %copy.71), channel_id=1, replica_groups=mesh['tm'=4,'vert'=8] {'vert'}, dimensions={1} | all-to-all | bytes 1024 | tf_op jit(solution)/shard_map/all_to_all | solution.py:65
  12.4 3.1 gather_fusion.1
  15.4 2.6 broadcast_select_fusion
  20.5 4.7 %all-to-all-start.1 = ((bf16[8,8,2,128,128]{4,3,2,0,1:T(8,128)(2,1)}), bf16[8,8,2,128,128]{4,3,2,0,1:T(8,128)(2,1)}, u32[]{:S(2)}, u32[]{:S(2)}) async-start(bf16[8,8,2,128,128]{4,3,2,0,1:T(8,128)(2,1)} %copy.74), calls=%async_computation.1 | async-start | bytes 8388608 | tf_op jit(solution)/shard_map/all_to_all | solution.py:71
  27.2 89.2 %all-to-all-done.1 = bf16[8,8,2,128,128]{4,3,2,0,1:T(8,128)(2,1)} async-done(((bf16[8,8,2,128,128]{4,3,2,0,1:T(8,128)(2,1)}), bf16[8,8,2,128,128]{4,3,2,0,1:T(8,128)(2,1)}, u32[]{:S(2)}, u32[]{:S(2)}) %all-to-all-start.1) | async-done | bytes 4194336 | tf_op jit(solution)/shard_map/all_to_all | solution.py:71
  116.4 4.7 %copy.75 = bf16[8,8,2,128,128]{4,3,2,1,0:T(8,128)(2,1)} copy(bf16[8,8,2,128,128]{4,3,2,0,1:T(8,128)(2,1)} %all-to-all-done.1) | data formatting | bytes 8388608 | tf_op jit(solution)/shard_map/all_to_all | solution.py:71
  121.1 12.3 %gather_fusion.2 = bf16[256,128,128]{2,1,0:T(8,128)(2,1)} fusion(bf16[8,16,128,128]{3,2,1,0:T(8,128)(2,1)} %bitcast.76, s32[256]{0:T(256)S(1)} %reshape.348), kind=kCustom, calls=%fused_computation.2 | custom fusion | bytes 16779264 | tf_op jit(solution)/shard_map/jit(take_along_axis)/gather | solution.py:75
  133.3 8.2 %bitcast_convert_fusion = bf16[8,4,128,128]{2,3,1,0:T(8,128)(2,1)S(1)} fusion(bf16[8,4,8,128,128]{4,3,2,1,0:T(8,128)(2,1)} %param.12, bf16[8,4,8,128,128]{4,3,2,1,0:T(8,128)(2,1)} %bitcast.80, pred[8,4,8]{2,1,0:T(4,128)(4,1)S(1)} %compare_and_fusion.1), kind=kOutput, calls=%fused_computation.26 | convolution fusion | flops 1078460416 | bytes 17826048 | tf_op jit(solution)/shard_map/srkij,srkjd->srid/dot_general | solution.py:77
  143.1 6.7 %all-to-all-start.2 = ((bf16[8,4,128,128]{3,2,0,1:T(8,128)(2,1)}), bf16[8,4,128,128]{3,2,0,1:T(8,128)(2,1)S(1)}, u32[]{:S(2)}, u32[]{:S(2)}) async-start(bf16[8,4,128,128]{3,2,0,1:T(8,128)(2,1)} %copy.76), calls=%async_computation.2 | async-start | bytes 2097152 | tf_op jit(solution)/shard_map/all_to_all | solution.py:102
  149.9 12.4 %all-to-all-done.2 = bf16[8,4,128,128]{3,2,0,1:T(8,128)(2,1)S(1)} async-done(((bf16[8,4,128,128]{3,2,0,1:T(8,128)(2,1)}), bf16[8,4,128,128]{3,2,0,1:T(8,128)(2,1)S(1)}, u32[]{:S(2)}, u32[]{:S(2)}) %all-to-all-start.2) | async-done | bytes 1048608 | tf_op jit(solution)/shard_map/all_to_all | solution.py:102
  165.3 4.8 %copy.77 = bf16[4096,384]{0,1:T(8,128)(2,1)} copy(bf16[4096,384]{1,0:T(8,128)(2,1)} %convolution_convert_fusion) | data formatting | bytes 6291456 | tf_op jit(solution)/shard_map/convert_element_type | solution.py:24
  170.1 2.7 copy.90
  174.5 7.2 %copy.88 = bf16[32,128,1,16,8]{0,4,3,1,2:T(8,128)(2,1)} copy(bf16[32,128,1,16,8]{1,0,4,3,2:T(8,128)(2,1)} %get-tuple-element.8) | data formatting | bytes 2097152
  181.7 6.4 %copy.89 = bf16[32,128,1,16,8]{0,4,3,1,2:T(8,128)(2,1)} copy(bf16[32,128,1,16,8]{1,0,4,3,2:T(8,128)(2,1)S(1)} %get-tuple-element.9) | data formatting | bytes 2097152
  188.1 15.3 %fusion.6 = f32[128,16,32,32]{2,3,1,0:T(8,128)} fusion(bf16[32,128,1,16,8]{0,4,3,1,2:T(8,128)(2,1)} %copy.89, bf16[32,128,1,16,8]{0,4,3,1,2:T(8,128)(2,1)} %copy.88), kind=kOutput, calls=%fused_computation.16 | convolution fusion | flops 33554432 | bytes 10485760 | tf_op jit(solution)/shard_map/tvhd,uvhd->vhtu/dot_general | solution.py:29
  203.4 26.7 %copy.81 = f32[128,16,32,32]{0,3,2,1:T(8,128)} copy(f32[128,16,32,32]{2,3,1,0:T(8,128)} %fusion.6) | data formatting | bytes 16777216 | tf_op jit(solution)/shard_map/tvhd,uvhd->vhtu/dot_general | solution.py:29
  230.1 6.7 %fusion.3 = f32[128,16,32]{0,2,1:T(8,128)S(1)} fusion(f32[128,16,32,32]{0,3,2,1:T(8,128)} %copy.81, pred[32,32]{1,0:T(8,128)(4,1)S(1)} %iota_compare_fusion.1), kind=kLoop, calls=%fused_computation.9 | loop fusion | flops 8323072 | bytes 8651776 | tf_op jit(solution)/shard_map/reduce_sum | solution.py:35
  236.8 4.3 %divide_convert_fusion = bf16[128,16,32,32]{0,3,2,1:T(8,128)(2,1)} fusion(f32[128,16,32,32]{0,3,2,1:T(8,128)S(1)} %copy-done.2, f32[128,16,32]{0,2,1:T(8,128)S(1)} %fusion.3, pred[32,32]{1,0:T(8,128)(4,1)S(1)} %iota_compare_fusion.1), kind=kLoop, calls=%fused_computation.4 | loop fusion | flops 10485760 | bytes 12846080 | tf_op jit(solution)/shard_map/convert_element_type | solution.py:35
  241.1 23.1 %copy.82 = bf16[128,16,32,32]{3,2,1,0:T(8,128)(2,1)} copy(bf16[128,16,32,32]{0,3,2,1:T(8,128)(2,1)} %divide_convert_fusion) | data formatting | bytes 8388608 | tf_op jit(solution)/shard_map/convert_element_type | solution.py:35
  264.2 6.4 %copy.87 = bf16[32,128,1,16,8]{0,4,3,1,2:T(8,128)(2,1)} copy(bf16[32,128,1,16,8]{1,0,4,3,2:T(8,128)(2,1)S(1)} %get-tuple-element.7) | data formatting | bytes 2097152
  270.6 14.2 %convert_bitcast_fusion = bf16[32,128,16,8]{0,3,2,1:T(8,128)(2,1)} fusion(bf16[128,16,32,32]{3,2,1,0:T(8,128)(2,1)} %copy.82, bf16[32,128,1,16,8]{0,4,3,1,2:T(8,128)(2,1)} %copy.87), kind=kOutput, calls=%fused_computation.21 | convolution fusion | flops 34078720 | bytes 6291456 | tf_op jit(solution)/shard_map/vhtu,uvhd->tvhd/dot_general | solution.py:36
  284.8 6.3 %copy.83 = bf16[32,128,16,8]{1,0,3,2:T(8,128)(2,1)} copy(bf16[32,128,16,8]{0,3,2,1:T(8,128)(2,1)} %convert_bitcast_fusion) | data formatting | bytes 2097152 | tf_op jit(solution)/shard_map/convert_element_type | solution.py:38
  294.8 3.4 %fusion.5 = bf16[4096,128]{1,0:T(8,128)(2,1)} fusion(f32[4096,128]{1,0:T(8,128)S(1)} %get-tuple-element.13, bf16[512,128]{1,0:T(8,128)(2,1)S(1)} %copy-done.8, bf16[128,512]{1,0:T(8,128)(2,1)S(1)} %copy-done.9, f32[128]{0:T(128)S(1)} %copy-done.10, f32[4096]{0:T(1024)S(1)} %add_rsqrt_fusion, f32[4096]{0:T(1024)S(1)} %broadcast_multiply_fusion), kind=kOutput, calls=%fused_computation.15 | convolution fusion | flops 1081081856 | bytes 3441152 | tf_op jit(solution)/shard_map/dot_general | solution.py:48
  298.2 18.0 %all_to_all.35 = bf16[32,1,128,128]{3,2,1,0:T(8,128)(2,1)S(1)} all-to-all(bf16[32,1,128,128]{3,2,1,0:T(8,128)(2,1)} %bitcast.84), channel_id=1, replica_groups=mesh['tm'=4,'vert'=8] {'tm'}, dimensions={0} | all-to-all | bytes 2097152 | tf_op jit(solution)/shard_map/all_to_all | solution.py:107
  (55 shorter events, 16.9 us)
Async XLA Ops:
  0.0 12.4 %copy-start = (bf16[8,512,128]{2,1,0:T(8,128)(2,1)S(1)}, bf16[8,512,128]{2,1,0:T(8,128)(2,1)}, u32[]{:S(2)}) copy-start(bf16[8,512,128]{2,1,0:T(8,128)(2,1)} %param.10) | copy-start | bytes 3145732
  20.5 4.7 %copy-start.3 = (s32[8,4,8]{2,1,0:T(4,128)S(1)}, s32[8,4,8]{2,1,0:T(4,128)}, u32[]{:S(2)}) copy-start(s32[8,4,8]{2,1,0:T(4,128)} %param.11) | copy-start | bytes 3076
  20.5 95.8 %all-to-all-start.1 = ((bf16[8,8,2,128,128]{4,3,2,0,1:T(8,128)(2,1)}), bf16[8,8,2,128,128]{4,3,2,0,1:T(8,128)(2,1)}, u32[]{:S(2)}, u32[]{:S(2)}) async-start(bf16[8,8,2,128,128]{4,3,2,0,1:T(8,128)(2,1)} %copy.74), calls=%async_computation.1 | async-start | bytes 8388608 | tf_op jit(solution)/shard_map/all_to_all | solution.py:71
  133.3 8.2 %copy-start.5 = (bf16[128,128]{1,0:T(8,128)(2,1)S(1)}, bf16[128,128]{1,0:T(8,128)(2,1)}, u32[]{:S(2)}) copy-start(bf16[128,128]{1,0:T(8,128)(2,1)} %param.13) | copy-start | bytes 98308
  141.6 8.3 %copy-start.7 = (bf16[32,128]{1,0:T(8,128)(2,1)S(1)}, bf16[32,128]{1,0:T(8,128)(2,1)}, u32[]{:S(2)}) copy-start(bf16[32,128]{1,0:T(8,128)(2,1)} %param.14) | copy-start | bytes 24580
  143.1 19.6 %copy-start.4 = (bf16[128,384]{1,0:T(8,128)(2,1)S(1)}, bf16[128,384]{1,0:T(8,128)(2,1)}, u32[]{:S(2)}) copy-start(bf16[128,384]{1,0:T(8,128)(2,1)} %param.15) | copy-start | bytes 294916
  143.1 19.2 %all-to-all-start.2 = ((bf16[8,4,128,128]{3,2,0,1:T(8,128)(2,1)}), bf16[8,4,128,128]{3,2,0,1:T(8,128)(2,1)S(1)}, u32[]{:S(2)}, u32[]{:S(2)}) async-start(bf16[8,4,128,128]{3,2,0,1:T(8,128)(2,1)} %copy.76), calls=%async_computation.2 | async-start | bytes 2097152 | tf_op jit(solution)/shard_map/all_to_all | solution.py:102
  230.1 6.7 %copy-start.2 = (f32[128,16,32,32]{0,3,2,1:T(8,128)S(1)}, f32[128,16,32,32]{0,3,2,1:T(8,128)}, u32[]{:S(2)}) copy-start(f32[128,16,32,32]{0,3,2,1:T(8,128)} %copy.81) | copy-start | bytes 25165828
  284.8 6.3 %copy-start.6 = (bf16[128,128]{1,0:T(8,128)(2,1)S(1)}, bf16[128,128]{1,0:T(8,128)(2,1)}, u32[]{:S(2)}) copy-start(bf16[128,128]{1,0:T(8,128)(2,1)} %param.16) | copy-start | bytes 98308
  291.1 3.7 %copy-start.8 = (bf16[512,128]{1,0:T(8,128)(2,1)S(1)}, bf16[512,128]{1,0:T(8,128)(2,1)}, u32[]{:S(2)}) copy-start(bf16[512,128]{1,0:T(8,128)(2,1)} %param.19) | copy-start | bytes 393220
  291.1 3.7 %copy-start.9 = (bf16[128,512]{1,0:T(8,128)(2,1)S(1)}, bf16[128,512]{1,0:T(8,128)(2,1)}, u32[]{:S(2)}) copy-start(bf16[128,512]{1,0:T(8,128)(2,1)} %param.18) | copy-start | bytes 393220
  291.1 3.7 %copy-start.10 = (f32[128]{0:T(128)S(1)}, f32[128]{0:T(128)}, u32[]{:S(2)}) copy-start(f32[128]{0:T(128)} %param.17) | copy-start | bytes 1540
  294.8 22.5 %copy-start.1 = (bf16[8,512,128]{2,1,0:T(8,128)(2,1)S(1)}, bf16[8,512,128]{2,1,0:T(8,128)(2,1)}, u32[]{:S(2)}) copy-start(bf16[8,512,128]{2,1,0:T(8,128)(2,1)} %param.10) | copy-start | bytes 3145732
where the time goes:
time: 321 us; the launch traced here: 317 us
  local copies, waits for them, and re-layouts  113 us (35%)
  waiting for transfers between devices  102 us (32%)
  matrix products  46.5 us (14%)
  blocking collectives  28.7 us (9%)
  other arithmetic  15.8 us (5%)
  starting transfers between devices  11.4 us (4%)
    all_to_all x1, waiting for transfers between devices, spatial(): lax.all_to_all(chosen, 'vert', split_axis=1, concat_axis=1, tiled=True)  89.2 us
    dot_general x1, local copies, waits for them, and re-layouts, temporal(): jnp.einsum('tvhd,uvhd->vhtu', query_part, key_part, preferred_element_typ...  26.7 us
    convert_element_type x1, local copies, waits for them, and re-layouts, temporal(): (raised / jnp.sum(raised, axis=-1, keepdims=True)).astype(jnp.bfloat16)  23.1 us
    unnamed x26, local copies, waits for them, and re-layouts  22.8 us
    all_to_all x1, blocking collectives, local(): lax.all_to_all(result, 'tm', split_axis=0, concat_axis=1, tiled=True)  18 us
    dot_general x1, matrix products, temporal(): jnp.einsum('tvhd,uvhd->vhtu', query_part, key_part, preferred_element_typ...  15.3 us
    dot_general x1, matrix products, temporal(): jnp.einsum('vhtu,uvhd->tvhd', weights, value_part, preferred_element_type...  14.2 us
    all_to_all x1, waiting for transfers between devices, local(): lax.all_to_all(grouped, 'tm', split_axis=1, concat_axis=0, tiled=True)  12.4 us
  transfers between devices with their start and end apart: 2, of which 2 were waited for; matrix products, arithmetic and copies ran while one was open for 1% of the time, Pallas kernels for 0%

commit v1 on v0

v1 whole, which is shorter than its diff:
```python
import functools
import math

import jax
import jax.numpy as jnp
from jax import lax
from jax.experimental import pallas as pl
from jax.experimental.pallas import tpu as pltpu
from jax.sharding import PartitionSpec as P

HEADS = 16
CAP = 4.0
EPS = 1e-05
VMEM = 56 * 1024 * 1024
BF16 = jnp.bfloat16
F32 = jnp.float32


def split_axis(count):
    inner = 1
    while (inner * 2) * (inner * 2) <= count and count % (inner * 2) == 0:
        inner *= 2
    return count // inner, inner


def dot(a, b):
    return jnp.dot(a, b, preferred_element_type=F32)


def pick_kernel(count, picks, idx_ref, *refs):
    srcs, outs = refs[:count], refs[count:]
    s = pl.program_id(0)
    per_dst = picks
    for d, out in enumerate(outs):
        for j in range(per_dst):
            src = srcs[j // 2]
            out[0, j] = src[0, idx_ref[d, s, j]]


def pick(srcs, idx):
    dsts, snaps, picks = idx.shape
    _, blocks, size, width = srcs[0].shape
    return pl.pallas_call(
        functools.partial(pick_kernel, len(srcs), picks),
        grid_spec=pltpu.PrefetchScalarGridSpec(
            num_scalar_prefetch=1,
            grid=(snaps,),
            in_specs=[pl.BlockSpec((1, blocks, size, width), lambda s, i: (s, 0, 0, 0))] * len(srcs),
            out_specs=[pl.BlockSpec((1, picks, size, width), lambda s, i: (s, 0, 0, 0))] * dsts,
        ),
        out_shape=[jax.ShapeDtypeStruct((snaps, picks, size, width), BF16)] * dsts,
        name="pick_blocks",
    )(idx, *srcs)


def spatial_kernel(count, slot_ref, vals_ref, weight_ref, pos_ref, *refs):
    srcs, out, held = refs[:count], refs[count], refs[count + 1]
    s = pl.program_id(0)
    base = 0
    for src in srcs:
        held[base : base + src.shape[1]] = src[0]
        base += src.shape[1]
    rows, tiles, size, _ = vals_ref.shape[1:]
    position = jnp.broadcast_to(pos_ref[pl.ds(s, 1), :], (size, pos_ref.shape[1])).T
    for r in range(rows):
        left = jnp.concatenate([vals_ref[0, r, k] for k in range(tiles)], axis=1)
        right = jnp.concatenate([held[slot_ref[s, r * tiles + k]] for k in range(tiles)], axis=0)
        summed = dot(left, right).astype(BF16)
        hidden = lax.dot_general(
            weight_ref[...], summed, (((1,), (1,)), ((), ())), preferred_element_type=F32
        )
        hidden = jnp.maximum(hidden, 0.0).astype(BF16).astype(F32)
        out[0, :, r * size : (r + 1) * size] = (hidden + position).astype(BF16)


def spatial(slots, vals, weight_t, pos, srcs):
    snaps, rows, tiles, size, _ = vals.shape
    width = weight_t.shape[0]
    held = sum(a.shape[1] for a in srcs)
    block = lambda a: pl.BlockSpec((1,) + a.shape[1:], lambda s, i: (s,) + (0,) * (a.ndim - 1))
    whole = lambda a: pl.BlockSpec(a.shape, lambda s, i: (0,) * a.ndim)
    return pl.pallas_call(
        functools.partial(spatial_kernel, len(srcs)),
        grid_spec=pltpu.PrefetchScalarGridSpec(
            num_scalar_prefetch=1,
            grid=(snaps,),
            in_specs=[block(vals), whole(weight_t), whole(pos)] + [block(a) for a in srcs],
            out_specs=pl.BlockSpec((1, width, rows * size), lambda s, i: (s, 0, 0)),
            scratch_shapes=[pltpu.VMEM((held, size, width), BF16)],
        ),
        out_shape=jax.ShapeDtypeStruct((snaps, width, rows * size), BF16),
        compiler_params=pltpu.CompilerParams(vmem_limit_bytes=VMEM),
        name="spatial",
    )(slots, vals, weight_t, pos, *srcs)


def temporal_kernel(
    others, me_ref, qkv_ref, proj_ref, gain_ref, up_ref, down_ref, own_ref, *refs
):
    other_refs, out_ref = refs[:others], refs[others]
    q_s, k_s, v_s, att_s = refs[others + 1 :]
    snaps, width, lanes = own_ref.shape
    head_dim = width // HEADS
    me = me_ref[0]
    scale = 1.0 / (CAP * math.sqrt(head_dim))

    def project(ref, base, rows_from):
        for s in range(0, snaps, 2):
            two = jnp.concatenate([ref[s], ref[s + 1]], axis=1)
            got = dot(qkv_ref[rows_from:, :], two).astype(BF16).astype(F32)
            for i in range(2):
                half = got[:, i * lanes : (i + 1) * lanes]
                if rows_from == 0:
                    q_s[s + i] = half[:width] * scale
                k_s[base + s + i] = half[width - rows_from : 2 * width - rows_from]
                v_s[base + s + i] = half[2 * width - rows_from :]

    project(own_ref, 0, 0)
    for i, ref in enumerate(other_refs):

        @pl.when((me ^ (i + 1)) < me)
        def _(i=i, ref=ref):
            project(ref, (i + 1) * snaps, width)

    def pair(q, u, carry):
        total, acc = carry
        k = k_s[u].reshape(head_dim, HEADS, lanes)
        v = v_s[u].reshape(head_dim, HEADS, lanes)
        raw = q[0] * k[0]
        for d in range(1, head_dim):
            raw = raw + q[d] * k[d]
        e = jnp.exp(CAP * jnp.tanh(raw))
        return total + e, tuple(acc[d] + e * v[d] for d in range(head_dim))

    for t in range(snaps):
        q3 = q_s[t].reshape(head_dim, HEADS, lanes)
        q = tuple(q3[d] for d in range(head_dim))
        zero = jnp.zeros((HEADS, lanes), F32)
        carry = (zero, (zero,) * head_dim)
        for u in range(t + 1):
            carry = pair(q, u, carry)
        for i in range(others):
            base = (i + 1) * snaps
            steps = jnp.where((me ^ (i + 1)) < me, snaps // 4, 0)

            def four(n, c, base=base):
                for j in range(4):
                    c = pair(q, base + n * 4 + j, c)
                return c

            carry = lax.fori_loop(0, steps, four, carry)
        total, acc = carry
        inv = 1.0 / total
        att_s[t] = jnp.concatenate([acc[d] * inv for d in range(head_dim)], axis=0).astype(BF16)

    for s in range(0, snaps, 2):
        two = jnp.concatenate([own_ref[s], own_ref[s + 1]], axis=1).astype(F32)
        att = jnp.concatenate([att_s[s], att_s[s + 1]], axis=1)
        stream = two + dot(proj_ref[...], att)
        centre = jnp.mean(stream, axis=0, keepdims=True)
        away = stream - centre
        spread = jnp.mean(away * away, axis=0, keepdims=True)
        gain = jnp.concatenate([gain_ref[...]] * 2, axis=1)
        normed = (away * lax.rsqrt(spread + EPS) * gain).astype(BF16)
        expanded = jnp.maximum(dot(up_ref[...], normed), 0.0).astype(BF16)
        final = stream + dot(down_ref[...], expanded)
        for i in range(2):
            out_ref[s + i] = final[:, i * lanes : (i + 1) * lanes].T.astype(BF16)


def temporal(me, qkv_t, proj_t, gain, up_t, down_t, own, others):
    snaps, width, verts = own.shape
    lanes = 128
    whole = lambda a: pl.BlockSpec(a.shape, lambda g, i: (0,) * a.ndim)
    part = pl.BlockSpec((snaps, width, lanes), lambda g, i: (0, 0, g))
    total = snaps * (len(others) + 1)
    return pl.pallas_call(
        functools.partial(temporal_kernel, len(others)),
        grid_spec=pltpu.PrefetchScalarGridSpec(
            num_scalar_prefetch=1,
            grid=(verts // lanes,),
            in_specs=[whole(a) for a in (qkv_t, proj_t, gain, up_t, down_t)]
            + [part] * (1 + len(others)),
            out_specs=pl.BlockSpec((snaps, lanes, width), lambda g, i: (0, g, 0)),
            scratch_shapes=[
                pltpu.VMEM((snaps, width, lanes), F32),
                pltpu.VMEM((total, width, lanes), F32),
                pltpu.VMEM((total, width, lanes), F32),
                pltpu.VMEM((snaps, width, lanes), BF16),
            ],
        ),
        out_shape=jax.ShapeDtypeStruct((snaps, verts, width), BF16),
        compiler_params=pltpu.CompilerParams(vmem_limit_bytes=VMEM),
        name="temporal",
    )(me, qkv_t, proj_t, gain, up_t, down_t, own, *others)


def local(
    features,
    tile_cols,
    tile_vals,
    space_weight,
    positions,
    attn_proj,
    attn_out,
    norm_gain,
    mlp_up,
    mlp_down,
):
    snaps, verts, width = features.shape
    rows, tiles, size = tile_vals.shape[1:4]
    head_dim = width // HEADS
    times = lax.axis_size("tm")
    count = lax.axis_size("vert")
    outer, inner = split_axis(count)
    me_t = lax.axis_index("tm")
    me_v = lax.axis_index("vert")
    me_o, me_i = me_v // inner, me_v % inner
    blocks = features.reshape(snaps, rows, size, width)

    all_cols = lax.all_gather(tile_cols.reshape(snaps, rows * tiles), "vert", axis=0)
    owner = all_cols // rows
    loc = all_cols % rows
    hit = owner[..., None] == jnp.arange(count, dtype=jnp.int32)
    low = jnp.min(jnp.where(hit, loc[..., None], rows - 1), axis=2)
    high = jnp.max(jnp.where(hit, loc[..., None], 0), axis=2)
    wanted = jnp.stack([low, high], axis=-1)

    cols = tile_cols.reshape(snaps, rows * tiles)
    col_owner, col_loc = cols // rows, cols % rows
    col_o, col_i = col_owner // inner, col_owner % inner
    my_hit = col_owner[..., None] == jnp.arange(count, dtype=jnp.int32)
    my_low = jnp.min(jnp.where(my_hit, col_loc[..., None], rows - 1), axis=1)
    slot_low = jnp.sum(jnp.where(my_hit, my_low[:, None, :], 0), axis=2)
    second = (col_loc != slot_low).astype(jnp.int32)
    near = (col_i ^ me_i) * rows + col_loc
    far = inner * rows + ((col_o ^ me_o) - 1) * (2 * inner) + (col_i ^ me_i) * 2 + second
    slots = jnp.where(col_o == me_o, near, far)

    def send_inner(a, k):
        return lax.ppermute(a, "vert", [(v, v ^ k) for v in range(count)])

    def send_outer(a, k):
        return lax.ppermute(a, "vert", [(v, v ^ (k * inner)) for v in range(count)])

    idx = []
    for k in range(1, outer):
        want = wanted[me_v ^ (k * inner)]
        mine = [want[:, me_v ^ j] for j in range(inner)]
        idx.append(jnp.concatenate(mine, axis=-1))
    idx = jnp.stack(idx)

    layer = [blocks] + [send_inner(blocks, j) for j in range(1, inner)]
    picked = pick(layer, idx)
    arrived = [send_outer(picked[k - 1], k) for k in range(1, outer)]

    pos = lax.dynamic_slice_in_dim(positions, me_t * snaps, snaps, 0).astype(F32)
    mixed = spatial(slots, tile_vals, space_weight.T, pos, layer + arrived)

    others = [
        lax.ppermute(mixed, "tm", [(m, m ^ k) for m in range(times) if m < (m ^ k)])
        for k in range(1, times)
    ]

    by_head = lambda w: w.reshape(width, HEADS, head_dim).transpose(2, 1, 0).reshape(width, width)
    qkv_t = jnp.concatenate(
        [by_head(attn_proj[:, i * width : (i + 1) * width]) for i in range(3)], axis=0
    )
    proj_t = attn_out.reshape(HEADS, head_dim, width).transpose(2, 1, 0).reshape(width, width)
    gain = jnp.broadcast_to(norm_gain[:, None], (width, 128))
    me = me_t.astype(jnp.int32).reshape(1)
    return temporal(me, qkv_t, proj_t, gain, mlp_up.T, mlp_down.T, mixed, others)


def solution(mesh):
    placed = (
        P("tm", "vert", None),
        P("tm", "vert", None),
        P("tm", "vert", None, None, None),
        P(),
        P(),
        P(),
        P(),
        P(),
        P(),
        P(),
    )
    return jax.shard_map(
        local, mesh=mesh, in_specs=placed, out_specs=P("tm", "vert", None), check_vma=False
    )
```

time: 321 us -> 234 us (0.73)
  the two profiles are of different devices: /device:TPU:5 before, /device:TPU:15 now
where the time goes in v1:
time: 234 us; the launch traced here: 233 us
  waiting for transfers between devices  122 us (52%)
  Pallas kernels  46.5 us (20%)
  blocking collectives  39.1 us (17%)
  local copies, waits for them, and re-layouts  10.4 us (4%)
  starting transfers between devices  9.24 us (4%)
  other arithmetic  6.1 us (3%)
    ppermute x3, waiting for transfers between devices, send_outer(): return lax.ppermute(a, 'vert', [(v, v ^ k * inner) for v in range(count)])  79.6 us
    ppermute x3, waiting for transfers between devices, local(): lax.ppermute(mixed, 'tm', [(m, m ^ k) for m in range(times) if m < m ^ k])  42 us
    all_gather x1, blocking collectives, local(): lax.all_gather(tile_cols.reshape(snaps, rows * tiles), 'vert', axis=0)  39.1 us
    pallas_call x1, Pallas kernels, temporal(): pl.pallas_call(functools.partial(temporal_kernel, len(others)), grid_spec...  27.1 us
    pallas_call x1, Pallas kernels, spatial(): pl.pallas_call(functools.partial(spatial_kernel, len(srcs)), grid_spec=pl...  12.6 us
    pallas_call x1, Pallas kernels, pick(): pl.pallas_call(functools.partial(pick_kernel, len(srcs), picks), grid_spe...  6.88 us
    unnamed x26, local copies, waits for them, and re-layouts  5.44 us
    ppermute x3, starting transfers between devices, send_outer(): return lax.ppermute(a, 'vert', [(v, v ^ k * inner) for v in range(count)])  5.12 us
  transfers between devices with their start and end apart: 7, of which 6 were waited for; matrix products, arithmetic and copies ran while one was open for 6% of the time, Pallas kernels for 0%

profile of v1, /device:TPU:15, one launch (start us, length us, event | category | flops | bytes accessed | tf_op | source)
XLA Modules:
  0.0 233.1 jit_solution(15803874479668943736)
XLA Ops:
  0.3 0.8 all_gather_reshape.3
  1.1 39.1 %all_gather.3 = s32[8,8,32]{2,1,0:T(8,128)S(1)} all-gather(s32[1,8,32]{2,1,0:T(8,128)S(1)} %all_gather_reshape.3), channel_id=1, replica_groups=mesh['tm'=4,'vert'=8] {'vert'}, dimensions={0}, use_global_device_ids=true | all-gather | bytes 9216 | tf_op jit(solution)/shard_map/all_gather | solution.py:221
  40.2 2.2 select_reduce_fusion.1
  43.7 1.0 copy-done
  44.6 6.9 %pick_blocks.1 = (bf16[8,4,128,128]{3,2,1,0:T(8,128)(2,1)}, bf16[8,4,128,128]{3,2,1,0:T(8,128)(2,1)}, bf16[8,4,128,128]{3,2,1,0:T(8,128)(2,1)}) custom-call(s32[3,8,4]{2,1,0:T(8,128)} %pad_add_fusion.idx_ref, bf16[8,4,128,128]{3,2,1,0:T(8,128)(2,1)} %bitcast.30, bf16[8,4,128,128]{3,2,1,0:T(8,128)(2,1)} %copy-done), custom_call_target="tpu_custom_call" | custom-call | tf_op jit(solution)/shard_map/pick_blocks/pallas_call | solution.py:43
  51.5 3.0 %collective-permute-start.1 = (bf16[8,4,128,128]{3,2,1,0:T(8,128)(2,1)}, bf16[8,4,128,128]{3,2,1,0:T(8,128)(2,1)S(1)}, u32[]{:S(2)}, u32[]{:S(2)}) collective-permute-start(bf16[8,4,128,128]{3,2,1,0:T(8,128)(2,1)} %get-tuple-element.8), channel_id=1, source_target_pairs={{0,2},{1,3},{2,0},{3,1},{4,6},{5,7},{6,4},{7,5},{8,10},{9,11},{10,... | collective-permute-start | bytes 3145736 | tf_op jit(solution)/shard_map/ppermute | solution.py:244
  54.6 1.9 collective-permute-start.2
  56.6 0.8 reshape.107
  57.4 1.5 copy.85
  58.9 1.3 fusion.18.pos_ref
  61.1 33.5 %collective-permute-done.1.refs_2_ = bf16[8,4,128,128]{3,2,1,0:T(8,128)(2,1)S(1)} collective-permute-done((bf16[8,4,128,128]{3,2,1,0:T(8,128)(2,1)}, bf16[8,4,128,128]{3,2,1,0:T(8,128)(2,1)S(1)}, u32[]{:S(2)}, u32[]{:S(2)}) %collective-permute-start.1) | collective-permute-done | bytes 1048608 | tf_op jit(solution)/shard_map/ppermute | solution.py:244
  94.6 1.1 collective-permute-done.2.refs_3_
  95.7 45.0 %collective-permute-done.3.refs_4_ = bf16[8,4,128,128]{3,2,1,0:T(8,128)(2,1)S(1)} collective-permute-done((bf16[8,4,128,128]{3,2,1,0:T(8,128)(2,1)}, bf16[8,4,128,128]{3,2,1,0:T(8,128)(2,1)S(1)}, u32[]{:S(2)}, u32[]{:S(2)}) %collective-permute-start.3) | collective-permute-done | bytes 1048608 | tf_op jit(solution)/shard_map/ppermute | solution.py:244
  140.7 1.0 copy-done.3
  141.7 12.6 %spatial.1.own_ref = bf16[8,128,512]{2,1,0:T(8,128)(2,1)} custom-call(s32[8,32]{1,0:T(8,128)} %add_select_fusion.6.slot_ref, bf16[8,4,8,128,128]{4,3,2,1,0:T(8,128)(2,1)} %vals_ref.1, bf16[128,128]{1,0:T(8,128)(2,1)} %bitcast.34, f32[8,128]{1,0:T(8,128)} %fusion.18.pos_ref, bf16[8,4,128,128]{3,2,1,0:T(8,128)(2,1)} %bitcast.31, ...), custom_call_target="tpu_custom_call" | custom-call | tf_op jit(solution)/shard_map/spatial/pallas_call | solution.py:82
  154.2 1.3 collective-permute-start.4
  155.5 1.3 collective-permute-start.5
  156.8 1.3 collective-permute-start.6
  158.1 0.8 fusion.19
  163.0 2.6 %collective-permute-done.4.refs_0_ = bf16[8,128,512]{2,1,0:T(8,128)(2,1)S(1)} collective-permute-done((bf16[8,128,512]{2,1,0:T(8,128)(2,1)}, bf16[8,128,512]{2,1,0:T(8,128)(2,1)S(1)}, u32[]{:S(2)}, u32[]{:S(2)}) %collective-permute-start.4) | collective-permute-done | bytes 1048608 | tf_op jit(solution)/shard_map/ppermute | solution.py:261
  165.6 8.9 %collective-permute-done.5.refs_1_ = bf16[8,128,512]{2,1,0:T(8,128)(2,1)S(1)} collective-permute-done((bf16[8,128,512]{2,1,0:T(8,128)(2,1)}, bf16[8,128,512]{2,1,0:T(8,128)(2,1)S(1)}, u32[]{:S(2)}, u32[]{:S(2)}) %collective-permute-start.5) | collective-permute-done | bytes 1048608 | tf_op jit(solution)/shard_map/ppermute | solution.py:261
  174.5 30.5 %collective-permute-done.6.refs_2_ = bf16[8,128,512]{2,1,0:T(8,128)(2,1)S(1)} collective-permute-done((bf16[8,128,512]{2,1,0:T(8,128)(2,1)}, bf16[8,128,512]{2,1,0:T(8,128)(2,1)S(1)}, u32[]{:S(2)}, u32[]{:S(2)}) %collective-permute-start.6) | collective-permute-done | bytes 1048608 | tf_op jit(solution)/shard_map/ppermute | solution.py:261
  205.0 0.8 broadcast_in_dim.56.gain_ref
  206.0 27.1 %temporal.1 = bf16[8,512,128]{2,1,0:T(8,128)(2,1)} custom-call(s32[1]{0:T(128)} %bitcast.me_ref, bf16[384,128]{1,0:T(8,128)(2,1)} %pad_maximum_fusion.qkv_ref, bf16[128,128]{1,0:T(8,128)(2,1)} %copy.89.proj_ref, f32[128,128]{1,0:T(8,128)} %broadcast_in_dim.56.gain_ref, bf16[512,128]{1,0:T(8,128)(2,1)} %bitcast.32, bf16[128,512]{1,0:T(8,128)(2,1)} %bitcast.33, ...), custom_call_target="tpu_custom_call" | custom-call | tf_op jit(solution)/shard_map/temporal/pallas_call | solution.py:177
  (44 shorter events, 6.8 us)
Async XLA Ops:
  0.0 43.7 %collective-permute-start = (bf16[8,4,128,128]{3,2,1,0:T(8,128)(2,1)}, bf16[8,4,128,128]{3,2,1,0:T(8,128)(2,1)S(1)}, u32[]{:S(2)}, u32[]{:S(2)}) collective-permute-start(bf16[8,4,128,128]{3,2,1,0:T(8,128)(2,1)} %bitcast.29), channel_id=1, source_target_pairs={{0,1},{1,0},{2,3},{3,2},{4,5},{5,4},{6,7},{7,6},{8,9},{9,8},{10,11... | collective-permute-start | bytes 3145736 | tf_op jit(solution)/shard_map/ppermute | solution.py:241
  43.7 115.7 %copy-start.7 = (bf16[128,512]{1,0:T(8,128)(2,1)S(1)}, bf16[128,512]{1,0:T(8,128)(2,1)}, u32[]{:S(2)}) copy-start(bf16[128,512]{1,0:T(8,128)(2,1)} %param.18) | copy-start | bytes 393220
  43.7 1.0 copy-start
  51.5 108.6 %copy-start.8 = (bf16[512,128]{1,0:T(8,128)(2,1)S(1)}, bf16[512,128]{1,0:T(8,128)(2,1)}, u32[]{:S(2)}) copy-start(bf16[512,128]{1,0:T(8,128)(2,1)} %param.19) | copy-start | bytes 393220
  51.5 153.5 %copy-start.9 = (f32[128]{0:T(128)S(1)}, f32[128]{0:T(128)}, u32[]{:S(2)}) copy-start(f32[128]{0:T(128)} %param.17) | copy-start | bytes 1540
  51.5 43.1 %collective-permute-start.1 = (bf16[8,4,128,128]{3,2,1,0:T(8,128)(2,1)}, bf16[8,4,128,128]{3,2,1,0:T(8,128)(2,1)S(1)}, u32[]{:S(2)}, u32[]{:S(2)}) collective-permute-start(bf16[8,4,128,128]{3,2,1,0:T(8,128)(2,1)} %get-tuple-element.8), channel_id=1, source_target_pairs={{0,2},{1,3},{2,0},{3,1},{4,6},{5,7},{6,4},{7,5},{8,10},{9,11},{10,... | collective-permute-start | bytes 3145736 | tf_op jit(solution)/shard_map/ppermute | solution.py:244
  54.6 41.1 %collective-permute-start.2 = (bf16[8,4,128,128]{3,2,1,0:T(8,128)(2,1)}, bf16[8,4,128,128]{3,2,1,0:T(8,128)(2,1)S(1)}, u32[]{:S(2)}, u32[]{:S(2)}) collective-permute-start(bf16[8,4,128,128]{3,2,1,0:T(8,128)(2,1)} %get-tuple-element.9), channel_id=1, source_target_pairs={{0,4},{1,5},{2,6},{3,7},{4,0},{5,1},{6,2},{7,3},{8,12},{9,13},{10,... | collective-permute-start | bytes 3145736 | tf_op jit(solution)/shard_map/ppermute | solution.py:244
  56.4 84.3 %collective-permute-start.3 = (bf16[8,4,128,128]{3,2,1,0:T(8,128)(2,1)}, bf16[8,4,128,128]{3,2,1,0:T(8,128)(2,1)S(1)}, u32[]{:S(2)}, u32[]{:S(2)}) collective-permute-start(bf16[8,4,128,128]{3,2,1,0:T(8,128)(2,1)} %get-tuple-element.10), channel_id=1, source_target_pairs={{0,6},{1,7},{2,4},{3,5},{4,2},{5,3},{6,0},{7,1},{8,14},{9,15},{10,... | collective-permute-start | bytes 3145736 | tf_op jit(solution)/shard_map/ppermute | solution.py:244
  94.6 46.1 %copy-start.1 = (bf16[8,4,128,128]{3,2,1,0:T(8,128)(2,1)}, bf16[8,4,128,128]{3,2,1,0:T(8,128)(2,1)S(1)}, u32[]{:S(2)}) copy-start(bf16[8,4,128,128]{3,2,1,0:T(8,128)(2,1)S(1)} %collective-permute-done.1.refs_2_) | copy-start | bytes 3145732
  95.7 45.0 %copy-start.2 = (bf16[8,4,128,128]{3,2,1,0:T(8,128)(2,1)}, bf16[8,4,128,128]{3,2,1,0:T(8,128)(2,1)S(1)}, u32[]{:S(2)}) copy-start(bf16[8,4,128,128]{3,2,1,0:T(8,128)(2,1)S(1)} %collective-permute-done.2.refs_3_) | copy-start | bytes 3145732
  140.7 1.0 copy-start.3
  154.2 11.4 %collective-permute-start.4 = (bf16[8,128,512]{2,1,0:T(8,128)(2,1)}, bf16[8,128,512]{2,1,0:T(8,128)(2,1)S(1)}, u32[]{:S(2)}, u32[]{:S(2)}) collective-permute-start(bf16[8,128,512]{2,1,0:T(8,128)(2,1)} %spatial.1.own_ref), channel_id=1, source_target_pairs={{0,8},{16,24},{1,9},{17,25},{2,10},{18,26},{3,11},{19,27},{4,12},{... | collective-permute-start | bytes 3145736 | tf_op jit(solution)/shard_map/ppermute | solution.py:261
  155.5 19.0 %collective-permute-start.5 = (bf16[8,128,512]{2,1,0:T(8,128)(2,1)}, bf16[8,128,512]{2,1,0:T(8,128)(2,1)S(1)}, u32[]{:S(2)}, u32[]{:S(2)}) collective-permute-start(bf16[8,128,512]{2,1,0:T(8,128)(2,1)} %spatial.1.own_ref), channel_id=1, source_target_pairs={{0,16},{8,24},{1,17},{9,25},{2,18},{10,26},{3,19},{11,27},{4,20},{... | collective-permute-start | bytes 3145736 | tf_op jit(solution)/shard_map/ppermute | solution.py:261
  156.8 48.2 %collective-permute-start.6 = (bf16[8,128,512]{2,1,0:T(8,128)(2,1)}, bf16[8,128,512]{2,1,0:T(8,128)(2,1)S(1)}, u32[]{:S(2)}, u32[]{:S(2)}) collective-permute-start(bf16[8,128,512]{2,1,0:T(8,128)(2,1)} %spatial.1.own_ref), channel_id=1, source_target_pairs={{0,24},{8,16},{1,25},{9,17},{2,26},{10,18},{3,27},{11,19},{4,28},{... | collective-permute-start | bytes 3145736 | tf_op jit(solution)/shard_map/ppermute | solution.py:261
  165.6 40.2 %copy-start.4 = (bf16[8,128,512]{2,1,0:T(8,128)(2,1)}, bf16[8,128,512]{2,1,0:T(8,128)(2,1)S(1)}, u32[]{:S(2)}) copy-start(bf16[8,128,512]{2,1,0:T(8,128)(2,1)S(1)} %collective-permute-done.4.refs_0_) | copy-start | bytes 3145732
  174.5 31.3 %copy-start.5 = (bf16[8,128,512]{2,1,0:T(8,128)(2,1)}, bf16[8,128,512]{2,1,0:T(8,128)(2,1)S(1)}, u32[]{:S(2)}) copy-start(bf16[8,128,512]{2,1,0:T(8,128)(2,1)S(1)} %collective-permute-done.5.refs_1_) | copy-start | bytes 3145732
  205.0 1.0 copy-start.6

commit v2 on v0

v2 whole, which is shorter than its diff:
```python
import functools
import math

import jax
import jax.numpy as jnp
from jax import lax
from jax.experimental import pallas as pl
from jax.experimental.pallas import tpu as pltpu
from jax.sharding import PartitionSpec as P

HEADS = 16
CAP = 4.0
EPS = 1e-05
VMEM = 56 * 1024 * 1024
BF16 = jnp.bfloat16
F32 = jnp.float32
after = lax.optimization_barrier


def split_axis(count):
    inner = 1
    while (inner * 2) * (inner * 2) <= count and count % (inner * 2) == 0:
        inner *= 2
    return count // inner, inner


def dot(a, b):
    return jnp.dot(a, b, preferred_element_type=F32)


def dot_nt(a, b):
    return lax.dot_general(a, b, (((1,), (1,)), ((), ())), preferred_element_type=F32)


def whole(a):
    return pl.BlockSpec(a.shape, lambda *i: (0,) * len(a.shape))


def cost(us):
    return pl.CostEstimate(flops=int(us * 1.15e9), bytes_accessed=1024, transcendentals=0)


def prepare_kernel(rows, count, inner, forward, at_ref, *refs):
    cols_ref, pos_ref, qkv_ref, proj_ref, gain_ref, up_ref, down_ref, space_ref = refs[:8]
    want_o, slot_o, pos_o, qkv_o, proj_o, gain_o, up_o, down_o, space_o, pos_s = refs[8:]
    me = at_ref[0]
    cols = cols_ref[...]
    rel = (cols // rows) ^ me
    loc = cols % rows
    slots = jnp.zeros_like(cols)
    for k in range(count):
        hit = rel == k
        least = lambda a: jnp.min(jnp.min(a, axis=2, keepdims=True), axis=1, keepdims=True)
        low = least(jnp.where(hit, loc, rows - 1))
        high = -least(jnp.where(hit, -loc, 0))
        want_o[:, :, 2 * k : 2 * k + 1] = low
        want_o[:, :, 2 * k + 1 : 2 * k + 2] = high
        second = jnp.where(loc == low, 0, 1)
        if forward:
            o = me // inner
            middle = jnp.where((o == 1) | (o == 2), 1, 0)
            half = (k // 2 - 2) * 2
            if k in (0, 2):
                at = (k // 2) * rows + loc
            elif k in (1, 3):
                at = 4 * rows + (k // 2) * 2 + second
            elif k % 2 == 0:
                at = jnp.where(middle == 1, (3 if k == 4 else 2) * rows + loc, 6 * rows + half + second)
            else:
                at = (7 - 2 * middle) * rows + half + second
        elif k < inner:
            at = k * rows + loc
        else:
            at = inner * rows + (k - inner) * 2 + second
        slots = jnp.where(hit, at, slots)
    slot_o[...] = slots

    width = proj_ref.shape[0]
    head_dim = width // HEADS
    snaps = pos_o.shape[0]
    pos_s[...] = pos_ref[...].astype(F32)
    pos_o[...] = pos_s[pl.ds(at_ref[1] * snaps, snaps), :]
    to = lax.broadcasted_iota(jnp.int32, (width, width), 0)
    source = lax.broadcasted_iota(jnp.int32, (width, width), 1)
    by_head = jnp.where((to % HEADS) * head_dim + to // HEADS == source, 1.0, 0.0).astype(BF16)
    for i in range(3):
        part = slice(i * width, (i + 1) * width)
        qkv_o[part, :] = dot_nt(by_head, qkv_ref[:, part]).astype(BF16)
    flip = lambda a: a.astype(F32).T.astype(BF16)
    proj_o[...] = dot_nt(flip(proj_ref[...]), by_head).astype(BF16)
    gain_o[...] = jnp.broadcast_to(gain_ref[...], gain_o.shape).T
    for i in range(up_ref.shape[1] // width):
        part = slice(i * width, (i + 1) * width)
        up_o[part, :] = flip(up_ref[:, part])
        down_o[:, part] = flip(down_ref[part, :])
    space_o[...] = flip(space_ref[...])


def prepare(at, cols, positions, weights, rows, count, inner, forward):
    snaps = cols.shape[0]
    qkv, proj, gain, up, down, space = weights
    width = proj.shape[0]
    ins = [cols, positions, qkv, proj, gain.reshape(1, width), up, down, space]
    shape = jax.ShapeDtypeStruct
    outs = [
        shape((snaps, 1, 2 * count), jnp.int32),
        shape(cols.shape, jnp.int32),
        shape((snaps, width), F32),
        shape((3 * width, width), BF16),
        shape((width, width), BF16),
        shape((width, width), F32),
        shape((up.shape[1], width), BF16),
        shape((width, down.shape[0]), BF16),
        shape((width, width), BF16),
    ]
    return pl.pallas_call(
        functools.partial(prepare_kernel, rows, count, inner, forward),
        grid_spec=pltpu.PrefetchScalarGridSpec(
            num_scalar_prefetch=1,
            grid=(1,),
            in_specs=[whole(a) for a in ins],
            out_specs=[whole(a) for a in outs],
            scratch_shapes=[pltpu.VMEM(positions.shape, F32)],
        ),
        out_shape=outs,
        compiler_params=pltpu.CompilerParams(vmem_limit_bytes=VMEM),
        name="prepare",
    )(at, *ins)


def pick_kernel(jobs, wants, offsets, *refs):
    outs = refs[len(refs) - len(jobs) :]
    want_refs, srcs = refs[:wants], refs[wants : len(refs) - len(jobs)]
    for (which, pairs, lo, _), out in zip(jobs, outs):
        for s in range(out.shape[0]):
            for j, (src, rel) in enumerate(pairs):
                for i in range(2):
                    block = want_refs[which][lo + s, 0, 2 * rel + i]
                    out[s, 2 * j + i] = srcs[src][lo + s - offsets[src], block]


def pick(srcs, offsets, wants, jobs):
    size, width = srcs[0].shape[2:]
    shapes = [
        jax.ShapeDtypeStruct((hi - lo, 2 * len(pairs), size, width), BF16)
        for _, pairs, lo, hi in jobs
    ]
    return pl.pallas_call(
        functools.partial(pick_kernel, jobs, len(wants), offsets),
        grid_spec=pltpu.PrefetchScalarGridSpec(
            num_scalar_prefetch=len(wants),
            grid=(1,),
            in_specs=[whole(a) for a in srcs],
            out_specs=[whole(a) for a in shapes],
        ),
        out_shape=shapes,
        compiler_params=pltpu.CompilerParams(vmem_limit_bytes=VMEM),
        cost_estimate=cost(3),
        name="pick_blocks",
    )(*wants, *srcs)


def spatial_kernel(start, offsets, slot_ref, vals_ref, weight_ref, pos_ref, *refs):
    srcs, (*outs, held, vals, sums, held_sem, vals_sem) = refs[: len(offsets)], refs[len(offsets) :]
    snaps, rows, tiles, size, _ = vals.shape
    each = rows // len(outs)
    copies, arriving = [], []
    for src, offset in zip(srcs, offsets):
        for first in range(0, src.shape[1], rows):
            unit = len(copies)
            span = slice(start - offset, start - offset + snaps)
            copies.append(
                pltpu.make_async_copy(
                    src.at[span, first : first + rows], held.at[unit], held_sem.at[unit]
                )
            )
    for s in range(snaps):
        arriving.append(pltpu.make_async_copy(vals_ref.at[start + s], vals.at[s], vals_sem.at[s]))
    for copy in arriving[:1] + copies + arriving[1:]:
        copy.start()
    for copy in copies:
        copy.wait()
    for s in range(snaps):
        arriving[s].wait()
        for r in range(rows):
            left = jnp.concatenate([vals[s, r, k] for k in range(tiles)], axis=1)
            right = []
            for k in range(tiles):
                slot = slot_ref[start + s, r, k]
                right.append(held[slot // rows, s, slot % rows])
            summed = dot(left, jnp.concatenate(right, axis=0)).astype(BF16)
            sums[(s * rows + r) * size : (s * rows + r + 1) * size, :] = summed
    for s in range(snaps):
        pos = pos_ref[start + s : start + s + 1, :]
        position = jnp.broadcast_to(pos, (size, pos.shape[1])).T
        some = sums[s * rows * size : (s + 1) * rows * size, :]
        hidden = jnp.maximum(dot_nt(weight_ref[...], some), 0.0).astype(BF16).astype(F32)
        for r in range(rows):
            mixed = hidden[:, r * size : (r + 1) * size] + position
            outs[r // each][r % each, s] = mixed.astype(BF16)


def spatial(slots, vals, start, stop, weight_t, pos, srcs, parts):
    rows, tiles, size, _ = vals.shape[1:]
    snaps = stop - start
    width = weight_t.shape[0]
    units = sum(a.shape[1] for a, _ in srcs) // rows
    anywhere = pl.BlockSpec(memory_space=pl.ANY)
    out = jax.ShapeDtypeStruct((rows // parts, snaps, width, size), BF16)
    return pl.pallas_call(
        functools.partial(spatial_kernel, start, [first for _, first in srcs]),
        grid_spec=pltpu.PrefetchScalarGridSpec(
            num_scalar_prefetch=1,
            grid=(1,),
            in_specs=[anywhere, whole(weight_t), whole(pos)] + [anywhere] * len(srcs),
            out_specs=[whole(out)] * parts,
            scratch_shapes=[
                pltpu.VMEM((units, snaps, rows, size, width), BF16),
                pltpu.VMEM((snaps, rows, tiles, size, size), BF16),
                pltpu.VMEM((snaps * rows * size, width), BF16),
                pltpu.SemaphoreType.DMA((units,)),
                pltpu.SemaphoreType.DMA((snaps,)),
            ],
        ),
        out_shape=[out] * parts,
        compiler_params=pltpu.CompilerParams(vmem_limit_bytes=VMEM),
        cost_estimate=cost(2 * snaps),
        name="spatial",
    )(slots, vals, weight_t, pos, *[a for a, _ in srcs])


def temporal_kernel(sizes, others, me_ref, qkv_ref, proj_ref, gain_ref, up_ref, down_ref, *refs):
    count = 1 + others
    arrays = refs[: count * len(sizes)]
    out_ref, k_s, v_s, q_s, acc_s, total_s, att_s = refs[-7:]
    snaps = sum(sizes)
    width, lanes = arrays[0].shape[2:]
    head_dim = width // HEADS
    me = me_ref[0]
    scale = 1.0 / (CAP * math.sqrt(head_dim))
    steep = CAP * math.log2(math.e)

    def held(i):
        return [arrays[c * count + i][0, s] for c, n in enumerate(sizes) for s in range(n)]

    def project(i):
        skip = 0 if i == 0 else width
        base = (me ^ i) * snaps
        found = held(i)
        for first in range(0, snaps, 4):
            some = found[first : first + 4]
            got = dot(qkv_ref[skip:, :], jnp.concatenate(some, axis=1)).astype(BF16).astype(F32)
            for j in range(len(some)):
                part = got[:, j * lanes : (j + 1) * lanes]
                if i == 0:
                    q_s[first + j] = part[:width] * scale
                k_s[base + first + j] = part[width - skip : 2 * width - skip]
                v_s[base + first + j] = part[2 * width - skip :]

    project(0)
    for i in range(1, count):
        pl.when((me ^ i) < me)(functools.partial(project, i))

    def attend(at, keys, fresh=False):
        q = [q_s[at, d * HEADS : (d + 1) * HEADS] for d in range(head_dim)]
        total, acc = None, None
        for u in keys:
            row = lambda ref, d: ref[u, d * HEADS : (d + 1) * HEADS]
            raw = q[0] * row(k_s, 0)
            for d in range(1, head_dim):
                raw = raw + q[d] * row(k_s, d)
            e = jnp.exp2(steep * jnp.tanh(raw))
            if total is None:
                total, acc = e, [e * row(v_s, d) for d in range(head_dim)]
            else:
                total = total + e
                acc = [acc[d] + e * row(v_s, d) for d in range(head_dim)]
        for d in range(head_dim):
            span = slice(d * HEADS, (d + 1) * HEADS)
            acc_s[at, span] = acc[d] if fresh else acc_s[at, span] + acc[d]
        total_s[at] = total if fresh else total_s[at] + total

    for s in range(snaps):
        attend(s, [me * snaps + j for j in range(s + 1)], fresh=True)

    def earlier(m, none):
        for at in range(snaps):
            attend(at, [m * snaps + j for j in range(snaps)])
        return none

    lax.fori_loop(0, me, earlier, 0)

    mine = held(0)
    for at in range(snaps):
        inv = 1.0 / total_s[at]
        for d in range(head_dim):
            span = slice(d * HEADS, (d + 1) * HEADS)
            att_s[span, at * lanes : (at + 1) * lanes] = (acc_s[at, span] * inv).astype(BF16)
    half = snaps // 2
    for h in range(2):
        span = slice(h * half * lanes, (h + 1) * half * lanes)
        base = jnp.concatenate(mine[h * half : (h + 1) * half], axis=1).astype(F32)
        stream = base + dot(proj_ref[...], att_s[:, span])
        centre = jnp.mean(stream, axis=0, keepdims=True)
        away = stream - centre
        spread = jnp.mean(away * away, axis=0, keepdims=True)
        gain = jnp.concatenate([gain_ref[...]] * half, axis=1)
        normed = (away * lax.rsqrt(spread + EPS) * gain).astype(BF16)
        expanded = jnp.maximum(dot(up_ref[...], normed), 0.0).astype(BF16)
        out = stream + dot(down_ref[...], expanded)
        for i in range(half):
            out_ref[h * half + i] = out[:, i * lanes : (i + 1) * lanes].T.astype(BF16)


def temporal(me, weights, chunks, first, groups, total, so_far):
    width, lanes = chunks[0][0].shape[2:]
    count = len(chunks[0])
    sizes = [chunk[0].shape[1] for chunk in chunks]
    snaps = sum(sizes)

    def part(a):
        at = first if a.shape[0] == total else 0
        return pl.BlockSpec((1,) + a.shape[1:], lambda g, i: (g + at, 0, 0, 0))

    parts = [a for chunk in chunks for a in chunk]
    extra = [] if so_far is None else [so_far]
    return pl.pallas_call(
        functools.partial(temporal_kernel, sizes, count - 1),
        grid_spec=pltpu.PrefetchScalarGridSpec(
            num_scalar_prefetch=1,
            grid=(groups,),
            in_specs=[whole(a) for a in weights]
            + [part(a) for a in parts]
            + [pl.BlockSpec(memory_space=pl.ANY)] * len(extra),
            out_specs=pl.BlockSpec((snaps, lanes, width), lambda g, i: (0, g + first, 0)),
            scratch_shapes=[
                pltpu.VMEM((snaps * count, width, lanes), F32),
                pltpu.VMEM((snaps * count, width, lanes), F32),
                pltpu.VMEM((snaps, width, lanes), F32),
                pltpu.VMEM((snaps, width, lanes), F32),
                pltpu.VMEM((snaps, HEADS, lanes), F32),
                pltpu.VMEM((width, snaps * lanes), BF16),
            ],
        ),
        out_shape=jax.ShapeDtypeStruct((snaps, total * lanes, width), BF16),
        input_output_aliases={1 + len(weights) + len(parts): 0} if extra else {},
        compiler_params=pltpu.CompilerParams(vmem_limit_bytes=VMEM),
        cost_estimate=cost(10),
        name="temporal",
    )(me, *weights, *parts, *extra)


def send(a, k):
    return lax.ppermute(a, "vert", [(v, v ^ k) for v in range(lax.axis_size("vert"))])


def exchange_direct(blocks, want, inner):
    snaps = blocks.shape[0]
    count = lax.axis_size("vert")
    outer = count // inner
    wants = [send(want, k * inner) for k in range(1, outer)]
    layer = [blocks] + [send(blocks, j) for j in range(1, inner)]
    jobs = [
        (k - 1, [(j, k * inner + j) for j in range(inner)], 0, snaps) for k in range(1, outer)
    ]
    picked = pick(layer, [0] * inner, wants, jobs)
    arrived = [send(picked[k - 1], k * inner) for k in range(1, outer)]
    return [(0, snaps, [(a, 0) for a in layer + arrived])]


def exchange_forward(blocks, want):
    snaps = blocks.shape[0]
    layers = lambda pairs, x=0: [(a * 2 + i, b * 2 + (i ^ x)) for a, b in pairs for i in range(2)]
    go = lambda a, pairs, x=0: lax.ppermute(a, "vert", layers(pairs, x))
    cross = [(1, 2), (2, 1)]
    skip = [(0, 2), (3, 1)]
    ends = [(2, 3), (1, 0)]
    back = [(3, 2), (0, 1)]

    cut = snaps // 2
    first, rest = blocks[:cut], blocks[cut:]
    p1, p2, near = go(first, cross), go(first, skip), send(first, 2)
    wants = [send(want, 1), go(want, back), go(want, back, 1)]
    rest, *wants = after((rest, *wants))

    def forward(own, near, p1, p2, lo, hi):
        srcs = [own, near, p1, p2]
        offsets = [0 if a.shape[0] == snaps else lo for a in srcs]
        jobs = [
            (1, [(2, 4), (3, 6)], lo, hi),
            (2, [(2, 5), (3, 7)], lo, hi),
            (0, [(0, 1), (1, 3)], lo, hi),
            (0, [(3, 5), (2, 7)], lo, hi),
        ]
        f0, f1, x1, x2 = pick(srcs, offsets, wants, jobs)
        f0, f1 = go(f0, ends), go(f1, ends, 1)
        x1, x2 = send(x1, 1), go(x2, [(1, 1), (2, 2)], 1)
        return (lo, hi, list(zip(srcs, offsets)) + [(a, lo) for a in (x1, x2, f0, f1)])

    parts = [forward(first, near, p1, p2, 0, cut)]
    q1, q2, far = go(rest, cross), go(rest, skip), send(rest, 2)
    return parts + [forward(rest, far, q1, q2, cut, snaps)]


def gather_times(own):
    times = lax.axis_size("tm")
    got = [own] + [None] * (times - 1)
    for k in range(1, times):
        if k == 1 or k % 2 == 0:
            pairs = [(m, m ^ k) for m in range(times) if m < (m ^ k)]
            got[k] = lax.ppermute(own, "tm", pairs)
    return got


def pass_on(got, late):
    times = lax.axis_size("tm")
    got = list(got)
    for k in range(3, times, 2):
        pairs = [(m, m ^ 1) for m in range(times) if (m ^ (k - 1)) < m]
        got[k - 1], _ = after((got[k - 1], late))
        got[k] = lax.ppermute(got[k - 1], "tm", pairs)
    return got


def local(
    features,
    tile_cols,
    tile_vals,
    space_weight,
    positions,
    attn_proj,
    attn_out,
    norm_gain,
    mlp_up,
    mlp_down,
):
    snaps, verts, width = features.shape
    rows, tiles, size = tile_vals.shape[1:4]
    count = lax.axis_size("vert")
    outer, inner = split_axis(count)
    me_t = lax.axis_index("tm").astype(jnp.int32)
    me_v = lax.axis_index("vert").astype(jnp.int32)
    blocks = features.reshape(snaps, rows, size, width)

    forward = (outer, inner) == (4, 2)
    weights = (attn_proj, attn_out, norm_gain, mlp_up, mlp_down, space_weight)
    want, slots, pos, *weights, space_t = prepare(
        jnp.stack([me_v, me_t]), tile_cols, positions, weights, rows, count, inner, forward
    )
    me = me_t.reshape(1)
    parts = exchange_forward(blocks, want) if forward else exchange_direct(blocks, want, inner)

    started = []
    for start, stop, srcs in parts[:-1]:
        (own,) = spatial(slots, tile_vals, start, stop, space_t, pos, srcs, 1)
        started.append(gather_times(own))
    start, stop, srcs = parts[-1]
    halves = 2 if rows % 2 == 0 else 1
    owns = spatial(slots, tile_vals, start, stop, space_t, pos, srcs, halves)
    done = [pass_on(got, owns[0]) for got in started]
    last = [gather_times(own) for own in owns]
    out = None
    for h, got in enumerate(last):
        chunks = done + [pass_on(got, owns[0])]
        groups = owns[h].shape[0]
        out = temporal(me, weights, chunks, h * groups, groups, rows, out)
    return out


def solution(mesh):
    placed = (
        P("tm", "vert", None),
        P("tm", "vert", None),
        P("tm", "vert", None, None, None),
        P(),
        P(),
        P(),
        P(),
        P(),
        P(),
        P(),
    )
    return jax.shard_map(
        local, mesh=mesh, in_specs=placed, out_specs=P("tm", "vert", None), check_vma=False
    )
```

time: 321 us -> 144 us (0.45)
  local copies, waits for them, and re-layouts: 113 us -> 7.66 us
  waiting for transfers between devices: 102 us -> 35.4 us
  Pallas kernels: 0 us -> 49.6 us
  matrix products: 46.5 us -> 0 us
  starting transfers between devices: 11.4 us -> 48.8 us
  blocking collectives: 28.7 us -> 0 us
  other arithmetic: 15.8 us -> 0.67 us
    all_to_all x2 -> x0, waiting for transfers between devices: 102 us -> none  [the longest x1 89.2 us: spatial(): lax.all_to_all(chosen, 'vert', split_axis=1, concat_axis=1, tiled=True)]
    pallas_call x0 -> x7, Pallas kernels: none -> 49.6 us  [the longest x2 23.3 us: temporal(): pl.pallas_call(functools.partial(temporal_kernel, sizes, count - 1), grid...]
    ppermute x0 -> x26, starting transfers between devices: none -> 48.8 us  [the longest x12 21.9 us: exchange_forward(): go = lambda a, pairs, x=0: lax.ppermute(a, 'vert', layers(pairs, x))]
    dot_general x7 -> x0, matrix products: 46.5 us -> none  [the longest x1 15.3 us: temporal(): jnp.einsum('tvhd,uvhd->vhtu', query_part, key_part, preferred_element_typ...]
    ppermute x0 -> x26, waiting for transfers between devices: none -> 35.4 us  [the longest x12 31.1 us: exchange_forward(): go = lambda a, pairs, x=0: lax.ppermute(a, 'vert', layers(pairs, x))]
    convert_element_type x3 -> x0, local copies, waits for them, and re-layouts: 34.1 us -> none  [the longest x1 23.1 us: temporal(): (raised / jnp.sum(raised, axis=-1, keepdims=True)).astype(jnp.bfloat16)]
    all_to_all x2 -> x0, blocking collectives: 28.7 us -> none  [the longest x1 18 us: local(): lax.all_to_all(result, 'tm', split_axis=0, concat_axis=1, tiled=True)]
    dot_general x1 -> x0, local copies, waits for them, and re-layouts: 26.7 us -> none  [temporal(): jnp.einsum('tvhd,uvhd->vhtu', query_part, key_part, preferred_element_typ...]
  transfers between devices with their start and end apart: 2 -> 26, of which waited for: 2 -> 7; matrix products, arithmetic and copies ran while one was open for 1% -> 0% of each run, Pallas kernels for 0% -> 27%
where the time goes in v2:
time: 144 us; the launch traced here: 143 us
  Pallas kernels  49.6 us (34%)
  starting transfers between devices  48.8 us (34%)
  waiting for transfers between devices  35.4 us (25%)
  local copies, waits for them, and re-layouts  7.66 us (5%)
    ppermute x12, waiting for transfers between devices, exchange_forward(): go = lambda a, pairs, x=0: lax.ppermute(a, 'vert', layers(pairs, x))  31.1 us
    pallas_call x2, Pallas kernels, temporal(): pl.pallas_call(functools.partial(temporal_kernel, sizes, count - 1), grid...  23.3 us
    ppermute x12, starting transfers between devices, exchange_forward(): go = lambda a, pairs, x=0: lax.ppermute(a, 'vert', layers(pairs, x))  21.9 us
    pallas_call x2, Pallas kernels, spatial(): pl.pallas_call(functools.partial(spatial_kernel, start, [first for _, fir...  15.3 us
    ppermute x3, starting transfers between devices, pass_on(): got[k] = lax.ppermute(got[k - 1], 'tm', pairs)  13 us
    pallas_call x2, Pallas kernels, pick(): pl.pallas_call(functools.partial(pick_kernel, jobs, len(wants), offsets),...  7.79 us
    ppermute x6, starting transfers between devices, gather_times(): got[k] = lax.ppermute(own, 'tm', pairs)  7.73 us
    unnamed x56, local copies, waits for them, and re-layouts  6.39 us
  transfers between devices with their start and end apart: 26, of which 7 were waited for; matrix products, arithmetic and copies ran while one was open for 0% of the time, Pallas kernels for 27%

profile of v2, /device:TPU:5, one launch (start us, length us, event | category | flops | bytes accessed | tf_op | source)
XLA Modules:
  0.0 142.7 jit_solution(2854853095996892755)
XLA Ops:
  1.3 1.4 collective-permute-start
  3.4 5.5 %collective-permute-start.2 = (bf16[4,4,128,128]{3,2,1,0:T(8,128)(2,1)S(1)}, bf16[4,4,128,128]{3,2,1,0:T(8,128)(2,1)S(1)}, u32[]{:S(2)}, u32[]{:S(2)}) collective-permute-start(bf16[4,4,128,128]{3,2,1,0:T(8,128)(2,1)S(1)} %bitcast.12), channel_id=1, source_target_pairs={{0,4},{1,5},{6,2},{7,3},{8,12},{9,13},{14,10},{15,11},{16,20},{17,... | collective-permute-start | bytes 1572872 | tf_op jit(solution)/shard_map/ppermute | solution.py:374
  9.5 3.2 %prepare.1 = (s32[8,1,16]{2,1,0:T(1,128)}, s32[8,4,8]{2,1,0:T(4,128)}, f32[8,128]{1,0:T(8,128)}, bf16[384,128]{1,0:T(8,128)(2,1)}, bf16[128,128]{1,0:T(8,128)(2,...) custom-call(s32[2]{0:T(128)} %pad_add_fusion.at_ref, ...), custom_call_target="tpu_custom_call" | custom-call | tf_op jit(solution)/shard_map/prepare/pallas_call | solution.py:116
  13.9 1.5 %collective-permute-start.4 = (s32[8,1,16]{2,1,0:T(1,128)}, s32[8,1,16]{2,1,0:T(1,128)S(1)}, u32[]{:S(2)}, u32[]{:S(2)}) collective-permute-start(s32[8,1,16]{2,1,0:T(1,128)} %get-tuple-element.39), channel_id=1, source_target_pairs={{6,4},{7,5},{0,2},{1,3},{14,12},{15,13},{8,10},{9,11},{22,20},{23,... | collective-permute-start | bytes 1544 | tf_op jit(solution)/shard_map/ppermute | solution.py:374
  15.4 2.7 %collective-permute-start.5 = (s32[8,1,16]{2,1,0:T(1,128)}, s32[8,1,16]{2,1,0:T(1,128)S(1)}, u32[]{:S(2)}, u32[]{:S(2)}) collective-permute-start(s32[8,1,16]{2,1,0:T(1,128)} %get-tuple-element.39), channel_id=1, source_target_pairs={{6,5},{7,4},{0,3},{1,2},{14,13},{15,12},{8,11},{9,10},{22,21},{23,... | collective-permute-start | bytes 1544 | tf_op jit(solution)/shard_map/ppermute | solution.py:374
  18.1 6.5 %collective-permute-done.4.refs_1_ = s32[8,1,16]{2,1,0:T(1,128)S(1)} collective-permute-done((s32[8,1,16]{2,1,0:T(1,128)}, s32[8,1,16]{2,1,0:T(1,128)S(1)}, u32[]{:S(2)}, u32[]{:S(2)}) %collective-permute-start.4) | collective-permute-done | bytes 544 | tf_op jit(solution)/shard_map/ppermute | solution.py:374
  24.7 3.1 %collective-permute-start.12 = (bf16[4,4,128,128]{3,2,1,0:T(8,128)(2,1)S(1)}, bf16[4,4,128,128]{3,2,1,0:T(8,128)(2,1)S(1)}, u32[]{:S(2)}, u32[]{:S(2)}) collective-permute-start(bf16[4,4,128,128]{3,2,1,0:T(8,128)(2,1)S(1)} %bitcast.5), channel_id=1, source_target_pairs={{0,2},{1,3},{2,0},{3,1},{4,6},{5,7},{6,4},{7,5},{8,10},{9,11},{10,... | collective-permute-start | bytes 1572872 | tf_op jit(solution)/shard_map/ppermute | solution.py:354
  28.5 4.3 %collective-permute-start.14 = (bf16[4,4,128,128]{3,2,1,0:T(8,128)(2,1)S(1)}, bf16[4,4,128,128]{3,2,1,0:T(8,128)(2,1)S(1)}, u32[]{:S(2)}, u32[]{:S(2)}) collective-permute-start(bf16[4,4,128,128]{3,2,1,0:T(8,128)(2,1)S(1)} %bitcast.7), channel_id=1, source_target_pairs={{0,4},{1,5},{6,2},{7,3},{8,12},{9,13},{14,10},{15,11},{16,20},{17,... | collective-permute-start | bytes 1572872 | tf_op jit(solution)/shard_map/ppermute | solution.py:374
  34.5 3.9 %pick_blocks.2 = (bf16[4,4,128,128]{3,2,1,0:T(8,128)(2,1)}, bf16[4,4,128,128]{3,2,1,0:T(8,128)(2,1)}, bf16[4,4,128,128]{3,2,1,0:T(8,128)(2,1)}, bf16[4,4,128,128]{3,2,1,0:T(8,128)(2,1)}) custom-call(s32[8,1,16]{2,1,0:T(1,128)} %copy-done.25, s32[8,1,16]{2,1,0:T(1,128)} %copy-done.26, s32[8,1,16]{2,1,0:T(1,128)} %copy-done.27, ...), custom_call_target="tpu_custom_call" | custom-call | flops 3449999872 | bytes 1024 | tf_op jit(solution)/shard_map/pick_blocks/pallas_call | solution.py:148
  39.4 1.3 collective-permute-start.8
  42.0 6.8 %collective-permute-done.14.refs_6_.refs_3_ = bf16[4,4,128,128]{3,2,1,0:T(8,128)(2,1)S(1)} collective-permute-done((bf16[4,4,128,128]{3,2,1,0:T(8,128)(2,1)S(1)}, bf16[4,4,128,128]{3,2,1,0:T(8,128)(2,1)S(1)}, u32[]{:S(2)}, u32[]{:S(2)}) %collective-permute-start.14) | collective-permute-done | bytes 524320 | tf_op jit(solution)/shard_map/ppermute | solution.py:374
  49.6 3.9 %pick_blocks.3 = (bf16[4,4,128,128]{3,2,1,0:T(8,128)(2,1)}, bf16[4,4,128,128]{3,2,1,0:T(8,128)(2,1)}, bf16[4,4,128,128]{3,2,1,0:T(8,128)(2,1)}, bf16[4,4,128,128]{3,2,1,0:T(8,128)(2,1)}) custom-call(s32[8,1,16]{2,1,0:T(1,128)} %copy-done.25, s32[8,1,16]{2,1,0:T(1,128)} %copy-done.26, s32[8,1,16]{2,1,0:T(1,128)} %copy-done.27, ...), custom_call_target="tpu_custom_call" | custom-call | flops 3449999872 | bytes 1024 | tf_op jit(solution)/shard_map/pick_blocks/pallas_call | solution.py:148
  55.7 1.3 collective-permute-start.18
  57.0 7.7 %collective-permute-done.9.refs_7_ = bf16[4,4,128,128]{3,2,1,0:T(8,128)(2,1)S(1)} collective-permute-done((bf16[4,4,128,128]{3,2,1,0:T(8,128)(2,1)}, bf16[4,4,128,128]{3,2,1,0:T(8,128)(2,1)S(1)}, u32[]{:S(2)}, u32[]{:S(2)}) %collective-permute-start.9) | collective-permute-done | bytes 524320 | tf_op jit(solution)/shard_map/ppermute | solution.py:374
  65.6 7.7 %spatial.2.refs_0_ = bf16[4,4,128,128]{3,2,1,0:T(8,128)(2,1)} custom-call(s32[8,4,8]{2,1,0:T(4,128)} %get-tuple-element.36.slot_ref, bf16[8,4,8,128,128]{4,3,2,1,0:T(8,128)(2,1)} %vals_ref.3, bf16[128,128]{1,0:T(8,128)(2,1)} %get-tuple-element.37.weight_ref, f32[8,128]{1,0:T(8,128)} %get-tuple-element.38.pos_ref, bf16[4,4,128,128]{3,2,1,0:T(8,128)(2,1)} %bitcast.14, ...), custom_call_target="tpu_custom_call" | custom-call | flops 9200000000 | bytes 1024 | tf_op jit(solution)/shard_map/spatial/pallas_call | solution.py:210
  73.3 1.3 collective-permute-start.11
  77.2 10.0 %collective-permute-done.18.refs_7_ = bf16[4,4,128,128]{3,2,1,0:T(8,128)(2,1)S(1)} collective-permute-done((bf16[4,4,128,128]{3,2,1,0:T(8,128)(2,1)}, bf16[4,4,128,128]{3,2,1,0:T(8,128)(2,1)S(1)}, u32[]{:S(2)}, u32[]{:S(2)}) %collective-permute-start.18) | collective-permute-done | bytes 524320 | tf_op jit(solution)/shard_map/ppermute | solution.py:374
  88.0 7.6 %spatial.3 = (bf16[2,4,128,128]{3,2,1,0:T(8,128)(2,1)}, bf16[2,4,128,128]{3,2,1,0:T(8,128)(2,1)}) custom-call(s32[8,4,8]{2,1,0:T(4,128)} %get-tuple-element.36.slot_ref, bf16[8,4,8,128,128]{4,3,2,1,0:T(8,128)(2,1)} %vals_ref.3, bf16[128,128]{1,0:T(8,128)(2,1)} %get-tuple-element.37.weight_ref, f32[8,128]{1,0:T(8,128)} %get-tuple-element.38.pos_ref, ...), custom_call_target="tpu_custom_call" | custom-call | flops 9200000000 | bytes 1024 | tf_op jit(solution)/shard_map/spatial/pallas_call | solution.py:210
  97.0 5.2 %collective-permute-start.19 = (bf16[4,4,128,128]{3,2,1,0:T(8,128)(2,1)S(1)}, bf16[4,4,128,128]{3,2,1,0:T(8,128)(2,1)S(1)}, u32[]{:S(2)}, u32[]{:S(2)}) collective-permute-start(bf16[4,4,128,128]{3,2,1,0:T(8,128)(2,1)S(1)} %collective-permute-done.11.refs_2_), channel_id=1, source_target_pairs={{16,24},{24,16},{17,25},{25,17},{18,26},{26,18},{19,27},{27,19},{2... | collective-permute-start | bytes 1572872 | tf_op jit(solution)/shard_map/ppermute | solution.py:421
  104.8 4.5 %collective-permute-start.25 = (bf16[2,4,128,128]{3,2,1,0:T(8,128)(2,1)S(1)}, bf16[2,4,128,128]{3,2,1,0:T(8,128)(2,1)S(1)}, u32[]{:S(2)}, u32[]{:S(2)}) collective-permute-start(bf16[2,4,128,128]{3,2,1,0:T(8,128)(2,1)S(1)} %collective-permute-done.24.refs_6_), channel_id=1, source_target_pairs={{16,24},{24,16},{17,25},{25,17},{18,26},{26,18},{19,27},{27,19},{2... | collective-permute-start | bytes 786440 | tf_op jit(solution)/shard_map/ppermute | solution.py:421
  109.4 2.9 %collective-permute-done.21.refs_6_ = bf16[2,4,128,128]{3,2,1,0:T(8,128)(2,1)S(1)} collective-permute-done((bf16[2,4,128,128]{3,2,1,0:T(8,128)(2,1)}, bf16[2,4,128,128]{3,2,1,0:T(8,128)(2,1)S(1)}, u32[]{:S(2)}, u32[]{:S(2)}) %collective-permute-start.21) | collective-permute-done | bytes 262176 | tf_op jit(solution)/shard_map/ppermute | solution.py:411
  113.6 3.2 %collective-permute-start.22 = (bf16[2,4,128,128]{3,2,1,0:T(8,128)(2,1)S(1)}, bf16[2,4,128,128]{3,2,1,0:T(8,128)(2,1)S(1)}, u32[]{:S(2)}, u32[]{:S(2)}) collective-permute-start(bf16[2,4,128,128]{3,2,1,0:T(8,128)(2,1)S(1)} %collective-permute-done.21.refs_6_), channel_id=1, source_target_pairs={{16,24},{24,16},{17,25},{25,17},{18,26},{26,18},{19,27},{27,19},{2... | collective-permute-start | bytes 786440 | tf_op jit(solution)/shard_map/ppermute | solution.py:421
  117.9 11.6 %temporal.2.refs_8_ = bf16[8,512,128]{2,1,0:T(8,128)(2,1)} custom-call(s32[1]{0:T(128)} %bitcast.me_ref, bf16[384,128]{1,0:T(8,128)(2,1)} %get-tuple-element.31.qkv_ref, bf16[128,128]{1,0:T(8,128)(2,1)} %get-tuple-element.32.proj_ref, f32[128,128]{1,0:T(8,128)} %get-tuple-element.33.gain_ref, bf16[512,128]{1,0:T(8,128)(2,1)} %get-tuple-element.34.up_ref, ...), custom_call_target="tpu_custom_call" | custom-call | flops 11500000256 | bytes 1024 | tf_op jit(solution)/shard_map/temporal/pallas_call | solution.py:327
  131.0 11.7 %temporal.3 = bf16[8,512,128]{2,1,0:T(8,128)(2,1)} custom-call(s32[1]{0:T(128)} %bitcast.me_ref, bf16[384,128]{1,0:T(8,128)(2,1)} %get-tuple-element.31.qkv_ref, bf16[128,128]{1,0:T(8,128)(2,1)} %get-tuple-element.32.proj_ref, f32[128,128]{1,0:T(8,128)} %get-tuple-element.33.gain_ref, ...), custom_call_target="tpu_custom_call", output_to_operand_aliasing={{}: (14, {})} | custom-call | flops 11500000256 | bytes 1024 | tf_op jit(solution)/shard_map/temporal/pallas_call | solution.py:327
  (93 shorter events, 23.2 us)
Async XLA Ops:
  1.3 27.2 %collective-permute-start = (bf16[4,4,128,128]{3,2,1,0:T(8,128)(2,1)S(1)}, bf16[4,4,128,128]{3,2,1,0:T(8,128)(2,1)S(1)}, u32[]{:S(2)}, u32[]{:S(2)}) collective-permute-start(bf16[4,4,128,128]{3,2,1,0:T(8,128)(2,1)S(1)} %bitcast.10), channel_id=1, source_target_pairs={{0,2},{1,3},{2,0},{3,1},{4,6},{5,7},{6,4},{7,5},{8,10},{9,11},{10,... | collective-permute-start | bytes 1572872 | tf_op jit(solution)/shard_map/ppermute | solution.py:354
  2.7 30.2 %collective-permute-start.1 = (bf16[4,4,128,128]{3,2,1,0:T(8,128)(2,1)S(1)}, bf16[4,4,128,128]{3,2,1,0:T(8,128)(2,1)S(1)}, u32[]{:S(2)}, u32[]{:S(2)}) collective-permute-start(bf16[4,4,128,128]{3,2,1,0:T(8,128)(2,1)S(1)} %bitcast.11), channel_id=1, source_target_pairs={{2,4},{3,5},{4,2},{5,3},{10,12},{11,13},{12,10},{13,11},{18,20},{1... | collective-permute-start | bytes 1572872 | tf_op jit(solution)/shard_map/ppermute | solution.py:374
  3.4 29.6 %collective-permute-start.2 = (bf16[4,4,128,128]{3,2,1,0:T(8,128)(2,1)S(1)}, bf16[4,4,128,128]{3,2,1,0:T(8,128)(2,1)S(1)}, u32[]{:S(2)}, u32[]{:S(2)}) collective-permute-start(bf16[4,4,128,128]{3,2,1,0:T(8,128)(2,1)S(1)} %bitcast.12), channel_id=1, source_target_pairs={{0,4},{1,5},{6,2},{7,3},{8,12},{9,13},{14,10},{15,11},{16,20},{17,... | collective-permute-start | bytes 1572872 | tf_op jit(solution)/shard_map/ppermute | solution.py:374
  13.9 10.7 %collective-permute-start.4 = (s32[8,1,16]{2,1,0:T(1,128)}, s32[8,1,16]{2,1,0:T(1,128)S(1)}, u32[]{:S(2)}, u32[]{:S(2)}) collective-permute-start(s32[8,1,16]{2,1,0:T(1,128)} %get-tuple-element.39), channel_id=1, source_target_pairs={{6,4},{7,5},{0,2},{1,3},{14,12},{15,13},{8,10},{9,11},{22,20},{23,... | collective-permute-start | bytes 1544 | tf_op jit(solution)/shard_map/ppermute | solution.py:374
  15.4 9.3 %collective-permute-start.5 = (s32[8,1,16]{2,1,0:T(1,128)}, s32[8,1,16]{2,1,0:T(1,128)S(1)}, u32[]{:S(2)}, u32[]{:S(2)}) collective-permute-start(s32[8,1,16]{2,1,0:T(1,128)} %get-tuple-element.39), channel_id=1, source_target_pairs={{6,5},{7,4},{0,3},{1,2},{14,13},{15,12},{8,11},{9,10},{22,21},{23,... | collective-permute-start | bytes 1544 | tf_op jit(solution)/shard_map/ppermute | solution.py:374
  24.7 14.7 %collective-permute-start.12 = (bf16[4,4,128,128]{3,2,1,0:T(8,128)(2,1)S(1)}, bf16[4,4,128,128]{3,2,1,0:T(8,128)(2,1)S(1)}, u32[]{:S(2)}, u32[]{:S(2)}) collective-permute-start(bf16[4,4,128,128]{3,2,1,0:T(8,128)(2,1)S(1)} %bitcast.5), channel_id=1, source_target_pairs={{0,2},{1,3},{2,0},{3,1},{4,6},{5,7},{6,4},{7,5},{8,10},{9,11},{10,... | collective-permute-start | bytes 1572872 | tf_op jit(solution)/shard_map/ppermute | solution.py:354
  27.8 12.9 %collective-permute-start.13 = (bf16[4,4,128,128]{3,2,1,0:T(8,128)(2,1)S(1)}, bf16[4,4,128,128]{3,2,1,0:T(8,128)(2,1)S(1)}, u32[]{:S(2)}, u32[]{:S(2)}) collective-permute-start(bf16[4,4,128,128]{3,2,1,0:T(8,128)(2,1)S(1)} %bitcast.6), channel_id=1, source_target_pairs={{2,4},{3,5},{4,2},{5,3},{10,12},{11,13},{12,10},{13,11},{18,20},{1... | collective-permute-start | bytes 1572872 | tf_op jit(solution)/shard_map/ppermute | solution.py:374
  28.5 20.2 %collective-permute-start.14 = (bf16[4,4,128,128]{3,2,1,0:T(8,128)(2,1)S(1)}, bf16[4,4,128,128]{3,2,1,0:T(8,128)(2,1)S(1)}, u32[]{:S(2)}, u32[]{:S(2)}) collective-permute-start(bf16[4,4,128,128]{3,2,1,0:T(8,128)(2,1)S(1)} %bitcast.7), channel_id=1, source_target_pairs={{0,4},{1,5},{6,2},{7,3},{8,12},{9,13},{14,10},{15,11},{16,20},{17,... | collective-permute-start | bytes 1572872 | tf_op jit(solution)/shard_map/ppermute | solution.py:374
  38.4 15.3 %collective-permute-start.6 = (bf16[4,4,128,128]{3,2,1,0:T(8,128)(2,1)}, bf16[4,4,128,128]{3,2,1,0:T(8,128)(2,1)S(1)}, u32[]{:S(2)}, u32[]{:S(2)}) collective-permute-start(bf16[4,4,128,128]{3,2,1,0:T(8,128)(2,1)} %get-tuple-element.43), channel_id=1, source_target_pairs={{0,1},{1,0},{2,3},{3,2},{4,5},{5,4},{6,7},{7,6},{8,9},{9,8},{10,11... | collective-permute-start | bytes 1572872 | tf_op jit(solution)/shard_map/ppermute | solution.py:354
  38.7 15.7 %collective-permute-start.7 = (bf16[4,4,128,128]{3,2,1,0:T(8,128)(2,1)}, bf16[4,4,128,128]{3,2,1,0:T(8,128)(2,1)S(1)}, u32[]{:S(2)}, u32[]{:S(2)}) collective-permute-start(bf16[4,4,128,128]{3,2,1,0:T(8,128)(2,1)} %get-tuple-element.44), channel_id=1, source_target_pairs={{2,3},{3,2},{4,5},{5,4},{10,11},{11,10},{12,13},{13,12},{18,19},{1... | collective-permute-start | bytes 1572872 | tf_op jit(solution)/shard_map/ppermute | solution.py:374
  39.4 16.3 %collective-permute-start.8 = (bf16[4,4,128,128]{3,2,1,0:T(8,128)(2,1)}, bf16[4,4,128,128]{3,2,1,0:T(8,128)(2,1)S(1)}, u32[]{:S(2)}, u32[]{:S(2)}) collective-permute-start(bf16[4,4,128,128]{3,2,1,0:T(8,128)(2,1)} %get-tuple-element.45), channel_id=1, source_target_pairs={{4,6},{5,7},{2,0},{3,1},{12,14},{13,15},{10,8},{11,9},{20,22},{21,... | collective-permute-start | bytes 1572872 | tf_op jit(solution)/shard_map/ppermute | solution.py:374
  40.7 24.0 %collective-permute-start.9 = (bf16[4,4,128,128]{3,2,1,0:T(8,128)(2,1)}, bf16[4,4,128,128]{3,2,1,0:T(8,128)(2,1)S(1)}, u32[]{:S(2)}, u32[]{:S(2)}) collective-permute-start(bf16[4,4,128,128]{3,2,1,0:T(8,128)(2,1)} %get-tuple-element.46), channel_id=1, source_target_pairs={{4,7},{5,6},{2,1},{3,0},{12,15},{13,14},{10,9},{11,8},{20,23},{21,... | collective-permute-start | bytes 1572872 | tf_op jit(solution)/shard_map/ppermute | solution.py:374
  53.5 22.4 %collective-permute-start.15 = (bf16[4,4,128,128]{3,2,1,0:T(8,128)(2,1)}, bf16[4,4,128,128]{3,2,1,0:T(8,128)(2,1)S(1)}, u32[]{:S(2)}, u32[]{:S(2)}) collective-permute-start(bf16[4,4,128,128]{3,2,1,0:T(8,128)(2,1)} %get-tuple-element.48), channel_id=1, source_target_pairs={{0,1},{1,0},{2,3},{3,2},{4,5},{5,4},{6,7},{7,6},{8,9},{9,8},{10,11... | collective-permute-start | bytes 1572872 | tf_op jit(solution)/shard_map/ppermute | solution.py:354
  53.7 23.5 %collective-permute-start.16 = (bf16[4,4,128,128]{3,2,1,0:T(8,128)(2,1)}, bf16[4,4,128,128]{3,2,1,0:T(8,128)(2,1)S(1)}, u32[]{:S(2)}, u32[]{:S(2)}) collective-permute-start(bf16[4,4,128,128]{3,2,1,0:T(8,128)(2,1)} %get-tuple-element.49), channel_id=1, source_target_pairs={{2,3},{3,2},{4,5},{5,4},{10,11},{11,10},{12,13},{13,12},{18,19},{1... | collective-permute-start | bytes 1572872 | tf_op jit(solution)/shard_map/ppermute | solution.py:374
  54.4 22.8 %collective-permute-start.17 = (bf16[4,4,128,128]{3,2,1,0:T(8,128)(2,1)}, bf16[4,4,128,128]{3,2,1,0:T(8,128)(2,1)S(1)}, u32[]{:S(2)}, u32[]{:S(2)}) collective-permute-start(bf16[4,4,128,128]{3,2,1,0:T(8,128)(2,1)} %get-tuple-element.50), channel_id=1, source_target_pairs={{4,6},{5,7},{2,0},{3,1},{12,14},{13,15},{10,8},{11,9},{20,22},{21,... | collective-permute-start | bytes 1572872 | tf_op jit(solution)/shard_map/ppermute | solution.py:374
  55.7 31.5 %collective-permute-start.18 = (bf16[4,4,128,128]{3,2,1,0:T(8,128)(2,1)}, bf16[4,4,128,128]{3,2,1,0:T(8,128)(2,1)S(1)}, u32[]{:S(2)}, u32[]{:S(2)}) collective-permute-start(bf16[4,4,128,128]{3,2,1,0:T(8,128)(2,1)} %get-tuple-element.51), channel_id=1, source_target_pairs={{4,7},{5,6},{2,1},{3,0},{12,15},{13,14},{10,9},{11,8},{20,23},{21,... | collective-permute-start | bytes 1572872 | tf_op jit(solution)/shard_map/ppermute | solution.py:374
  73.3 23.7 %collective-permute-start.11 = (bf16[4,4,128,128]{3,2,1,0:T(8,128)(2,1)}, bf16[4,4,128,128]{3,2,1,0:T(8,128)(2,1)S(1)}, u32[]{:S(2)}, u32[]{:S(2)}) collective-permute-start(bf16[4,4,128,128]{3,2,1,0:T(8,128)(2,1)} %spatial.2.refs_0_), channel_id=1, source_target_pairs={{0,16},{8,24},{1,17},{9,25},{2,18},{10,26},{3,19},{11,27},{4,20},{... | collective-permute-start | bytes 1572872 | tf_op jit(solution)/shard_map/ppermute | solution.py:411
  75.9 41.0 %collective-permute-start.10 = (bf16[4,4,128,128]{3,2,1,0:T(8,128)(2,1)}, bf16[4,4,128,128]{3,2,1,0:T(8,128)(2,1)S(1)}, u32[]{:S(2)}, u32[]{:S(2)}) collective-permute-start(bf16[4,4,128,128]{3,2,1,0:T(8,128)(2,1)} %spatial.2.refs_0_), channel_id=1, source_target_pairs={{0,8},{16,24},{1,9},{17,25},{2,10},{18,26},{3,11},{19,27},{4,12},{... | collective-permute-start | bytes 1572872 | tf_op jit(solution)/shard_map/ppermute | solution.py:411
  97.0 19.9 %collective-permute-start.19 = (bf16[4,4,128,128]{3,2,1,0:T(8,128)(2,1)S(1)}, bf16[4,4,128,128]{3,2,1,0:T(8,128)(2,1)S(1)}, u32[]{:S(2)}, u32[]{:S(2)}) collective-permute-start(bf16[4,4,128,128]{3,2,1,0:T(8,128)(2,1)S(1)} %collective-permute-done.11.refs_2_), channel_id=1, source_target_pairs={{16,24},{24,16},{17,25},{25,17},{18,26},{26,18},{19,27},{27,19},{2... | collective-permute-start | bytes 1572872 | tf_op jit(solution)/shard_map/ppermute | solution.py:421
  102.2 10.1 %collective-permute-start.21 = (bf16[2,4,128,128]{3,2,1,0:T(8,128)(2,1)}, bf16[2,4,128,128]{3,2,1,0:T(8,128)(2,1)S(1)}, u32[]{:S(2)}, u32[]{:S(2)}) collective-permute-start(bf16[2,4,128,128]{3,2,1,0:T(8,128)(2,1)} %get-tuple-element.54.refs_4_), channel_id=1, source_target_pairs={{0,16},{8,24},{1,17},{9,25},{2,18},{10,26},{3,19},{11,27},{4,20},{... | collective-permute-start | bytes 786440 | tf_op jit(solution)/shard_map/ppermute | solution.py:411
  103.5 10.1 %collective-permute-start.23 = (bf16[2,4,128,128]{3,2,1,0:T(8,128)(2,1)}, bf16[2,4,128,128]{3,2,1,0:T(8,128)(2,1)S(1)}, u32[]{:S(2)}, u32[]{:S(2)}) collective-permute-start(bf16[2,4,128,128]{3,2,1,0:T(8,128)(2,1)} %get-tuple-element.52.refs_4_), channel_id=1, source_target_pairs={{0,8},{16,24},{1,9},{17,25},{2,10},{18,26},{3,11},{19,27},{4,12},{... | collective-permute-start | bytes 786440 | tf_op jit(solution)/shard_map/ppermute | solution.py:411
  104.8 12.0 %collective-permute-start.25 = (bf16[2,4,128,128]{3,2,1,0:T(8,128)(2,1)S(1)}, bf16[2,4,128,128]{3,2,1,0:T(8,128)(2,1)S(1)}, u32[]{:S(2)}, u32[]{:S(2)}) collective-permute-start(bf16[2,4,128,128]{3,2,1,0:T(8,128)(2,1)S(1)} %collective-permute-done.24.refs_6_), channel_id=1, source_target_pairs={{16,24},{24,16},{17,25},{25,17},{18,26},{26,18},{19,27},{27,19},{2... | collective-permute-start | bytes 786440 | tf_op jit(solution)/shard_map/ppermute | solution.py:421
  112.3 17.3 %collective-permute-start.20 = (bf16[2,4,128,128]{3,2,1,0:T(8,128)(2,1)}, bf16[2,4,128,128]{3,2,1,0:T(8,128)(2,1)S(1)}, u32[]{:S(2)}, u32[]{:S(2)}) collective-permute-start(bf16[2,4,128,128]{3,2,1,0:T(8,128)(2,1)} %get-tuple-element.54.refs_4_), channel_id=1, source_target_pairs={{0,8},{16,24},{1,9},{17,25},{2,10},{18,26},{3,11},{19,27},{4,12},{... | collective-permute-start | bytes 786440 | tf_op jit(solution)/shard_map/ppermute | solution.py:411
  113.6 16.0 %collective-permute-start.22 = (bf16[2,4,128,128]{3,2,1,0:T(8,128)(2,1)S(1)}, bf16[2,4,128,128]{3,2,1,0:T(8,128)(2,1)S(1)}, u32[]{:S(2)}, u32[]{:S(2)}) collective-permute-start(bf16[2,4,128,128]{3,2,1,0:T(8,128)(2,1)S(1)} %collective-permute-done.21.refs_6_), channel_id=1, source_target_pairs={{16,24},{24,16},{17,25},{25,17},{18,26},{26,18},{19,27},{27,19},{2... | collective-permute-start | bytes 786440 | tf_op jit(solution)/shard_map/ppermute | solution.py:421
  (30 other events, 269.7 us)

commit v3 on v2

--- a/solution.py
+++ b/solution.py
@@ -11,7 +11,7 @@
 HEADS = 16
 CAP = 4.0
 EPS = 1e-05
-VMEM = 56 * 1024 * 1024
+VMEM = 24 * 1024 * 1024
 BF16 = jnp.bfloat16
 F32 = jnp.float32
 after = lax.optimization_barrier
@@ -34,6 +34,10 @@
 
 def whole(a):
     return pl.BlockSpec(a.shape, lambda *i: (0,) * len(a.shape))
+
+
+def near(a):
+    return pltpu.with_memory_space_constraint(a, pltpu.VMEM)
 
 
 def cost(us):
@@ -150,36 +154,33 @@
         grid_spec=pltpu.PrefetchScalarGridSpec(
             num_scalar_prefetch=len(wants),
             grid=(1,),
-            in_specs=[whole(a) for a in srcs],
+            in_specs=[whole(srcs[0])] + [pl.BlockSpec(memory_space=pltpu.VMEM)] * (len(srcs) - 1),
             out_specs=[whole(a) for a in shapes],
         ),
         out_shape=shapes,
         compiler_params=pltpu.CompilerParams(vmem_limit_bytes=VMEM),
         cost_estimate=cost(3),
         name="pick_blocks",
-    )(*wants, *srcs)
+    )(*wants, srcs[0], *[near(a) for a in srcs[1:]])
 
 
 def spatial_kernel(start, offsets, slot_ref, vals_ref, weight_ref, pos_ref, *refs):
-    srcs, (*outs, held, vals, sums, held_sem, vals_sem) = refs[: len(offsets)], refs[len(offsets) :]
+    srcs, (*outs, held, vals, sums, own_sem, vals_sem) = refs[: len(offsets)], refs[len(offsets) :]
     snaps, rows, tiles, size, _ = vals.shape
     each = rows // len(outs)
-    copies, arriving = [], []
-    for src, offset in zip(srcs, offsets):
-        for first in range(0, src.shape[1], rows):
-            unit = len(copies)
-            span = slice(start - offset, start - offset + snaps)
-            copies.append(
-                pltpu.make_async_copy(
-                    src.at[span, first : first + rows], held.at[unit], held_sem.at[unit]
-                )
-            )
+    span = slice(start - offsets[0], start - offsets[0] + snaps)
+    own = pltpu.make_async_copy(srcs[0].at[span], held.at[0], own_sem)
+    own.start()
+    arriving = []
     for s in range(snaps):
         arriving.append(pltpu.make_async_copy(vals_ref.at[start + s], vals.at[s], vals_sem.at[s]))
-    for copy in arriving[:1] + copies + arriving[1:]:
-        copy.start()
-    for copy in copies:
-        copy.wait()
+        arriving[s].start()
+    unit = 1
+    for src, offset in zip(srcs[1:], offsets[1:]):
+        for first in range(0, src.shape[1], rows):
+            held[unit] = src[start - offset : start - offset + snaps, first : first + rows]
+            unit += 1
+    own.wait()
     for s in range(snaps):
         arriving[s].wait()
         for r in range(rows):
@@ -212,13 +213,14 @@
         grid_spec=pltpu.PrefetchScalarGridSpec(
             num_scalar_prefetch=1,
             grid=(1,),
-            in_specs=[anywhere, whole(weight_t), whole(pos)] + [anywhere] * len(srcs),
+            in_specs=[anywhere, whole(weight_t), whole(pos), anywhere]
+            + [pl.BlockSpec(memory_space=pltpu.VMEM)] * (len(srcs) - 1),
             out_specs=[whole(out)] * parts,
             scratch_shapes=[
                 pltpu.VMEM((units, snaps, rows, size, width), BF16),
                 pltpu.VMEM((snaps, rows, tiles, size, size), BF16),
                 pltpu.VMEM((snaps * rows * size, width), BF16),
-                pltpu.SemaphoreType.DMA((units,)),
+                pltpu.SemaphoreType.DMA,
                 pltpu.SemaphoreType.DMA((snaps,)),
             ],
         ),
@@ -226,7 +228,7 @@
         compiler_params=pltpu.CompilerParams(vmem_limit_bytes=VMEM),
         cost_estimate=cost(2 * snaps),
         name="spatial",
-    )(slots, vals, weight_t, pos, *[a for a, _ in srcs])
+    )(slots, vals, weight_t, pos, srcs[0][0], *[near(a) for a, _ in srcs[1:]])
 
 
 def temporal_kernel(sizes, others, me_ref, qkv_ref, proj_ref, gain_ref, up_ref, down_ref, *refs):
@@ -379,27 +381,27 @@
 
     cut = snaps // 2
     first, rest = blocks[:cut], blocks[cut:]
-    p1, p2, near = go(first, cross), go(first, skip), send(first, 2)
+    p1, p2, beside = go(first, cross), go(first, skip), send(first, 2)
     wants = [send(want, 1), go(want, back), go(want, back, 1)]
     rest, *wants = after((rest, *wants))
 
-    def forward(own, near, p1, p2, lo, hi):
-        srcs = [own, near, p1, p2]
-        offsets = [0 if a.shape[0] == snaps else lo for a in srcs]
-        jobs = [
-            (1, [(2, 4), (3, 6)], lo, hi),
-            (2, [(2, 5), (3, 7)], lo, hi),
-            (0, [(0, 1), (1, 3)], lo, hi),
-            (0, [(3, 5), (2, 7)], lo, hi),
+    def forward(own, beside, p1, p2, lo, cuts):
+        srcs, hi = [own, beside, p1, p2], cuts[-1]
+        jobs = [(0, [(0, 1), (1, 3)], lo, hi), (0, [(3, 5), (2, 7)], lo, hi)]
+        spans = list(zip([lo] + cuts, cuts))
+        for span in spans:
+            jobs += [(1, [(2, 4), (3, 6)], *span), (2, [(2, 5), (3, 7)], *span)]
+        x1, x2, *ends_of = pick(srcs, [lo] * 4, wants, jobs)
+        sent = [(go(ends_of[2 * i], ends), go(ends_of[2 * i + 1], ends, 1)) for i in range(len(spans))]
+        x1, x2 = send(x1, 1), go(x2, [(1, 1), (2, 2)], 1)
+        return [
+            (first, stop, [(a, lo) for a in (*srcs, x1, x2)] + [(a, first) for a in pair])
+            for (first, stop), pair in zip(spans, sent)
         ]
-        f0, f1, x1, x2 = pick(srcs, offsets, wants, jobs)
-        f0, f1 = go(f0, ends), go(f1, ends, 1)
-        x1, x2 = send(x1, 1), go(x2, [(1, 1), (2, 2)], 1)
-        return (lo, hi, list(zip(srcs, offsets)) + [(a, lo) for a in (x1, x2, f0, f1)])
-
-    parts = [forward(first, near, p1, p2, 0, cut)]
+
+    parts = forward(first, beside, p1, p2, 0, [cut])
     q1, q2, far = go(rest, cross), go(rest, skip), send(rest, 2)
-    return parts + [forward(rest, far, q1, q2, cut, snaps)]
+    return parts + forward(rest, far, q1, q2, cut, [cut + (snaps - cut) // 2, snaps])
 
 
 def gather_times(own):
@@ -450,21 +452,14 @@
     me = me_t.reshape(1)
     parts = exchange_forward(blocks, want) if forward else exchange_direct(blocks, want, inner)
 
-    started = []
-    for start, stop, srcs in parts[:-1]:
-        (own,) = spatial(slots, tile_vals, start, stop, space_t, pos, srcs, 1)
-        started.append(gather_times(own))
-    start, stop, srcs = parts[-1]
-    halves = 2 if rows % 2 == 0 else 1
-    owns = spatial(slots, tile_vals, start, stop, space_t, pos, srcs, halves)
-    done = [pass_on(got, owns[0]) for got in started]
-    last = [gather_times(own) for own in owns]
-    out = None
-    for h, got in enumerate(last):
-        chunks = done + [pass_on(got, owns[0])]
-        groups = owns[h].shape[0]
-        out = temporal(me, weights, chunks, h * groups, groups, rows, out)
-    return out
+    started, owns = [], []
+    for start, stop, srcs in parts:
+        if owns:
+            srcs[0] = (after((srcs[0][0], owns[-1]))[0], srcs[0][1])
+        owns.append(spatial(slots, tile_vals, start, stop, space_t, pos, srcs, 1)[0])
+        started.append(gather_times(owns[-1]))
+    chunks = [pass_on(got, own) for got, own in zip(started, owns[1:] + owns[-1:])]
+    return temporal(me, weights, chunks, 0, rows, rows, None)
 
 
 def solution(mesh):

time: 144 us -> 127 us (0.88)
  Pallas kernels: 49.6 us -> 30.4 us
  starting transfers between devices: 48.8 us -> 52.1 us
    pallas_call x2 -> x3, Pallas kernels: 15.3 us -> 7.91 us  [spatial(): pl.pallas_call(functools.partial(spatial_kernel, start, [first for _, fir...]
    pallas_call x2, Pallas kernels: 7.79 us -> 1.74 us  [pick(): pl.pallas_call(functools.partial(pick_kernel, jobs, len(wants), offsets),...]
    pallas_call x2 -> x1, Pallas kernels: 23.3 us -> 19.5 us  [temporal(): pl.pallas_call(functools.partial(temporal_kernel, sizes, count - 1), grid...]
    ppermute x5, waiting for transfers between devices: 1.28 us -> 4.92 us  [send(): lax.ppermute(a, 'vert', [(v, v ^ k) for v in range(lax.axis_size('vert'))])]
    ppermute x6, waiting for transfers between devices: 2.96 us -> 0.02 us  [gather_times(): got[k] = lax.ppermute(own, 'tm', pairs)]
    ppermute x12 -> x14, starting transfers between devices: 21.9 us -> 24.6 us  [exchange_forward(): go = lambda a, pairs, x=0: lax.ppermute(a, 'vert', layers(pairs, x))]
    ppermute x12 -> x14, waiting for transfers between devices: 31.1 us -> 28.6 us  [exchange_forward(): go = lambda a, pairs, x=0: lax.ppermute(a, 'vert', layers(pairs, x))]
    pallas_call x1, Pallas kernels: 3.18 us -> 1.21 us  [prepare(): pl.pallas_call(functools.partial(prepare_kernel, rows, count, inner, forw...]
  transfers between devices with their start and end apart: 26 -> 28, of which waited for: 7 -> 10; matrix products, arithmetic and copies ran while one was open for 0% -> 0% of each run, Pallas kernels for 27% -> 9%
where the time goes in v3:
time: 127 us; the launch traced here: 126 us
  starting transfers between devices  52.1 us (41%)
  waiting for transfers between devices  35 us (28%)
  Pallas kernels  30.4 us (24%)
  local copies, waits for them, and re-layouts  7.57 us (6%)
    ppermute x14, waiting for transfers between devices, exchange_forward(): go = lambda a, pairs, x=0: lax.ppermute(a, 'vert', layers(pairs, x))  28.6 us
    ppermute x14, starting transfers between devices, exchange_forward(): go = lambda a, pairs, x=0: lax.ppermute(a, 'vert', layers(pairs, x))  24.6 us
    pallas_call x1, Pallas kernels, temporal(): pl.pallas_call(functools.partial(temporal_kernel, sizes, count - 1), grid...  19.5 us
    ppermute x3, starting transfers between devices, pass_on(): got[k] = lax.ppermute(got[k - 1], 'tm', pairs)  13.4 us
    pallas_call x3, Pallas kernels, spatial(): pl.pallas_call(functools.partial(spatial_kernel, start, [first for _, fir...  7.91 us
    ppermute x6, starting transfers between devices, gather_times(): got[k] = lax.ppermute(own, 'tm', pairs)  7.74 us
    ppermute x5, starting transfers between devices, send(): lax.ppermute(a, 'vert', [(v, v ^ k) for v in range(lax.axis_size('vert'))])  6.41 us
    unnamed x20, local copies, waits for them, and re-layouts  6.3 us
  transfers between devices with their start and end apart: 28, of which 10 were waited for; matrix products, arithmetic and copies ran while one was open for 0% of the time, Pallas kernels for 9%

profile of v3, /device:TPU:5, one launch (start us, length us, event | category | flops | bytes accessed | tf_op | source)
XLA Modules:
  0.0 125.6 jit_solution(17231055777074592720)
XLA Ops:
  1.3 1.4 %collective-permute-start = (bf16[4,4,128,128]{3,2,1,0:T(8,128)(2,1)S(1)}, bf16[4,4,128,128]{3,2,1,0:T(8,128)(2,1)S(1)}, u32[]{:S(2)}, u32[]{:S(2)}) collective-permute-start(bf16[4,4,128,128]{3,2,1,0:T(8,128)(2,1)S(1)} %bitcast.11), channel_id=1, source_target_pairs={{0,2},{1,3},{2,0},{3,1},{4,6},{5,7},{6,4},{7,5},{8,10},{9,11},{10,... | collective-permute-start | bytes 1572872 | tf_op jit(solution)/shard_map/ppermute | solution.py:356
  3.3 5.5 %collective-permute-start.2 = (bf16[4,4,128,128]{3,2,1,0:T(8,128)(2,1)S(1)}, bf16[4,4,128,128]{3,2,1,0:T(8,128)(2,1)S(1)}, u32[]{:S(2)}, u32[]{:S(2)}) collective-permute-start(bf16[4,4,128,128]{3,2,1,0:T(8,128)(2,1)S(1)} %bitcast.13), channel_id=1, source_target_pairs={{0,4},{1,5},{6,2},{7,3},{8,12},{9,13},{14,10},{15,11},{16,20},{17,... | collective-permute-start | bytes 1572872 | tf_op jit(solution)/shard_map/ppermute | solution.py:376
  17.7 1.5 %collective-permute-start.4 = (s32[8,1,16]{2,1,0:T(1,128)S(1)}, s32[8,1,16]{2,1,0:T(1,128)S(1)}, u32[]{:S(2)}, u32[]{:S(2)}) collective-permute-start(s32[8,1,16]{2,1,0:T(1,128)S(1)} %get-tuple-element.41), channel_id=1, source_target_pairs={{6,4},{7,5},{0,2},{1,3},{14,12},{15,13},{8,10},{9,11},{22,20},{23,... | collective-permute-start | bytes 1544 | tf_op jit(solution)/shard_map/ppermute | solution.py:376
  19.2 2.5 %collective-permute-start.5 = (s32[8,1,16]{2,1,0:T(1,128)S(1)}, s32[8,1,16]{2,1,0:T(1,128)S(1)}, u32[]{:S(2)}, u32[]{:S(2)}) collective-permute-start(s32[8,1,16]{2,1,0:T(1,128)S(1)} %get-tuple-element.41), channel_id=1, source_target_pairs={{6,5},{7,4},{0,3},{1,2},{14,13},{15,12},{8,11},{9,10},{22,21},{23,... | collective-permute-start | bytes 1544 | tf_op jit(solution)/shard_map/ppermute | solution.py:376
  21.7 2.9 %collective-permute-done.4.refs_1_ = s32[8,1,16]{2,1,0:T(1,128)S(1)} collective-permute-done((s32[8,1,16]{2,1,0:T(1,128)S(1)}, s32[8,1,16]{2,1,0:T(1,128)S(1)}, u32[]{:S(2)}, u32[]{:S(2)}) %collective-permute-start.4) | collective-permute-done | bytes 544 | tf_op jit(solution)/shard_map/ppermute | solution.py:376
  24.7 3.1 %collective-permute-start.12 = (bf16[4,4,128,128]{3,2,1,0:T(8,128)(2,1)S(1)}, bf16[4,4,128,128]{3,2,1,0:T(8,128)(2,1)S(1)}, u32[]{:S(2)}, u32[]{:S(2)}) collective-permute-start(bf16[4,4,128,128]{3,2,1,0:T(8,128)(2,1)S(1)} %bitcast.5), channel_id=1, source_target_pairs={{0,2},{1,3},{2,0},{3,1},{4,6},{5,7},{6,4},{7,5},{8,10},{9,11},{10,... | collective-permute-start | bytes 1572872 | tf_op jit(solution)/shard_map/ppermute | solution.py:356
  28.5 4.3 %collective-permute-start.14 = (bf16[4,4,128,128]{3,2,1,0:T(8,128)(2,1)S(1)}, bf16[4,4,128,128]{3,2,1,0:T(8,128)(2,1)S(1)}, u32[]{:S(2)}, u32[]{:S(2)}) collective-permute-start(bf16[4,4,128,128]{3,2,1,0:T(8,128)(2,1)S(1)} %bitcast.7), channel_id=1, source_target_pairs={{0,4},{1,5},{6,2},{7,3},{8,12},{9,13},{14,10},{15,11},{16,20},{17,... | collective-permute-start | bytes 1572872 | tf_op jit(solution)/shard_map/ppermute | solution.py:376
  34.9 3.6 %collective-permute-done.12.refs_4_.refs_1_ = bf16[4,4,128,128]{3,2,1,0:T(8,128)(2,1)S(1)} collective-permute-done((bf16[4,4,128,128]{3,2,1,0:T(8,128)(2,1)S(1)}, bf16[4,4,128,128]{3,2,1,0:T(8,128)(2,1)S(1)}, u32[]{:S(2)}, u32[]{:S(2)}) %collective-permute-start.12) | collective-permute-done | bytes 524320 | tf_op jit(solution)/shard_map/ppermute | solution.py:356
  39.8 1.6 %collective-permute-start.9 = (bf16[4,4,128,128]{3,2,1,0:T(8,128)(2,1)S(1)}, bf16[4,4,128,128]{3,2,1,0:T(8,128)(2,1)S(1)}, u32[]{:S(2)}, u32[]{:S(2)}) collective-permute-start(bf16[4,4,128,128]{3,2,1,0:T(8,128)(2,1)S(1)} %get-tuple-element.48), channel_id=1, source_target_pairs={{4,7},{5,6},{2,1},{3,0},{12,15},{13,14},{10,9},{11,8},{20,23},{21,... | collective-permute-start | bytes 1572872 | tf_op jit(solution)/shard_map/ppermute | solution.py:376
  41.4 7.4 %collective-permute-done.14.refs_6_.refs_3_ = bf16[4,4,128,128]{3,2,1,0:T(8,128)(2,1)S(1)} collective-permute-done((bf16[4,4,128,128]{3,2,1,0:T(8,128)(2,1)S(1)}, bf16[4,4,128,128]{3,2,1,0:T(8,128)(2,1)S(1)}, u32[]{:S(2)}, u32[]{:S(2)}) %collective-permute-start.14) | collective-permute-done | bytes 524320 | tf_op jit(solution)/shard_map/ppermute | solution.py:376
  50.7 1.3 %collective-permute-start.17 = (bf16[2,4,128,128]{3,2,1,0:T(8,128)(2,1)S(1)}, bf16[2,4,128,128]{3,2,1,0:T(8,128)(2,1)S(1)}, u32[]{:S(2)}, u32[]{:S(2)}) collective-permute-start(bf16[2,4,128,128]{3,2,1,0:T(8,128)(2,1)S(1)} %get-tuple-element.53), channel_id=1, source_target_pairs={{4,6},{5,7},{2,0},{3,1},{12,14},{13,15},{10,8},{11,9},{20,22},{21,... | collective-permute-start | bytes 786440 | tf_op jit(solution)/shard_map/ppermute | solution.py:376
  52.0 1.3 %collective-permute-start.18 = (bf16[2,4,128,128]{3,2,1,0:T(8,128)(2,1)S(1)}, bf16[2,4,128,128]{3,2,1,0:T(8,128)(2,1)S(1)}, u32[]{:S(2)}, u32[]{:S(2)}) collective-permute-start(bf16[2,4,128,128]{3,2,1,0:T(8,128)(2,1)S(1)} %get-tuple-element.54), channel_id=1, source_target_pairs={{4,7},{5,6},{2,1},{3,0},{12,15},{13,14},{10,9},{11,8},{20,23},{21,... | collective-permute-start | bytes 786440 | tf_op jit(solution)/shard_map/ppermute | solution.py:376
  53.3 8.3 %collective-permute-done.9.refs_7_ = bf16[4,4,128,128]{3,2,1,0:T(8,128)(2,1)S(1)} collective-permute-done((bf16[4,4,128,128]{3,2,1,0:T(8,128)(2,1)S(1)}, bf16[4,4,128,128]{3,2,1,0:T(8,128)(2,1)S(1)}, u32[]{:S(2)}, u32[]{:S(2)}) %collective-permute-start.9) | collective-permute-done | bytes 524320 | tf_op jit(solution)/shard_map/ppermute | solution.py:376
  62.8 3.4 %spatial.3.refs_0_ = bf16[4,4,128,128]{3,2,1,0:T(8,128)(2,1)S(1)} custom-call(s32[8,4,8]{2,1,0:T(4,128)S(1)} %get-tuple-element.38.slot_ref, bf16[8,4,8,128,128]{4,3,2,1,0:T(8,128)(2,1)S(1)} %bitcast.18, bf16[128,128]{1,0:T(8,128)(2,1)S(1)} %get-tuple-element.39.weight_ref, f32[8,128]{1,0:T(8,128)S(1)} %get-tuple-element.40.pos_ref, ...), custom_call_target="tpu_custom_call" | custom-call | flops 9200000000 | bytes 1024 | tf_op jit(solution)/shard_map/spatial/pallas_call | solution.py:211
  68.5 4.0 %collective-permute-done.18.refs_7_ = bf16[2,4,128,128]{3,2,1,0:T(8,128)(2,1)S(1)} collective-permute-done((bf16[2,4,128,128]{3,2,1,0:T(8,128)(2,1)S(1)}, bf16[2,4,128,128]{3,2,1,0:T(8,128)(2,1)S(1)}, u32[]{:S(2)}, u32[]{:S(2)}) %collective-permute-start.18) | collective-permute-done | bytes 262176 | tf_op jit(solution)/shard_map/ppermute | solution.py:376
  73.8 1.3 %collective-permute-done.15.refs_4_ = bf16[4,4,128,128]{3,2,1,0:T(8,128)(2,1)S(1)} collective-permute-done((bf16[4,4,128,128]{3,2,1,0:T(8,128)(2,1)S(1)}, bf16[4,4,128,128]{3,2,1,0:T(8,128)(2,1)S(1)}, u32[]{:S(2)}, u32[]{:S(2)}) %collective-permute-start.15) | collective-permute-done | bytes 524320 | tf_op jit(solution)/shard_map/ppermute | solution.py:356
  75.1 2.2 %spatial.4.refs_4_ = bf16[4,2,128,128]{3,2,1,0:T(8,128)(2,1)S(1)} custom-call(s32[8,4,8]{2,1,0:T(4,128)S(1)} %get-tuple-element.38.slot_ref, bf16[8,4,8,128,128]{4,3,2,1,0:T(8,128)(2,1)S(1)} %bitcast.18, bf16[128,128]{1,0:T(8,128)(2,1)S(1)} %get-tuple-element.39.weight_ref, f32[8,128]{1,0:T(8,128)S(1)} %get-tuple-element.40.pos_ref, ...), custom_call_target="tpu_custom_call" | custom-call | flops 4600000000 | bytes 1024 | tf_op jit(solution)/shard_map/spatial/pallas_call | solution.py:211
  78.6 5.1 %collective-permute-done.23.refs_7_ = bf16[2,4,128,128]{3,2,1,0:T(8,128)(2,1)S(1)} collective-permute-done((bf16[2,4,128,128]{3,2,1,0:T(8,128)(2,1)S(1)}, bf16[2,4,128,128]{3,2,1,0:T(8,128)(2,1)S(1)}, u32[]{:S(2)}, u32[]{:S(2)}) %collective-permute-start.23) | collective-permute-done | bytes 262176 | tf_op jit(solution)/shard_map/ppermute | solution.py:376
  83.7 2.2 %spatial.5.refs_8_ = bf16[4,2,128,128]{3,2,1,0:T(8,128)(2,1)S(1)} custom-call(s32[8,4,8]{2,1,0:T(4,128)S(1)} %get-tuple-element.38.slot_ref, bf16[8,4,8,128,128]{4,3,2,1,0:T(8,128)(2,1)S(1)} %bitcast.18, bf16[128,128]{1,0:T(8,128)(2,1)S(1)} %get-tuple-element.39.weight_ref, f32[8,128]{1,0:T(8,128)S(1)} %get-tuple-element.40.pos_ref, ...), custom_call_target="tpu_custom_call" | custom-call | flops 4600000000 | bytes 1024 | tf_op jit(solution)/shard_map/spatial/pallas_call | solution.py:211
  89.9 6.7 %collective-permute-start.19 = (bf16[4,4,128,128]{3,2,1,0:T(8,128)(2,1)S(1)}, bf16[4,4,128,128]{3,2,1,0:T(8,128)(2,1)S(1)}, u32[]{:S(2)}, u32[]{:S(2)}) collective-permute-start(bf16[4,4,128,128]{3,2,1,0:T(8,128)(2,1)S(1)} %collective-permute-done.11.refs_2_), channel_id=1, source_target_pairs={{16,24},{24,16},{17,25},{25,17},{18,26},{26,18},{19,27},{27,19},{2... | collective-permute-start | bytes 1572872 | tf_op jit(solution)/shard_map/ppermute | solution.py:423
  97.9 4.8 %collective-permute-start.24 = (bf16[4,2,128,128]{3,2,1,0:T(8,128)(2,1)S(1)}, bf16[4,2,128,128]{3,2,1,0:T(8,128)(2,1)S(1)}, u32[]{:S(2)}, u32[]{:S(2)}) collective-permute-start(bf16[4,2,128,128]{3,2,1,0:T(8,128)(2,1)S(1)} %collective-permute-done.21.refs_6_), channel_id=1, source_target_pairs={{16,24},{24,16},{17,25},{25,17},{18,26},{26,18},{19,27},{27,19},{2... | collective-permute-start | bytes 786440 | tf_op jit(solution)/shard_map/ppermute | solution.py:423
  102.7 1.9 %collective-permute-start.27 = (bf16[4,2,128,128]{3,2,1,0:T(8,128)(2,1)S(1)}, bf16[4,2,128,128]{3,2,1,0:T(8,128)(2,1)S(1)}, u32[]{:S(2)}, u32[]{:S(2)}) collective-permute-start(bf16[4,2,128,128]{3,2,1,0:T(8,128)(2,1)S(1)} %collective-permute-done.26.refs_10_), channel_id=1, source_target_pairs={{16,24},{24,16},{17,25},{25,17},{18,26},{26,18},{19,27},{27,19},{2... | collective-permute-start | bytes 786440 | tf_op jit(solution)/shard_map/ppermute | solution.py:423
  104.6 1.5 %collective-permute-done.27.refs_11_ = bf16[4,2,128,128]{3,2,1,0:T(8,128)(2,1)S(1)} collective-permute-done((bf16[4,2,128,128]{3,2,1,0:T(8,128)(2,1)S(1)}, bf16[4,2,128,128]{3,2,1,0:T(8,128)(2,1)S(1)}, u32[]{:S(2)}, u32[]{:S(2)}) %collective-permute-start.27) | collective-permute-done | bytes 262176 | tf_op jit(solution)/shard_map/ppermute | solution.py:423
  106.1 19.5 %temporal.1 = bf16[8,512,128]{2,1,0:T(8,128)(2,1)} custom-call(s32[1]{0:T(128)} %bitcast.me_ref, bf16[384,128]{1,0:T(8,128)(2,1)S(1)} %get-tuple-element.33.qkv_ref, bf16[128,128]{1,0:T(8,128)(2,1)S(1)} %get-tuple-element.34.proj_ref, f32[128,128]{1,0:T(8,128)S(1)} %get-tuple-element.35.gain_ref, bf16[512,128]{1,0:T(8,128)(2,1)S(1)} %get-tuple-element.36.up_ref, ...), custom_call_target="tpu_custom_call" | custom-call | flops 11500000256 | bytes 1024 | tf_op jit(solution)/shard_map/temporal/pallas_call | solution.py:329
  (62 shorter events, 28.0 us)
Async XLA Ops:
  1.3 27.2 %collective-permute-start = (bf16[4,4,128,128]{3,2,1,0:T(8,128)(2,1)S(1)}, bf16[4,4,128,128]{3,2,1,0:T(8,128)(2,1)S(1)}, u32[]{:S(2)}, u32[]{:S(2)}) collective-permute-start(bf16[4,4,128,128]{3,2,1,0:T(8,128)(2,1)S(1)} %bitcast.11), channel_id=1, source_target_pairs={{0,2},{1,3},{2,0},{3,1},{4,6},{5,7},{6,4},{7,5},{8,10},{9,11},{10,... | collective-permute-start | bytes 1572872 | tf_op jit(solution)/shard_map/ppermute | solution.py:356
  2.6 30.2 %collective-permute-start.1 = (bf16[4,4,128,128]{3,2,1,0:T(8,128)(2,1)S(1)}, bf16[4,4,128,128]{3,2,1,0:T(8,128)(2,1)S(1)}, u32[]{:S(2)}, u32[]{:S(2)}) collective-permute-start(bf16[4,4,128,128]{3,2,1,0:T(8,128)(2,1)S(1)} %bitcast.12), channel_id=1, source_target_pairs={{2,4},{3,5},{4,2},{5,3},{10,12},{11,13},{12,10},{13,11},{18,20},{1... | collective-permute-start | bytes 1572872 | tf_op jit(solution)/shard_map/ppermute | solution.py:376
  3.3 29.5 %collective-permute-start.2 = (bf16[4,4,128,128]{3,2,1,0:T(8,128)(2,1)S(1)}, bf16[4,4,128,128]{3,2,1,0:T(8,128)(2,1)S(1)}, u32[]{:S(2)}, u32[]{:S(2)}) collective-permute-start(bf16[4,4,128,128]{3,2,1,0:T(8,128)(2,1)S(1)} %bitcast.13), channel_id=1, source_target_pairs={{0,4},{1,5},{6,2},{7,3},{8,12},{9,13},{14,10},{15,11},{16,20},{17,... | collective-permute-start | bytes 1572872 | tf_op jit(solution)/shard_map/ppermute | solution.py:376
  17.7 6.9 %collective-permute-start.4 = (s32[8,1,16]{2,1,0:T(1,128)S(1)}, s32[8,1,16]{2,1,0:T(1,128)S(1)}, u32[]{:S(2)}, u32[]{:S(2)}) collective-permute-start(s32[8,1,16]{2,1,0:T(1,128)S(1)} %get-tuple-element.41), channel_id=1, source_target_pairs={{6,4},{7,5},{0,2},{1,3},{14,12},{15,13},{8,10},{9,11},{22,20},{23,... | collective-permute-start | bytes 1544 | tf_op jit(solution)/shard_map/ppermute | solution.py:376
  24.7 13.8 %collective-permute-start.12 = (bf16[4,4,128,128]{3,2,1,0:T(8,128)(2,1)S(1)}, bf16[4,4,128,128]{3,2,1,0:T(8,128)(2,1)S(1)}, u32[]{:S(2)}, u32[]{:S(2)}) collective-permute-start(bf16[4,4,128,128]{3,2,1,0:T(8,128)(2,1)S(1)} %bitcast.5), channel_id=1, source_target_pairs={{0,2},{1,3},{2,0},{3,1},{4,6},{5,7},{6,4},{7,5},{8,10},{9,11},{10,... | collective-permute-start | bytes 1572872 | tf_op jit(solution)/shard_map/ppermute | solution.py:356
  27.8 12.0 %collective-permute-start.13 = (bf16[4,4,128,128]{3,2,1,0:T(8,128)(2,1)S(1)}, bf16[4,4,128,128]{3,2,1,0:T(8,128)(2,1)S(1)}, u32[]{:S(2)}, u32[]{:S(2)}) collective-permute-start(bf16[4,4,128,128]{3,2,1,0:T(8,128)(2,1)S(1)} %bitcast.6), channel_id=1, source_target_pairs={{2,4},{3,5},{4,2},{5,3},{10,12},{11,13},{12,10},{13,11},{18,20},{1... | collective-permute-start | bytes 1572872 | tf_op jit(solution)/shard_map/ppermute | solution.py:376
  28.5 20.3 %collective-permute-start.14 = (bf16[4,4,128,128]{3,2,1,0:T(8,128)(2,1)S(1)}, bf16[4,4,128,128]{3,2,1,0:T(8,128)(2,1)S(1)}, u32[]{:S(2)}, u32[]{:S(2)}) collective-permute-start(bf16[4,4,128,128]{3,2,1,0:T(8,128)(2,1)S(1)} %bitcast.7), channel_id=1, source_target_pairs={{0,4},{1,5},{6,2},{7,3},{8,12},{9,13},{14,10},{15,11},{16,20},{17,... | collective-permute-start | bytes 1572872 | tf_op jit(solution)/shard_map/ppermute | solution.py:376
  33.8 16.2 %collective-permute-start.6 = (bf16[4,4,128,128]{3,2,1,0:T(8,128)(2,1)S(1)}, bf16[4,4,128,128]{3,2,1,0:T(8,128)(2,1)S(1)}, u32[]{:S(2)}, u32[]{:S(2)}) collective-permute-start(bf16[4,4,128,128]{3,2,1,0:T(8,128)(2,1)S(1)} %get-tuple-element.45), channel_id=1, source_target_pairs={{0,1},{1,0},{2,3},{3,2},{4,5},{5,4},{6,7},{7,6},{8,9},{9,8},{10,11... | collective-permute-start | bytes 1572872 | tf_op jit(solution)/shard_map/ppermute | solution.py:356
  34.1 16.6 %collective-permute-start.7 = (bf16[4,4,128,128]{3,2,1,0:T(8,128)(2,1)S(1)}, bf16[4,4,128,128]{3,2,1,0:T(8,128)(2,1)S(1)}, u32[]{:S(2)}, u32[]{:S(2)}) collective-permute-start(bf16[4,4,128,128]{3,2,1,0:T(8,128)(2,1)S(1)} %get-tuple-element.46), channel_id=1, source_target_pairs={{2,3},{3,2},{4,5},{5,4},{10,11},{11,10},{12,13},{13,12},{18,19},{1... | collective-permute-start | bytes 1572872 | tf_op jit(solution)/shard_map/ppermute | solution.py:376
  38.5 13.5 %collective-permute-start.8 = (bf16[4,4,128,128]{3,2,1,0:T(8,128)(2,1)S(1)}, bf16[4,4,128,128]{3,2,1,0:T(8,128)(2,1)S(1)}, u32[]{:S(2)}, u32[]{:S(2)}) collective-permute-start(bf16[4,4,128,128]{3,2,1,0:T(8,128)(2,1)S(1)} %get-tuple-element.47), channel_id=1, source_target_pairs={{4,6},{5,7},{2,0},{3,1},{12,14},{13,15},{10,8},{11,9},{20,22},{21,... | collective-permute-start | bytes 1572872 | tf_op jit(solution)/shard_map/ppermute | solution.py:376
  39.8 21.7 %collective-permute-start.9 = (bf16[4,4,128,128]{3,2,1,0:T(8,128)(2,1)S(1)}, bf16[4,4,128,128]{3,2,1,0:T(8,128)(2,1)S(1)}, u32[]{:S(2)}, u32[]{:S(2)}) collective-permute-start(bf16[4,4,128,128]{3,2,1,0:T(8,128)(2,1)S(1)} %get-tuple-element.48), channel_id=1, source_target_pairs={{4,7},{5,6},{2,1},{3,0},{12,15},{13,14},{10,9},{11,8},{20,23},{21,... | collective-permute-start | bytes 1572872 | tf_op jit(solution)/shard_map/ppermute | solution.py:376
  49.6 25.4 %collective-permute-start.15 = (bf16[4,4,128,128]{3,2,1,0:T(8,128)(2,1)S(1)}, bf16[4,4,128,128]{3,2,1,0:T(8,128)(2,1)S(1)}, u32[]{:S(2)}, u32[]{:S(2)}) collective-permute-start(bf16[4,4,128,128]{3,2,1,0:T(8,128)(2,1)S(1)} %get-tuple-element.51), channel_id=1, source_target_pairs={{0,1},{1,0},{2,3},{3,2},{4,5},{5,4},{6,7},{7,6},{8,9},{9,8},{10,11... | collective-permute-start | bytes 1572872 | tf_op jit(solution)/shard_map/ppermute | solution.py:356
  50.0 25.1 %collective-permute-start.16 = (bf16[4,4,128,128]{3,2,1,0:T(8,128)(2,1)S(1)}, bf16[4,4,128,128]{3,2,1,0:T(8,128)(2,1)S(1)}, u32[]{:S(2)}, u32[]{:S(2)}) collective-permute-start(bf16[4,4,128,128]{3,2,1,0:T(8,128)(2,1)S(1)} %get-tuple-element.52), channel_id=1, source_target_pairs={{2,3},{3,2},{4,5},{5,4},{10,11},{11,10},{12,13},{13,12},{18,19},{1... | collective-permute-start | bytes 1572872 | tf_op jit(solution)/shard_map/ppermute | solution.py:376
  50.7 16.5 %collective-permute-start.17 = (bf16[2,4,128,128]{3,2,1,0:T(8,128)(2,1)S(1)}, bf16[2,4,128,128]{3,2,1,0:T(8,128)(2,1)S(1)}, u32[]{:S(2)}, u32[]{:S(2)}) collective-permute-start(bf16[2,4,128,128]{3,2,1,0:T(8,128)(2,1)S(1)} %get-tuple-element.53), channel_id=1, source_target_pairs={{4,6},{5,7},{2,0},{3,1},{12,14},{13,15},{10,8},{11,9},{20,22},{21,... | collective-permute-start | bytes 786440 | tf_op jit(solution)/shard_map/ppermute | solution.py:376
  52.0 20.5 %collective-permute-start.18 = (bf16[2,4,128,128]{3,2,1,0:T(8,128)(2,1)S(1)}, bf16[2,4,128,128]{3,2,1,0:T(8,128)(2,1)S(1)}, u32[]{:S(2)}, u32[]{:S(2)}) collective-permute-start(bf16[2,4,128,128]{3,2,1,0:T(8,128)(2,1)S(1)} %get-tuple-element.54), channel_id=1, source_target_pairs={{4,7},{5,6},{2,1},{3,0},{12,15},{13,14},{10,9},{11,8},{20,23},{21,... | collective-permute-start | bytes 786440 | tf_op jit(solution)/shard_map/ppermute | solution.py:376
  61.5 17.1 %collective-permute-start.22 = (bf16[2,4,128,128]{3,2,1,0:T(8,128)(2,1)S(1)}, bf16[2,4,128,128]{3,2,1,0:T(8,128)(2,1)S(1)}, u32[]{:S(2)}, u32[]{:S(2)}) collective-permute-start(bf16[2,4,128,128]{3,2,1,0:T(8,128)(2,1)S(1)} %get-tuple-element.57), channel_id=1, source_target_pairs={{4,6},{5,7},{2,0},{3,1},{12,14},{13,15},{10,8},{11,9},{20,22},{21,... | collective-permute-start | bytes 786440 | tf_op jit(solution)/shard_map/ppermute | solution.py:376
  67.2 16.5 %collective-permute-start.23 = (bf16[2,4,128,128]{3,2,1,0:T(8,128)(2,1)S(1)}, bf16[2,4,128,128]{3,2,1,0:T(8,128)(2,1)S(1)}, u32[]{:S(2)}, u32[]{:S(2)}) collective-permute-start(bf16[2,4,128,128]{3,2,1,0:T(8,128)(2,1)S(1)} %get-tuple-element.58), channel_id=1, source_target_pairs={{4,7},{5,6},{2,1},{3,0},{12,15},{13,14},{10,9},{11,8},{20,23},{21,... | collective-permute-start | bytes 786440 | tf_op jit(solution)/shard_map/ppermute | solution.py:376
  72.5 17.4 %collective-permute-start.11 = (bf16[4,4,128,128]{3,2,1,0:T(8,128)(2,1)S(1)}, bf16[4,4,128,128]{3,2,1,0:T(8,128)(2,1)S(1)}, u32[]{:S(2)}, u32[]{:S(2)}) collective-permute-start(bf16[4,4,128,128]{3,2,1,0:T(8,128)(2,1)S(1)} %spatial.3.refs_0_), channel_id=1, source_target_pairs={{0,16},{8,24},{1,17},{9,25},{2,18},{10,26},{3,19},{11,27},{4,20},{... | collective-permute-start | bytes 1572872 | tf_op jit(solution)/shard_map/ppermute | solution.py:413
  77.3 19.2 %collective-permute-start.21 = (bf16[4,2,128,128]{3,2,1,0:T(8,128)(2,1)S(1)}, bf16[4,2,128,128]{3,2,1,0:T(8,128)(2,1)S(1)}, u32[]{:S(2)}, u32[]{:S(2)}) collective-permute-start(bf16[4,2,128,128]{3,2,1,0:T(8,128)(2,1)S(1)} %spatial.4.refs_4_), channel_id=1, source_target_pairs={{0,16},{8,24},{1,17},{9,25},{2,18},{10,26},{3,19},{11,27},{4,20},{... | collective-permute-start | bytes 786440 | tf_op jit(solution)/shard_map/ppermute | solution.py:413
  85.9 11.9 %collective-permute-start.26 = (bf16[4,2,128,128]{3,2,1,0:T(8,128)(2,1)S(1)}, bf16[4,2,128,128]{3,2,1,0:T(8,128)(2,1)S(1)}, u32[]{:S(2)}, u32[]{:S(2)}) collective-permute-start(bf16[4,2,128,128]{3,2,1,0:T(8,128)(2,1)S(1)} %spatial.5.refs_8_), channel_id=1, source_target_pairs={{0,16},{8,24},{1,17},{9,25},{2,18},{10,26},{3,19},{11,27},{4,20},{... | collective-permute-start | bytes 786440 | tf_op jit(solution)/shard_map/ppermute | solution.py:413
  87.2 17.4 %collective-permute-start.10 = (bf16[4,4,128,128]{3,2,1,0:T(8,128)(2,1)S(1)}, bf16[4,4,128,128]{3,2,1,0:T(8,128)(2,1)S(1)}, u32[]{:S(2)}, u32[]{:S(2)}) collective-permute-start(bf16[4,4,128,128]{3,2,1,0:T(8,128)(2,1)S(1)} %spatial.3.refs_0_), channel_id=1, source_target_pairs={{0,8},{16,24},{1,9},{17,25},{2,10},{18,26},{3,11},{19,27},{4,12},{... | collective-permute-start | bytes 1572872 | tf_op jit(solution)/shard_map/ppermute | solution.py:413
  88.5 14.1 %collective-permute-start.20 = (bf16[4,2,128,128]{3,2,1,0:T(8,128)(2,1)S(1)}, bf16[4,2,128,128]{3,2,1,0:T(8,128)(2,1)S(1)}, u32[]{:S(2)}, u32[]{:S(2)}) collective-permute-start(bf16[4,2,128,128]{3,2,1,0:T(8,128)(2,1)S(1)} %spatial.4.refs_4_), channel_id=1, source_target_pairs={{0,8},{16,24},{1,9},{17,25},{2,10},{18,26},{3,11},{19,27},{4,12},{... | collective-permute-start | bytes 786440 | tf_op jit(solution)/shard_map/ppermute | solution.py:413
  89.9 16.2 %collective-permute-start.19 = (bf16[4,4,128,128]{3,2,1,0:T(8,128)(2,1)S(1)}, bf16[4,4,128,128]{3,2,1,0:T(8,128)(2,1)S(1)}, u32[]{:S(2)}, u32[]{:S(2)}) collective-permute-start(bf16[4,4,128,128]{3,2,1,0:T(8,128)(2,1)S(1)} %collective-permute-done.11.refs_2_), channel_id=1, source_target_pairs={{16,24},{24,16},{17,25},{25,17},{18,26},{26,18},{19,27},{27,19},{2... | collective-permute-start | bytes 1572872 | tf_op jit(solution)/shard_map/ppermute | solution.py:423
  96.6 8.0 %collective-permute-start.25 = (bf16[4,2,128,128]{3,2,1,0:T(8,128)(2,1)S(1)}, bf16[4,2,128,128]{3,2,1,0:T(8,128)(2,1)S(1)}, u32[]{:S(2)}, u32[]{:S(2)}) collective-permute-start(bf16[4,2,128,128]{3,2,1,0:T(8,128)(2,1)S(1)} %spatial.5.refs_8_), channel_id=1, source_target_pairs={{0,8},{16,24},{1,9},{17,25},{2,10},{18,26},{3,11},{19,27},{4,12},{... | collective-permute-start | bytes 786440 | tf_op jit(solution)/shard_map/ppermute | solution.py:413
  (14 other events, 77.7 us)

commit v4 on v3

--- a/solution.py
+++ b/solution.py
@@ -44,9 +44,7 @@
     return pl.CostEstimate(flops=int(us * 1.15e9), bytes_accessed=1024, transcendentals=0)
 
 
-def prepare_kernel(rows, count, inner, forward, at_ref, *refs):
-    cols_ref, pos_ref, qkv_ref, proj_ref, gain_ref, up_ref, down_ref, space_ref = refs[:8]
-    want_o, slot_o, pos_o, qkv_o, proj_o, gain_o, up_o, down_o, space_o, pos_s = refs[8:]
+def lists_kernel(rows, count, inner, forward, at_ref, cols_ref, want_o, slot_o):
     me = at_ref[0]
     cols = cols_ref[...]
     rel = (cols // rows) ^ me
@@ -62,16 +60,12 @@
         second = jnp.where(loc == low, 0, 1)
         if forward:
             o = me // inner
-            middle = jnp.where((o == 1) | (o == 2), 1, 0)
-            half = (k // 2 - 2) * 2
-            if k in (0, 2):
-                at = (k // 2) * rows + loc
-            elif k in (1, 3):
-                at = 4 * rows + (k // 2) * 2 + second
-            elif k % 2 == 0:
-                at = jnp.where(middle == 1, (3 if k == 4 else 2) * rows + loc, 6 * rows + half + second)
+            middle = (o == 1) | (o == 2)
+            inside = {4: 3 * rows + loc, 5: 7 * rows + second, 6: 2 * rows + loc, 7: 6 * rows + second}
+            if k < 4:
+                at = {0: loc, 1: 4 * rows + second, 2: rows + loc, 3: 5 * rows + second}[k]
             else:
-                at = (7 - 2 * middle) * rows + half + second
+                at = jnp.where(middle, inside[k], (4 + k) * rows + second)
         elif k < inner:
             at = k * rows + loc
         else:
@@ -79,6 +73,28 @@
         slots = jnp.where(hit, at, slots)
     slot_o[...] = slots
 
+
+def lists(at, cols, rows, count, inner, forward):
+    outs = [
+        jax.ShapeDtypeStruct((cols.shape[0], 1, 2 * count), jnp.int32),
+        jax.ShapeDtypeStruct(cols.shape, jnp.int32),
+    ]
+    return pl.pallas_call(
+        functools.partial(lists_kernel, rows, count, inner, forward),
+        grid_spec=pltpu.PrefetchScalarGridSpec(
+            num_scalar_prefetch=1,
+            grid=(1,),
+            in_specs=[whole(cols)],
+            out_specs=[whole(a) for a in outs],
+        ),
+        out_shape=outs,
+        cost_estimate=cost(1),
+        name="lists",
+    )(at, cols)
+
+
+def weights_kernel(at_ref, pos_ref, qkv_ref, proj_ref, gain_ref, up_ref, down_ref, space_ref, *refs):
+    pos_o, qkv_o, proj_o, gain_o, up_o, down_o, space_o, pos_s = refs
     width = proj_ref.shape[0]
     head_dim = width // HEADS
     snaps = pos_o.shape[0]
@@ -100,15 +116,11 @@
     space_o[...] = flip(space_ref[...])
 
 
-def prepare(at, cols, positions, weights, rows, count, inner, forward):
-    snaps = cols.shape[0]
-    qkv, proj, gain, up, down, space = weights
+def turned(at, snaps, positions, qkv, proj, gain, up, down, space):
     width = proj.shape[0]
-    ins = [cols, positions, qkv, proj, gain.reshape(1, width), up, down, space]
+    ins = [positions, qkv, proj, gain.reshape(1, width), up, down, space]
     shape = jax.ShapeDtypeStruct
     outs = [
-        shape((snaps, 1, 2 * count), jnp.int32),
-        shape(cols.shape, jnp.int32),
         shape((snaps, width), F32),
         shape((3 * width, width), BF16),
         shape((width, width), BF16),
@@ -118,7 +130,7 @@
         shape((width, width), BF16),
     ]
     return pl.pallas_call(
-        functools.partial(prepare_kernel, rows, count, inner, forward),
+        weights_kernel,
         grid_spec=pltpu.PrefetchScalarGridSpec(
             num_scalar_prefetch=1,
             grid=(1,),
@@ -128,7 +140,8 @@
         ),
         out_shape=outs,
         compiler_params=pltpu.CompilerParams(vmem_limit_bytes=VMEM),
-        name="prepare",
+        cost_estimate=cost(2),
+        name="turn_weights",
     )(at, *ins)
 
 
@@ -154,14 +167,14 @@
         grid_spec=pltpu.PrefetchScalarGridSpec(
             num_scalar_prefetch=len(wants),
             grid=(1,),
-            in_specs=[whole(srcs[0])] + [pl.BlockSpec(memory_space=pltpu.VMEM)] * (len(srcs) - 1),
+            in_specs=[pl.BlockSpec(memory_space=pltpu.VMEM)] * len(srcs),
             out_specs=[whole(a) for a in shapes],
         ),
         out_shape=shapes,
         compiler_params=pltpu.CompilerParams(vmem_limit_bytes=VMEM),
-        cost_estimate=cost(3),
+        cost_estimate=cost(1),
         name="pick_blocks",
-    )(*wants, srcs[0], *[near(a) for a in srcs[1:]])
+    )(*wants, *[near(a) for a in srcs])
 
 
 def spatial_kernel(start, offsets, slot_ref, vals_ref, weight_ref, pos_ref, *refs):
@@ -178,7 +191,9 @@
     unit = 1
     for src, offset in zip(srcs[1:], offsets[1:]):
         for first in range(0, src.shape[1], rows):
-            held[unit] = src[start - offset : start - offset + snaps, first : first + rows]
+            n = min(rows, src.shape[1] - first)
+            some = src[start - offset : start - offset + snaps, first : first + n]
+            held[unit, :, :n] = some
             unit += 1
     own.wait()
     for s in range(snaps):
@@ -205,7 +220,7 @@
     rows, tiles, size, _ = vals.shape[1:]
     snaps = stop - start
     width = weight_t.shape[0]
-    units = sum(a.shape[1] for a, _ in srcs) // rows
+    units = sum(-(-a.shape[1] // rows) for a, _ in srcs)
     anywhere = pl.BlockSpec(memory_space=pl.ANY)
     out = jax.ShapeDtypeStruct((rows // parts, snaps, width, size), BF16)
     return pl.pallas_call(
@@ -226,7 +241,7 @@
         ),
         out_shape=[out] * parts,
         compiler_params=pltpu.CompilerParams(vmem_limit_bytes=VMEM),
-        cost_estimate=cost(2 * snaps),
+        cost_estimate=cost(snaps),
         name="spatial",
     )(slots, vals, weight_t, pos, srcs[0][0], *[near(a) for a, _ in srcs[1:]])
 
@@ -238,12 +253,12 @@
     snaps = sum(sizes)
     width, lanes = arrays[0].shape[2:]
     head_dim = width // HEADS
-    me = me_ref[0]
+    me, g = me_ref[0], pl.program_id(0)
     scale = 1.0 / (CAP * math.sqrt(head_dim))
     steep = CAP * math.log2(math.e)
 
     def held(i):
-        return [arrays[c * count + i][0, s] for c, n in enumerate(sizes) for s in range(n)]
+        return [arrays[c * count + i][g, s] for c, n in enumerate(sizes) for s in range(n)]
 
     def project(i):
         skip = 0 if i == 0 else width
@@ -314,27 +329,21 @@
             out_ref[h * half + i] = out[:, i * lanes : (i + 1) * lanes].T.astype(BF16)
 
 
-def temporal(me, weights, chunks, first, groups, total, so_far):
-    width, lanes = chunks[0][0].shape[2:]
+def temporal(me, weights, chunks):
+    groups, _, width, lanes = chunks[0][0].shape
     count = len(chunks[0])
     sizes = [chunk[0].shape[1] for chunk in chunks]
     snaps = sum(sizes)
 
-    def part(a):
-        at = first if a.shape[0] == total else 0
-        return pl.BlockSpec((1,) + a.shape[1:], lambda g, i: (g + at, 0, 0, 0))
-
     parts = [a for chunk in chunks for a in chunk]
-    extra = [] if so_far is None else [so_far]
     return pl.pallas_call(
         functools.partial(temporal_kernel, sizes, count - 1),
         grid_spec=pltpu.PrefetchScalarGridSpec(
             num_scalar_prefetch=1,
             grid=(groups,),
             in_specs=[whole(a) for a in weights]
-            + [part(a) for a in parts]
-            + [pl.BlockSpec(memory_space=pl.ANY)] * len(extra),
-            out_specs=pl.BlockSpec((snaps, lanes, width), lambda g, i: (0, g + first, 0)),
+            + [pl.BlockSpec(memory_space=pltpu.VMEM)] * len(parts),
+            out_specs=pl.BlockSpec((snaps, lanes, width), lambda g, i: (0, g, 0)),
             scratch_shapes=[
                 pltpu.VMEM((snaps * count, width, lanes), F32),
                 pltpu.VMEM((snaps * count, width, lanes), F32),
@@ -344,12 +353,11 @@
                 pltpu.VMEM((width, snaps * lanes), BF16),
             ],
         ),
-        out_shape=jax.ShapeDtypeStruct((snaps, total * lanes, width), BF16),
-        input_output_aliases={1 + len(weights) + len(parts): 0} if extra else {},
+        out_shape=jax.ShapeDtypeStruct((snaps, groups * lanes, width), BF16),
         compiler_params=pltpu.CompilerParams(vmem_limit_bytes=VMEM),
         cost_estimate=cost(10),
         name="temporal",
-    )(me, *weights, *parts, *extra)
+    )(me, *weights, *[near(a) for a in parts])
 
 
 def send(a, k):
@@ -367,7 +375,7 @@
     ]
     picked = pick(layer, [0] * inner, wants, jobs)
     arrived = [send(picked[k - 1], k * inner) for k in range(1, outer)]
-    return [(0, snaps, [(a, 0) for a in layer + arrived])]
+    return [(0, snaps, lambda before: [(a, 0) for a in layer + arrived])]
 
 
 def exchange_forward(blocks, want):
@@ -375,33 +383,41 @@
     layers = lambda pairs, x=0: [(a * 2 + i, b * 2 + (i ^ x)) for a, b in pairs for i in range(2)]
     go = lambda a, pairs, x=0: lax.ppermute(a, "vert", layers(pairs, x))
     cross = [(1, 2), (2, 1)]
-    skip = [(0, 2), (3, 1)]
     ends = [(2, 3), (1, 0)]
     back = [(3, 2), (0, 1)]
-
-    cut = snaps // 2
-    first, rest = blocks[:cut], blocks[cut:]
-    p1, p2, beside = go(first, cross), go(first, skip), send(first, 2)
-    wants = [send(want, 1), go(want, back), go(want, back, 1)]
-    rest, *wants = after((rest, *wants))
-
-    def forward(own, beside, p1, p2, lo, cuts):
-        srcs, hi = [own, beside, p1, p2], cuts[-1]
-        jobs = [(0, [(0, 1), (1, 3)], lo, hi), (0, [(3, 5), (2, 7)], lo, hi)]
-        spans = list(zip([lo] + cuts, cuts))
-        for span in spans:
-            jobs += [(1, [(2, 4), (3, 6)], *span), (2, [(2, 5), (3, 7)], *span)]
-        x1, x2, *ends_of = pick(srcs, [lo] * 4, wants, jobs)
-        sent = [(go(ends_of[2 * i], ends), go(ends_of[2 * i + 1], ends, 1)) for i in range(len(spans))]
-        x1, x2 = send(x1, 1), go(x2, [(1, 1), (2, 2)], 1)
-        return [
-            (first, stop, [(a, lo) for a in (*srcs, x1, x2)] + [(a, first) for a in pair])
-            for (first, stop), pair in zip(spans, sent)
-        ]
-
-    parts = forward(first, beside, p1, p2, 0, [cut])
-    q1, q2, far = go(rest, cross), go(rest, skip), send(rest, 2)
-    return parts + forward(rest, far, q1, q2, cut, [cut + (snaps - cut) // 2, snaps])
+    inside = [(1, 1), (2, 2)]
+
+    p1, beside = go(blocks, cross), send(blocks, 2)
+    wants = [send(want, 1), None, None]
+    (xo,) = pick([blocks], [0], wants[:1], [(0, [(0, 1)], 0, snaps)])
+    xo = send(xo, 1)
+    both = go(jnp.concatenate([want, wants[0]], axis=1), back)
+    beside, both, xo, p1 = after((beside, both, xo, p1))
+    wants[1:] = both[:, :1], both[:, 1:]
+
+    p2 = go(beside, cross)
+    jobs = [(1, [(0, 4)], 0, snaps), (2, [(0, 5)], 0, snaps), (0, [(0, 7)], 0, snaps)]
+    f0, f1, x1, xn = pick([p1, beside], [0, 0], wants, jobs + [(0, [(1, 3)], 0, snaps)])
+    f0, f1, x1, xn = go(f0, ends), go(f1, ends, 1), go(x1, inside, 1), send(xn, 1)
+
+    cuts = sorted({0, snaps // 4, -(-5 * snaps // 8), snaps})
+    spans = list(zip(cuts, cuts[1:]))
+    jobs = [(0, [(0, 5)], 0, snaps)]
+    for span in spans:
+        jobs += [(1, [(0, 6)], *span), (2, [(0, 7)], *span)]
+    x2, *late = pick([p2], [0], wants, jobs)
+    x2 = go(x2, inside, 1)
+    all_snaps = [(a, 0) for a in (blocks, beside, p1, p2, xo, xn, x1, x2, f0, f1)]
+
+    def part(span, a, b):
+        def get(before):
+            pair = (a, b) if before is None else after((a, b, before))[:2]
+            sent = go(pair[0], ends), go(pair[1], ends, 1)
+            return all_snaps + [(c, span[0]) for c in sent]
+
+        return (*span, get)
+
+    return [part(span, a, b) for span, a, b in zip(spans, late[::2], late[1::2])]
 
 
 def gather_times(own):
@@ -445,21 +461,25 @@
     blocks = features.reshape(snaps, rows, size, width)
 
     forward = (outer, inner) == (4, 2)
-    weights = (attn_proj, attn_out, norm_gain, mlp_up, mlp_down, space_weight)
-    want, slots, pos, *weights, space_t = prepare(
-        jnp.stack([me_v, me_t]), tile_cols, positions, weights, rows, count, inner, forward
+    at = jnp.stack([me_v, me_t])
+    want, slots = lists(at, tile_cols, rows, count, inner, forward)
+    pos, *weights, space_t = turned(
+        at, snaps, positions, attn_proj, attn_out, norm_gain, mlp_up, mlp_down, space_weight
     )
     me = me_t.reshape(1)
     parts = exchange_forward(blocks, want) if forward else exchange_direct(blocks, want, inner)
 
     started, owns = [], []
-    for start, stop, srcs in parts:
+    held = [get(None) for _, _, get in parts[:2]]
+    for c, (start, stop, get) in enumerate(parts):
+        srcs = held[c] if c < 2 else get(owns[c - 2])
         if owns:
-            srcs[0] = (after((srcs[0][0], owns[-1]))[0], srcs[0][1])
+            sent = [a for a in started[c - 2] if a is not None] if c > 1 else []
+            srcs = [(after((srcs[0][0], owns[-1], *sent))[0], srcs[0][1])] + srcs[1:]
         owns.append(spatial(slots, tile_vals, start, stop, space_t, pos, srcs, 1)[0])
         started.append(gather_times(owns[-1]))
     chunks = [pass_on(got, own) for got, own in zip(started, owns[1:] + owns[-1:])]
-    return temporal(me, weights, chunks, 0, rows, rows, None)
+    return temporal(me, weights, chunks)
 
 
 def solution(mesh):

time: 127 us -> 125 us (0.984)
  local copies, waits for them, and re-layouts: 7.57 us -> 1.29 us
  starting transfers between devices: 52.1 us -> 45.9 us
  waiting for transfers between devices: 35 us -> 39.9 us
  Pallas kernels: 30.4 us -> 33.5 us
    ppermute x14 -> x13, starting transfers between devices: 24.6 us -> 19.2 us  [exchange_forward(): go = lambda a, pairs, x=0: lax.ppermute(a, 'vert', layers(pairs, x))]
    unnamed x20 -> x26, local copies, waits for them, and re-layouts: 6.3 us -> 1.29 us
    ppermute x14 -> x13, waiting for transfers between devices: 28.6 us -> 32 us  [exchange_forward(): go = lambda a, pairs, x=0: lax.ppermute(a, 'vert', layers(pairs, x))]
    pallas_call x1 -> x2, Pallas kernels: 1.21 us -> 3.43 us  [the longest x1 2.65 us: lists(): pl.pallas_call(functools.partial(lists_kernel, rows, count, inner, forwar...]
    ppermute x5 -> x4, waiting for transfers between devices: 4.92 us -> 6.38 us  [send(): lax.ppermute(a, 'vert', [(v, v ^ k) for v in range(lax.axis_size('vert'))])]
    ppermute x5 -> x4, starting transfers between devices: 6.41 us -> 5.06 us  [send(): lax.ppermute(a, 'vert', [(v, v ^ k) for v in range(lax.axis_size('vert'))])]
  transfers between devices with their start and end apart: 28 -> 26, of which waited for: 10 -> 12; matrix products, arithmetic and copies ran while one was open for 0% -> 1% of each run, Pallas kernels for 9% -> 11%
where the time goes in v4:
time: 125 us; the launch traced here: 122 us
  starting transfers between devices  45.9 us (37%)
  waiting for transfers between devices  39.9 us (32%)
  Pallas kernels  33.5 us (27%)
  other arithmetic  1.32 us (1%)
  local copies, waits for them, and re-layouts  1.29 us (1%)
    ppermute x13, waiting for transfers between devices, exchange_forward(): go = lambda a, pairs, x=0: lax.ppermute(a, 'vert', layers(pairs, x))  32 us
    pallas_call x1, Pallas kernels, temporal(): pl.pallas_call(functools.partial(temporal_kernel, sizes, count - 1), grid...  19.6 us
    ppermute x13, starting transfers between devices, exchange_forward(): go = lambda a, pairs, x=0: lax.ppermute(a, 'vert', layers(pairs, x))  19.2 us
    ppermute x3, starting transfers between devices, pass_on(): got[k] = lax.ppermute(got[k - 1], 'tm', pairs)  13.9 us
    pallas_call x3, Pallas kernels, spatial(): pl.pallas_call(functools.partial(spatial_kernel, start, [first for _, fir...  8.21 us
    ppermute x6, starting transfers between devices, gather_times(): got[k] = lax.ppermute(own, 'tm', pairs)  7.75 us
    ppermute x4, waiting for transfers between devices, send(): lax.ppermute(a, 'vert', [(v, v ^ k) for v in range(lax.axis_size('vert'))])  6.38 us
    ppermute x4, starting transfers between devices, send(): lax.ppermute(a, 'vert', [(v, v ^ k) for v in range(lax.axis_size('vert'))])  5.06 us
  transfers between devices with their start and end apart: 26, of which 12 were waited for; matrix products, arithmetic and copies ran while one was open for 1% of the time, Pallas kernels for 11%

profile of v4, /device:TPU:5, one launch (start us, length us, event | category | flops | bytes accessed | tf_op | source)
XLA Modules:
  0.0 122.4 jit_solution(12490326772323331643)
XLA Ops:
  0.0 1.3 %collective-permute-start = (bf16[8,4,128,128]{3,2,1,0:T(8,128)(2,1)}, bf16[8,4,128,128]{3,2,1,0:T(8,128)(2,1)S(1)}, u32[]{:S(2)}, u32[]{:S(2)}) collective-permute-start(bf16[8,4,128,128]{3,2,1,0:T(8,128)(2,1)} %bitcast.6), channel_id=1, source_target_pairs={{0,2},{1,3},{2,0},{3,1},{4,6},{5,7},{6,4},{7,5},{8,10},{9,11},{10,... | collective-permute-start | bytes 3145736 | tf_op jit(solution)/shard_map/ppermute | solution.py:364
  2.7 2.7 %lists.1 = (s32[8,1,16]{2,1,0:T(1,128)}, s32[8,4,8]{2,1,0:T(4,128)}) custom-call(s32[2]{0:T(128)} %pad_add_fusion.1.at_ref, s32[8,4,8]{2,1,0:T(4,128)} %cols_ref.1), custom_call_target="tpu_custom_call" | custom-call | flops 1150000000 | bytes 1024 | tf_op jit(solution)/shard_map/lists/pallas_call | solution.py:82
  6.6 1.8 %collective-permute-done.1.refs_0_ = s32[8,1,16]{2,1,0:T(1,128)S(1)} collective-permute-done((s32[8,1,16]{2,1,0:T(1,128)}, s32[8,1,16]{2,1,0:T(1,128)S(1)}, u32[]{:S(2)}, u32[]{:S(2)}) %collective-permute-start.1) | collective-permute-done | bytes 544 | tf_op jit(solution)/shard_map/ppermute | solution.py:364
  12.2 5.7 %collective-permute-start.2 = (s32[8,2,16]{2,1,0:T(2,128)S(1)}, s32[8,2,16]{2,1,0:T(2,128)S(1)}, u32[]{:S(2)}, u32[]{:S(2)}) collective-permute-start(s32[8,2,16]{2,1,0:T(2,128)S(1)} %pad_add_fusion), channel_id=1, source_target_pairs={{6,4},{7,5},{0,2},{1,3},{14,12},{15,13},{8,10},{9,11},{22,20},{23,... | collective-permute-start | bytes 3080 | tf_op jit(solution)/shard_map/ppermute | solution.py:384
  17.9 5.7 %collective-permute-done.2 = s32[8,2,16]{2,1,0:T(2,128)S(1)} collective-permute-done((s32[8,2,16]{2,1,0:T(2,128)S(1)}, s32[8,2,16]{2,1,0:T(2,128)S(1)}, u32[]{:S(2)}, u32[]{:S(2)}) %collective-permute-start.2) | collective-permute-done | bytes 1056 | tf_op jit(solution)/shard_map/ppermute | solution.py:384
  25.9 1.4 %collective-permute-start.10 = (bf16[8,2,128,128]{3,2,1,0:T(8,128)(2,1)S(1)}, bf16[8,2,128,128]{3,2,1,0:T(8,128)(2,1)S(1)}, u32[]{:S(2)}, u32[]{:S(2)}) collective-permute-start(bf16[8,2,128,128]{3,2,1,0:T(8,128)(2,1)S(1)} %get-tuple-element.53), channel_id=1, source_target_pairs={{4,7},{5,6},{2,1},{3,0},{12,15},{13,14},{10,9},{11,8},{20,23},{21,... | collective-permute-start | bytes 1572872 | tf_op jit(solution)/shard_map/ppermute | solution.py:384
  29.3 1.3 %collective-permute-start.9 = (bf16[8,2,128,128]{3,2,1,0:T(8,128)(2,1)S(1)}, bf16[8,2,128,128]{3,2,1,0:T(8,128)(2,1)S(1)}, u32[]{:S(2)}, u32[]{:S(2)}) collective-permute-start(bf16[8,2,128,128]{3,2,1,0:T(8,128)(2,1)S(1)} %get-tuple-element.52), channel_id=1, source_target_pairs={{4,6},{5,7},{2,0},{3,1},{12,14},{13,15},{10,8},{11,9},{20,22},{21,... | collective-permute-start | bytes 1572872 | tf_op jit(solution)/shard_map/ppermute | solution.py:384
  32.2 12.9 %collective-permute-done.10.refs_9_ = bf16[8,2,128,128]{3,2,1,0:T(8,128)(2,1)S(1)} collective-permute-done((bf16[8,2,128,128]{3,2,1,0:T(8,128)(2,1)S(1)}, bf16[8,2,128,128]{3,2,1,0:T(8,128)(2,1)S(1)}, u32[]{:S(2)}, u32[]{:S(2)}) %collective-permute-start.10) | collective-permute-done | bytes 524320 | tf_op jit(solution)/shard_map/ppermute | solution.py:384
  45.0 1.5 %collective-permute-start.11 = (bf16[2,2,128,128]{3,2,1,0:T(8,128)(2,1)S(1)}, bf16[2,2,128,128]{3,2,1,0:T(8,128)(2,1)S(1)}, u32[]{:S(2)}, u32[]{:S(2)}) collective-permute-start(bf16[2,2,128,128]{3,2,1,0:T(8,128)(2,1)S(1)} %get-tuple-element.54), channel_id=1, source_target_pairs={{4,6},{5,7},{2,0},{3,1},{12,14},{13,15},{10,8},{11,9},{20,22},{21,... | collective-permute-start | bytes 393224 | tf_op jit(solution)/shard_map/ppermute | solution.py:384
  46.6 3.9 %collective-permute-done.6.refs_5_ = bf16[8,2,128,128]{3,2,1,0:T(8,128)(2,1)S(1)} collective-permute-done((bf16[8,2,128,128]{3,2,1,0:T(8,128)(2,1)S(1)}, bf16[8,2,128,128]{3,2,1,0:T(8,128)(2,1)S(1)}, u32[]{:S(2)}, u32[]{:S(2)}) %collective-permute-start.6) | collective-permute-done | bytes 524320 | tf_op jit(solution)/shard_map/ppermute | solution.py:364
  52.7 1.3 %collective-permute-start.15 = (bf16[3,2,128,128]{3,2,1,0:T(8,128)(2,1)S(1)}, bf16[3,2,128,128]{3,2,1,0:T(8,128)(2,1)S(1)}, u32[]{:S(2)}, u32[]{:S(2)}) collective-permute-start(bf16[3,2,128,128]{3,2,1,0:T(8,128)(2,1)S(1)} %get-tuple-element.57), channel_id=1, source_target_pairs={{4,6},{5,7},{2,0},{3,1},{12,14},{13,15},{10,8},{11,9},{20,22},{21,... | collective-permute-start | bytes 589832 | tf_op jit(solution)/shard_map/ppermute | solution.py:384
  54.0 1.4 %collective-permute-done.9.refs_8_ = bf16[8,2,128,128]{3,2,1,0:T(8,128)(2,1)S(1)} collective-permute-done((bf16[8,2,128,128]{3,2,1,0:T(8,128)(2,1)S(1)}, bf16[8,2,128,128]{3,2,1,0:T(8,128)(2,1)S(1)}, u32[]{:S(2)}, u32[]{:S(2)}) %collective-permute-start.9) | collective-permute-done | bytes 524320 | tf_op jit(solution)/shard_map/ppermute | solution.py:384
  56.6 4.8 %collective-permute-done.11.refs_10_ = bf16[2,2,128,128]{3,2,1,0:T(8,128)(2,1)S(1)} collective-permute-done((bf16[2,2,128,128]{3,2,1,0:T(8,128)(2,1)S(1)}, bf16[2,2,128,128]{3,2,1,0:T(8,128)(2,1)S(1)}, u32[]{:S(2)}, u32[]{:S(2)}) %collective-permute-start.11) | collective-permute-done | bytes 131104 | tf_op jit(solution)/shard_map/ppermute | solution.py:384
  61.4 1.4 %collective-permute-done.12.refs_11_ = bf16[2,2,128,128]{3,2,1,0:T(8,128)(2,1)S(1)} collective-permute-done((bf16[2,2,128,128]{3,2,1,0:T(8,128)(2,1)S(1)}, bf16[2,2,128,128]{3,2,1,0:T(8,128)(2,1)S(1)}, u32[]{:S(2)}, u32[]{:S(2)}) %collective-permute-start.12) | collective-permute-done | bytes 131104 | tf_op jit(solution)/shard_map/ppermute | solution.py:384
  62.8 2.2 %spatial.3.refs_0_ = bf16[4,2,128,128]{3,2,1,0:T(8,128)(2,1)S(1)} custom-call(s32[8,4,8]{2,1,0:T(4,128)S(1)} %copy-done.2, bf16[8,4,8,128,128]{4,3,2,1,0:T(8,128)(2,1)S(1)} %bitcast.5, bf16[128,128]{1,0:T(8,128)(2,1)S(1)} %get-tuple-element.42.weight_ref, f32[8,128]{1,0:T(8,128)S(1)} %get-tuple-element.43.pos_ref, bf16[8,4,128,128]{3,2,1,0:T(8,128)(2,1)S(1)} %bitcast.9, ...), custom_call_target="tpu_custom_call" | custom-call | flops 2300000000 | bytes 1024 | tf_op jit(solution)/shard_map/spatial/pallas_call | solution.py:226
  70.3 1.5 %collective-permute-done.16.refs_11_ = bf16[3,2,128,128]{3,2,1,0:T(8,128)(2,1)S(1)} collective-permute-done((bf16[3,2,128,128]{3,2,1,0:T(8,128)(2,1)S(1)}, bf16[3,2,128,128]{3,2,1,0:T(8,128)(2,1)S(1)}, u32[]{:S(2)}, u32[]{:S(2)}) %collective-permute-start.16) | collective-permute-done | bytes 196640 | tf_op jit(solution)/shard_map/ppermute | solution.py:384
  71.8 3.0 %spatial.4.refs_4_ = bf16[4,3,128,128]{3,2,1,0:T(8,128)(2,1)S(1)} custom-call(s32[8,4,8]{2,1,0:T(4,128)S(1)} %copy-done.2, bf16[8,4,8,128,128]{4,3,2,1,0:T(8,128)(2,1)S(1)} %bitcast.5, bf16[128,128]{1,0:T(8,128)(2,1)S(1)} %get-tuple-element.42.weight_ref, f32[8,128]{1,0:T(8,128)S(1)} %get-tuple-element.43.pos_ref, bf16[8,4,128,128]{3,2,1,0:T(8,128)(2,1)S(1)} %bitcast.10, ...), custom_call_target="tpu_custom_call" | custom-call | flops 3449999872 | bytes 1024 | tf_op jit(solution)/shard_map/spatial/pallas_call | solution.py:226
  76.9 3.6 %collective-permute-done.21.refs_11_ = bf16[3,2,128,128]{3,2,1,0:T(8,128)(2,1)S(1)} collective-permute-done((bf16[3,2,128,128]{3,2,1,0:T(8,128)(2,1)S(1)}, bf16[3,2,128,128]{3,2,1,0:T(8,128)(2,1)S(1)}, u32[]{:S(2)}, u32[]{:S(2)}) %collective-permute-start.21) | collective-permute-done | bytes 196640 | tf_op jit(solution)/shard_map/ppermute | solution.py:384
  80.5 3.0 %spatial.5.refs_8_ = bf16[4,3,128,128]{3,2,1,0:T(8,128)(2,1)S(1)} custom-call(s32[8,4,8]{2,1,0:T(4,128)S(1)} %copy-done.2, bf16[8,4,8,128,128]{4,3,2,1,0:T(8,128)(2,1)S(1)} %bitcast.5, bf16[128,128]{1,0:T(8,128)(2,1)S(1)} %get-tuple-element.42.weight_ref, f32[8,128]{1,0:T(8,128)S(1)} %get-tuple-element.43.pos_ref, bf16[8,4,128,128]{3,2,1,0:T(8,128)(2,1)S(1)} %bitcast.11, ...), custom_call_target="tpu_custom_call" | custom-call | flops 3449999872 | bytes 1024 | tf_op jit(solution)/shard_map/spatial/pallas_call | solution.py:226
  87.4 6.3 %collective-permute-start.22 = (bf16[4,3,128,128]{3,2,1,0:T(8,128)(2,1)S(1)}, bf16[4,3,128,128]{3,2,1,0:T(8,128)(2,1)S(1)}, u32[]{:S(2)}, u32[]{:S(2)}) collective-permute-start(bf16[4,3,128,128]{3,2,1,0:T(8,128)(2,1)S(1)} %collective-permute-done.19.refs_6_), channel_id=1, source_target_pairs={{16,24},{24,16},{17,25},{25,17},{18,26},{26,18},{19,27},{27,19},{2... | collective-permute-start | bytes 1179656 | tf_op jit(solution)/shard_map/ppermute | solution.py:439
  93.7 5.7 %collective-permute-start.25 = (bf16[4,3,128,128]{3,2,1,0:T(8,128)(2,1)S(1)}, bf16[4,3,128,128]{3,2,1,0:T(8,128)(2,1)S(1)}, u32[]{:S(2)}, u32[]{:S(2)}) collective-permute-start(bf16[4,3,128,128]{3,2,1,0:T(8,128)(2,1)S(1)} %collective-permute-done.24.refs_10_), channel_id=1, source_target_pairs={{16,24},{24,16},{17,25},{25,17},{18,26},{26,18},{19,27},{27,19},{2... | collective-permute-start | bytes 1179656 | tf_op jit(solution)/shard_map/ppermute | solution.py:439
  99.4 1.9 %collective-permute-start.17 = (bf16[4,2,128,128]{3,2,1,0:T(8,128)(2,1)S(1)}, bf16[4,2,128,128]{3,2,1,0:T(8,128)(2,1)S(1)}, u32[]{:S(2)}, u32[]{:S(2)}) collective-permute-start(bf16[4,2,128,128]{3,2,1,0:T(8,128)(2,1)S(1)} %collective-permute-done.14.refs_2_), channel_id=1, source_target_pairs={{16,24},{24,16},{17,25},{25,17},{18,26},{26,18},{19,27},{27,19},{2... | collective-permute-start | bytes 786440 | tf_op jit(solution)/shard_map/ppermute | solution.py:439
  101.4 1.5 %collective-permute-done.17.refs_3_ = bf16[4,2,128,128]{3,2,1,0:T(8,128)(2,1)S(1)} collective-permute-done((bf16[4,2,128,128]{3,2,1,0:T(8,128)(2,1)S(1)}, bf16[4,2,128,128]{3,2,1,0:T(8,128)(2,1)S(1)}, u32[]{:S(2)}, u32[]{:S(2)}) %collective-permute-start.17) | collective-permute-done | bytes 262176 | tf_op jit(solution)/shard_map/ppermute | solution.py:439
  102.9 19.6 %temporal.1 = bf16[8,512,128]{2,1,0:T(8,128)(2,1)} custom-call(s32[1]{0:T(128)} %bitcast.me_ref, bf16[384,128]{1,0:T(8,128)(2,1)S(1)} %get-tuple-element.36.qkv_ref, bf16[128,128]{1,0:T(8,128)(2,1)S(1)} %get-tuple-element.37.proj_ref, f32[128,128]{1,0:T(8,128)S(1)} %get-tuple-element.38.gain_ref, bf16[512,128]{1,0:T(8,128)(2,1)S(1)} %get-tuple-element.39.up_ref, ...), custom_call_target="tpu_custom_call" | custom-call | flops 11500000256 | bytes 1024 | tf_op jit(solution)/shard_map/temporal/pallas_call | solution.py:339
  (67 shorter events, 26.7 us)
Async XLA Ops:
  0.0 24.2 %collective-permute-start = (bf16[8,4,128,128]{3,2,1,0:T(8,128)(2,1)}, bf16[8,4,128,128]{3,2,1,0:T(8,128)(2,1)S(1)}, u32[]{:S(2)}, u32[]{:S(2)}) collective-permute-start(bf16[8,4,128,128]{3,2,1,0:T(8,128)(2,1)} %bitcast.6), channel_id=1, source_target_pairs={{0,2},{1,3},{2,0},{3,1},{4,6},{5,7},{6,4},{7,5},{8,10},{9,11},{10,... | collective-permute-start | bytes 3145736 | tf_op jit(solution)/shard_map/ppermute | solution.py:364
  1.3 22.9 %collective-permute-start.4 = (bf16[8,4,128,128]{3,2,1,0:T(8,128)(2,1)}, bf16[8,4,128,128]{3,2,1,0:T(8,128)(2,1)S(1)}, u32[]{:S(2)}, u32[]{:S(2)}) collective-permute-start(bf16[8,4,128,128]{3,2,1,0:T(8,128)(2,1)} %bitcast.7), channel_id=1, source_target_pairs={{2,4},{3,5},{4,2},{5,3},{10,12},{11,13},{12,10},{13,11},{18,20},{1... | collective-permute-start | bytes 3145736 | tf_op jit(solution)/shard_map/ppermute | solution.py:384
  10.2 13.3 %collective-permute-start.3 = (bf16[8,2,128,128]{3,2,1,0:T(8,128)(2,1)S(1)}, bf16[8,2,128,128]{3,2,1,0:T(8,128)(2,1)S(1)}, u32[]{:S(2)}, u32[]{:S(2)}) collective-permute-start(bf16[8,2,128,128]{3,2,1,0:T(8,128)(2,1)S(1)} %pick_blocks.3), channel_id=1, source_target_pairs={{0,1},{1,0},{2,3},{3,2},{4,5},{5,4},{6,7},{7,6},{8,9},{9,8},{10,11... | collective-permute-start | bytes 1572872 | tf_op jit(solution)/shard_map/ppermute | solution.py:364
  12.2 11.3 %collective-permute-start.2 = (s32[8,2,16]{2,1,0:T(2,128)S(1)}, s32[8,2,16]{2,1,0:T(2,128)S(1)}, u32[]{:S(2)}, u32[]{:S(2)}) collective-permute-start(s32[8,2,16]{2,1,0:T(2,128)S(1)} %pad_add_fusion), channel_id=1, source_target_pairs={{6,4},{7,5},{0,2},{1,3},{14,12},{15,13},{8,10},{9,11},{22,20},{23,... | collective-permute-start | bytes 3080 | tf_op jit(solution)/shard_map/ppermute | solution.py:384
  24.2 6.4 %collective-permute-start.5 = (bf16[8,4,128,128]{3,2,1,0:T(8,128)(2,1)S(1)}, bf16[8,4,128,128]{3,2,1,0:T(8,128)(2,1)S(1)}, u32[]{:S(2)}, u32[]{:S(2)}) collective-permute-start(bf16[8,4,128,128]{3,2,1,0:T(8,128)(2,1)S(1)} %collective-permute-done.refs_4_.refs_1_), channel_id=1, source_target_pairs={{2,4},{3,5},{4,2},{5,3},{10,12},{11,13},{12,10},{13,11},{18,20},{1... | collective-permute-start | bytes 3145736 | tf_op jit(solution)/shard_map/ppermute | solution.py:384
  25.9 19.1 %collective-permute-start.10 = (bf16[8,2,128,128]{3,2,1,0:T(8,128)(2,1)S(1)}, bf16[8,2,128,128]{3,2,1,0:T(8,128)(2,1)S(1)}, u32[]{:S(2)}, u32[]{:S(2)}) collective-permute-start(bf16[8,2,128,128]{3,2,1,0:T(8,128)(2,1)S(1)} %get-tuple-element.53), channel_id=1, source_target_pairs={{4,7},{5,6},{2,1},{3,0},{12,15},{13,14},{10,9},{11,8},{20,23},{21,... | collective-permute-start | bytes 1572872 | tf_op jit(solution)/shard_map/ppermute | solution.py:384
  27.3 23.2 %collective-permute-start.6 = (bf16[8,2,128,128]{3,2,1,0:T(8,128)(2,1)S(1)}, bf16[8,2,128,128]{3,2,1,0:T(8,128)(2,1)S(1)}, u32[]{:S(2)}, u32[]{:S(2)}) collective-permute-start(bf16[8,2,128,128]{3,2,1,0:T(8,128)(2,1)S(1)} %get-tuple-element.49), channel_id=1, source_target_pairs={{0,1},{1,0},{2,3},{3,2},{4,5},{5,4},{6,7},{7,6},{8,9},{9,8},{10,11... | collective-permute-start | bytes 1572872 | tf_op jit(solution)/shard_map/ppermute | solution.py:364
  28.6 24.0 %collective-permute-start.7 = (bf16[8,2,128,128]{3,2,1,0:T(8,128)(2,1)S(1)}, bf16[8,2,128,128]{3,2,1,0:T(8,128)(2,1)S(1)}, u32[]{:S(2)}, u32[]{:S(2)}) collective-permute-start(bf16[8,2,128,128]{3,2,1,0:T(8,128)(2,1)S(1)} %get-tuple-element.50), channel_id=1, source_target_pairs={{2,3},{3,2},{4,5},{5,4},{10,11},{11,10},{12,13},{13,12},{18,19},{1... | collective-permute-start | bytes 1572872 | tf_op jit(solution)/shard_map/ppermute | solution.py:384
  29.3 26.1 %collective-permute-start.9 = (bf16[8,2,128,128]{3,2,1,0:T(8,128)(2,1)S(1)}, bf16[8,2,128,128]{3,2,1,0:T(8,128)(2,1)S(1)}, u32[]{:S(2)}, u32[]{:S(2)}) collective-permute-start(bf16[8,2,128,128]{3,2,1,0:T(8,128)(2,1)S(1)} %get-tuple-element.52), channel_id=1, source_target_pairs={{4,6},{5,7},{2,0},{3,1},{12,14},{13,15},{10,8},{11,9},{20,22},{21,... | collective-permute-start | bytes 1572872 | tf_op jit(solution)/shard_map/ppermute | solution.py:384
  31.4 31.4 %collective-permute-start.8 = (bf16[8,2,128,128]{3,2,1,0:T(8,128)(2,1)S(1)}, bf16[8,2,128,128]{3,2,1,0:T(8,128)(2,1)S(1)}, u32[]{:S(2)}, u32[]{:S(2)}) collective-permute-start(bf16[8,2,128,128]{3,2,1,0:T(8,128)(2,1)S(1)} %get-tuple-element.51), channel_id=1, source_target_pairs={{2,3},{3,2},{4,5},{5,4},{10,11},{11,10},{12,13},{13,12},{18,19},{1... | collective-permute-start | bytes 1572872 | tf_op jit(solution)/shard_map/ppermute | solution.py:384
  45.0 16.4 %collective-permute-start.11 = (bf16[2,2,128,128]{3,2,1,0:T(8,128)(2,1)S(1)}, bf16[2,2,128,128]{3,2,1,0:T(8,128)(2,1)S(1)}, u32[]{:S(2)}, u32[]{:S(2)}) collective-permute-start(bf16[2,2,128,128]{3,2,1,0:T(8,128)(2,1)S(1)} %get-tuple-element.54), channel_id=1, source_target_pairs={{4,6},{5,7},{2,0},{3,1},{12,14},{13,15},{10,8},{11,9},{20,22},{21,... | collective-permute-start | bytes 393224 | tf_op jit(solution)/shard_map/ppermute | solution.py:384
  50.5 12.3 %collective-permute-start.12 = (bf16[2,2,128,128]{3,2,1,0:T(8,128)(2,1)S(1)}, bf16[2,2,128,128]{3,2,1,0:T(8,128)(2,1)S(1)}, u32[]{:S(2)}, u32[]{:S(2)}) collective-permute-start(bf16[2,2,128,128]{3,2,1,0:T(8,128)(2,1)S(1)} %get-tuple-element.55), channel_id=1, source_target_pairs={{4,7},{5,6},{2,1},{3,0},{12,15},{13,14},{10,9},{11,8},{20,23},{21,... | collective-permute-start | bytes 393224 | tf_op jit(solution)/shard_map/ppermute | solution.py:384
  52.7 16.3 %collective-permute-start.15 = (bf16[3,2,128,128]{3,2,1,0:T(8,128)(2,1)S(1)}, bf16[3,2,128,128]{3,2,1,0:T(8,128)(2,1)S(1)}, u32[]{:S(2)}, u32[]{:S(2)}) collective-permute-start(bf16[3,2,128,128]{3,2,1,0:T(8,128)(2,1)S(1)} %get-tuple-element.57), channel_id=1, source_target_pairs={{4,6},{5,7},{2,0},{3,1},{12,14},{13,15},{10,8},{11,9},{20,22},{21,... | collective-permute-start | bytes 589832 | tf_op jit(solution)/shard_map/ppermute | solution.py:384
  55.4 16.5 %collective-permute-start.16 = (bf16[3,2,128,128]{3,2,1,0:T(8,128)(2,1)S(1)}, bf16[3,2,128,128]{3,2,1,0:T(8,128)(2,1)S(1)}, u32[]{:S(2)}, u32[]{:S(2)}) collective-permute-start(bf16[3,2,128,128]{3,2,1,0:T(8,128)(2,1)S(1)} %get-tuple-element.58), channel_id=1, source_target_pairs={{4,7},{5,6},{2,1},{3,0},{12,15},{13,14},{10,9},{11,8},{20,23},{21,... | collective-permute-start | bytes 589832 | tf_op jit(solution)/shard_map/ppermute | solution.py:384
  65.1 11.0 %collective-permute-start.13 = (bf16[4,2,128,128]{3,2,1,0:T(8,128)(2,1)S(1)}, bf16[4,2,128,128]{3,2,1,0:T(8,128)(2,1)S(1)}, u32[]{:S(2)}, u32[]{:S(2)}) collective-permute-start(bf16[4,2,128,128]{3,2,1,0:T(8,128)(2,1)S(1)} %spatial.3.refs_0_), channel_id=1, source_target_pairs={{0,8},{16,24},{1,9},{17,25},{2,10},{18,26},{3,11},{19,27},{4,12},{... | collective-permute-start | bytes 786440 | tf_op jit(solution)/shard_map/ppermute | solution.py:429
  66.4 9.7 %collective-permute-start.14 = (bf16[4,2,128,128]{3,2,1,0:T(8,128)(2,1)S(1)}, bf16[4,2,128,128]{3,2,1,0:T(8,128)(2,1)S(1)}, u32[]{:S(2)}, u32[]{:S(2)}) collective-permute-start(bf16[4,2,128,128]{3,2,1,0:T(8,128)(2,1)S(1)} %spatial.3.refs_0_), channel_id=1, source_target_pairs={{0,16},{8,24},{1,17},{9,25},{2,18},{10,26},{3,19},{11,27},{4,20},{... | collective-permute-start | bytes 786440 | tf_op jit(solution)/shard_map/ppermute | solution.py:429
  67.7 9.2 %collective-permute-start.20 = (bf16[3,2,128,128]{3,2,1,0:T(8,128)(2,1)S(1)}, bf16[3,2,128,128]{3,2,1,0:T(8,128)(2,1)S(1)}, u32[]{:S(2)}, u32[]{:S(2)}) collective-permute-start(bf16[3,2,128,128]{3,2,1,0:T(8,128)(2,1)S(1)} %get-tuple-element.63), channel_id=1, source_target_pairs={{4,6},{5,7},{2,0},{3,1},{12,14},{13,15},{10,8},{11,9},{20,22},{21,... | collective-permute-start | bytes 589832 | tf_op jit(solution)/shard_map/ppermute | solution.py:384
  69.0 11.5 %collective-permute-start.21 = (bf16[3,2,128,128]{3,2,1,0:T(8,128)(2,1)S(1)}, bf16[3,2,128,128]{3,2,1,0:T(8,128)(2,1)S(1)}, u32[]{:S(2)}, u32[]{:S(2)}) collective-permute-start(bf16[3,2,128,128]{3,2,1,0:T(8,128)(2,1)S(1)} %get-tuple-element.64), channel_id=1, source_target_pairs={{4,7},{5,6},{2,1},{3,0},{12,15},{13,14},{10,9},{11,8},{20,23},{21,... | collective-permute-start | bytes 589832 | tf_op jit(solution)/shard_map/ppermute | solution.py:384
  74.8 12.6 %collective-permute-start.19 = (bf16[4,3,128,128]{3,2,1,0:T(8,128)(2,1)S(1)}, bf16[4,3,128,128]{3,2,1,0:T(8,128)(2,1)S(1)}, u32[]{:S(2)}, u32[]{:S(2)}) collective-permute-start(bf16[4,3,128,128]{3,2,1,0:T(8,128)(2,1)S(1)} %spatial.4.refs_4_), channel_id=1, source_target_pairs={{0,16},{8,24},{1,17},{9,25},{2,18},{10,26},{3,19},{11,27},{4,20},{... | collective-permute-start | bytes 1179656 | tf_op jit(solution)/shard_map/ppermute | solution.py:429
  83.5 10.2 %collective-permute-start.24 = (bf16[4,3,128,128]{3,2,1,0:T(8,128)(2,1)S(1)}, bf16[4,3,128,128]{3,2,1,0:T(8,128)(2,1)S(1)}, u32[]{:S(2)}, u32[]{:S(2)}) collective-permute-start(bf16[4,3,128,128]{3,2,1,0:T(8,128)(2,1)S(1)} %spatial.5.refs_8_), channel_id=1, source_target_pairs={{0,16},{8,24},{1,17},{9,25},{2,18},{10,26},{3,19},{11,27},{4,20},{... | collective-permute-start | bytes 1179656 | tf_op jit(solution)/shard_map/ppermute | solution.py:429
  84.8 16.5 %collective-permute-start.18 = (bf16[4,3,128,128]{3,2,1,0:T(8,128)(2,1)S(1)}, bf16[4,3,128,128]{3,2,1,0:T(8,128)(2,1)S(1)}, u32[]{:S(2)}, u32[]{:S(2)}) collective-permute-start(bf16[4,3,128,128]{3,2,1,0:T(8,128)(2,1)S(1)} %spatial.4.refs_4_), channel_id=1, source_target_pairs={{0,8},{16,24},{1,9},{17,25},{2,10},{18,26},{3,11},{19,27},{4,12},{... | collective-permute-start | bytes 1179656 | tf_op jit(solution)/shard_map/ppermute | solution.py:429
  86.1 16.7 %collective-permute-start.23 = (bf16[4,3,128,128]{3,2,1,0:T(8,128)(2,1)S(1)}, bf16[4,3,128,128]{3,2,1,0:T(8,128)(2,1)S(1)}, u32[]{:S(2)}, u32[]{:S(2)}) collective-permute-start(bf16[4,3,128,128]{3,2,1,0:T(8,128)(2,1)S(1)} %spatial.5.refs_8_), channel_id=1, source_target_pairs={{0,8},{16,24},{1,9},{17,25},{2,10},{18,26},{3,11},{19,27},{4,12},{... | collective-permute-start | bytes 1179656 | tf_op jit(solution)/shard_map/ppermute | solution.py:429
  87.4 15.4 %collective-permute-start.22 = (bf16[4,3,128,128]{3,2,1,0:T(8,128)(2,1)S(1)}, bf16[4,3,128,128]{3,2,1,0:T(8,128)(2,1)S(1)}, u32[]{:S(2)}, u32[]{:S(2)}) collective-permute-start(bf16[4,3,128,128]{3,2,1,0:T(8,128)(2,1)S(1)} %collective-permute-done.19.refs_6_), channel_id=1, source_target_pairs={{16,24},{24,16},{17,25},{25,17},{18,26},{26,18},{19,27},{27,19},{2... | collective-permute-start | bytes 1179656 | tf_op jit(solution)/shard_map/ppermute | solution.py:439
  93.7 9.1 %collective-permute-start.25 = (bf16[4,3,128,128]{3,2,1,0:T(8,128)(2,1)S(1)}, bf16[4,3,128,128]{3,2,1,0:T(8,128)(2,1)S(1)}, u32[]{:S(2)}, u32[]{:S(2)}) collective-permute-start(bf16[4,3,128,128]{3,2,1,0:T(8,128)(2,1)S(1)} %collective-permute-done.24.refs_10_), channel_id=1, source_target_pairs={{16,24},{24,16},{17,25},{25,17},{18,26},{26,18},{19,27},{27,19},{2... | collective-permute-start | bytes 1179656 | tf_op jit(solution)/shard_map/ppermute | solution.py:439
  (15 other events, 531.9 us)

commit v5 on v4

--- a/solution.py
+++ b/solution.py
@@ -246,63 +246,112 @@
     )(slots, vals, weight_t, pos, srcs[0][0], *[near(a) for a, _ in srcs[1:]])
 
 
+def scales(width):
+    return 1.0 / (CAP * math.sqrt(width // HEADS)), CAP * math.log2(math.e)
+
+
+def attend(q_ref, k_ref, v_ref, at, keys, sums):
+    width = q_ref.shape[1]
+    spans = [slice(d, d + HEADS) for d in range(0, width, HEADS)]
+    steep = scales(width)[1]
+    q = [q_ref[at, span] for span in spans]
+    total, acc = sums if sums else (None, None)
+    for u in keys:
+        raw = q[0] * k_ref[u, spans[0]]
+        for d in range(1, len(spans)):
+            raw = raw + q[d] * k_ref[u, spans[d]]
+        e = jnp.exp2(steep * jnp.tanh(raw))
+        values = [e * v_ref[u, span] for span in spans]
+        total = e if total is None else total + e
+        acc = values if acc is None else [one + more for one, more in zip(acc, values)]
+    return total, acc
+
+
+def own_kernel(sizes, qkv_ref, *refs):
+    arrays = refs[: len(sizes)]
+    q_out, acc_out, total_out, q_s, k_s, v_s = refs[len(sizes) :]
+    snaps = sum(sizes)
+    g = pl.program_id(0)
+    width, lanes = arrays[0].shape[2:]
+    scale = scales(width)[0]
+    found = [a[g, s] for a, n in zip(arrays, sizes) for s in range(n)]
+    for first in range(0, snaps, 4):
+        some = found[first : first + 4]
+        got = dot(qkv_ref[...], jnp.concatenate(some, axis=1)).astype(BF16)
+        for j in range(len(some)):
+            part = got[:, j * lanes : (j + 1) * lanes]
+            q_out[0, first + j] = part[:width]
+            q_s[first + j] = part[:width].astype(F32) * scale
+            k_s[first + j] = part[width : 2 * width].astype(F32)
+            v_s[first + j] = part[2 * width :].astype(F32)
+    for s in range(snaps):
+        total, acc = attend(q_s, k_s, v_s, s, range(s + 1), None)
+        total_out[0, s] = total
+        for d, one in enumerate(acc):
+            acc_out[0, s, d * HEADS : (d + 1) * HEADS] = one
+
+
+def own_part(qkv_t, arrays):
+    groups, _, width, lanes = arrays[0].shape
+    sizes = [a.shape[1] for a in arrays]
+    snaps = sum(sizes)
+    shape = jax.ShapeDtypeStruct
+    outs = [
+        shape((groups, snaps, width, lanes), BF16),
+        shape((groups, snaps, width, lanes), F32),
+        shape((groups, snaps, HEADS, lanes), F32),
+    ]
+    return pl.pallas_call(
+        functools.partial(own_kernel, sizes),
+        grid=(groups,),
+        in_specs=[whole(qkv_t)] + [pl.BlockSpec(memory_space=pltpu.VMEM)] * len(arrays),
+        out_specs=[pl.BlockSpec((1,) + a.shape[1:], lambda g: (g, 0, 0, 0)) for a in outs],
+        scratch_shapes=[pltpu.VMEM((snaps, width, lanes), F32)] * 3,
+        out_shape=outs,
+        compiler_params=pltpu.CompilerParams(vmem_limit_bytes=VMEM),
+        cost_estimate=cost(6),
+        name="temporal_own",
+    )(qkv_t, *[near(a) for a in arrays])
+
+
 def temporal_kernel(sizes, others, me_ref, qkv_ref, proj_ref, gain_ref, up_ref, down_ref, *refs):
     count = 1 + others
     arrays = refs[: count * len(sizes)]
-    out_ref, k_s, v_s, q_s, acc_s, total_s, att_s = refs[-7:]
+    q_ref, acc_ref, total_ref, out_ref, k_s, v_s, q_s, acc_s, total_s, att_s = refs[-10:]
     snaps = sum(sizes)
     width, lanes = arrays[0].shape[2:]
-    head_dim = width // HEADS
     me, g = me_ref[0], pl.program_id(0)
-    scale = 1.0 / (CAP * math.sqrt(head_dim))
-    steep = CAP * math.log2(math.e)
+    scale = scales(width)[0]
+    spans = [slice(d, d + HEADS) for d in range(0, width, HEADS)]
 
     def held(i):
         return [arrays[c * count + i][g, s] for c, n in enumerate(sizes) for s in range(n)]
 
     def project(i):
-        skip = 0 if i == 0 else width
         base = (me ^ i) * snaps
         found = held(i)
         for first in range(0, snaps, 4):
             some = found[first : first + 4]
-            got = dot(qkv_ref[skip:, :], jnp.concatenate(some, axis=1)).astype(BF16).astype(F32)
+            got = dot(qkv_ref[width:, :], jnp.concatenate(some, axis=1)).astype(BF16).astype(F32)
             for j in range(len(some)):
                 part = got[:, j * lanes : (j + 1) * lanes]
-                if i == 0:
-                    q_s[first + j] = part[:width] * scale
-                k_s[base + first + j] = part[width - skip : 2 * width - skip]
-                v_s[base + first + j] = part[2 * width - skip :]
-
-    project(0)
+                k_s[base + first + j] = part[:width]
+                v_s[base + first + j] = part[width:]
+
     for i in range(1, count):
         pl.when((me ^ i) < me)(functools.partial(project, i))
-
-    def attend(at, keys, fresh=False):
-        q = [q_s[at, d * HEADS : (d + 1) * HEADS] for d in range(head_dim)]
-        total, acc = None, None
-        for u in keys:
-            row = lambda ref, d: ref[u, d * HEADS : (d + 1) * HEADS]
-            raw = q[0] * row(k_s, 0)
-            for d in range(1, head_dim):
-                raw = raw + q[d] * row(k_s, d)
-            e = jnp.exp2(steep * jnp.tanh(raw))
-            if total is None:
-                total, acc = e, [e * row(v_s, d) for d in range(head_dim)]
-            else:
-                total = total + e
-                acc = [acc[d] + e * row(v_s, d) for d in range(head_dim)]
-        for d in range(head_dim):
-            span = slice(d * HEADS, (d + 1) * HEADS)
-            acc_s[at, span] = acc[d] if fresh else acc_s[at, span] + acc[d]
-        total_s[at] = total if fresh else total_s[at] + total
-
-    for s in range(snaps):
-        attend(s, [me * snaps + j for j in range(s + 1)], fresh=True)
+    for at in range(snaps):
+        q_s[at] = q_ref[g, at].astype(F32) * scale
+        acc_s[at] = acc_ref[g, at]
+        total_s[at] = total_ref[g, at]
 
     def earlier(m, none):
+        keys = [m * snaps + j for j in range(snaps)]
         for at in range(snaps):
-            attend(at, [m * snaps + j for j in range(snaps)])
+            sums = total_s[at], [acc_s[at, span] for span in spans]
+            total_s[at], acc = attend(q_s, k_s, v_s, at, keys, sums)
+            for span, one in zip(spans, acc):
+                acc_s[at, span] = one
         return none
 
     lax.fori_loop(0, me, earlier, 0)
@@ -310,8 +359,7 @@
     mine = held(0)
     for at in range(snaps):
         inv = 1.0 / total_s[at]
-        for d in range(head_dim):
-            span = slice(d * HEADS, (d + 1) * HEADS)
+        for span in spans:
             att_s[span, at * lanes : (at + 1) * lanes] = (acc_s[at, span] * inv).astype(BF16)
     half = snaps // 2
     for h in range(2):
@@ -329,13 +377,12 @@
             out_ref[h * half + i] = out[:, i * lanes : (i + 1) * lanes].T.astype(BF16)
 
 
-def temporal(me, weights, chunks):
+def temporal(me, weights, chunks, own):
     groups, _, width, lanes = chunks[0][0].shape
     count = len(chunks[0])
     sizes = [chunk[0].shape[1] for chunk in chunks]
     snaps = sum(sizes)
-
-    parts = [a for chunk in chunks for a in chunk]
+    parts = [a for chunk in chunks for a in chunk] + list(own)
     return pl.pallas_call(
         functools.partial(temporal_kernel, sizes, count - 1),
         grid_spec=pltpu.PrefetchScalarGridSpec(
@@ -479,7 +526,7 @@
         owns.append(spatial(slots, tile_vals, start, stop, space_t, pos, srcs, 1)[0])
         started.append(gather_times(owns[-1]))
     chunks = [pass_on(got, own) for got, own in zip(started, owns[1:] + owns[-1:])]
-    return temporal(me, weights, chunks)
+    return temporal(me, weights, chunks, own_part(weights[0], owns))
 
 
 def solution(mesh):

time: 125 us -> 120 us (0.960); the launches traced: 122 us -> 120 us
  waiting for transfers between devices: 39.9 us -> 38.3 us
    ppermute x13, starting transfers between devices: 19.2 us -> 15.3 us  [exchange_forward(): go = lambda a, pairs, x=0: lax.ppermute(a, 'vert', layers(pairs, x))]
    ppermute x4, starting transfers between devices: 5.06 us -> 7.6 us  [send(): lax.ppermute(a, 'vert', [(v, v ^ k) for v in range(lax.axis_size('vert'))])]
    pallas_call x0 -> x1, Pallas kernels: none -> 2.42 us  [own_part(): pl.pallas_call(functools.partial(own_kernel, sizes), grid=(groups,), in_s...]
    pallas_call x1, Pallas kernels: 19.6 us -> 17.1 us  [temporal(): pl.pallas_call(functools.partial(temporal_kernel, sizes, count - 1), grid...]
    ppermute x13, waiting for transfers between devices: 32 us -> 29.9 us  [exchange_forward(): go = lambda a, pairs, x=0: lax.ppermute(a, 'vert', layers(pairs, x))]
    ppermute x4, waiting for transfers between devices: 6.38 us -> 8.45 us  [send(): lax.ppermute(a, 'vert', [(v, v ^ k) for v in range(lax.axis_size('vert'))])]
    ppermute x3, waiting for transfers between devices: 1.5 us -> 0.01 us  [pass_on(): got[k] = lax.ppermute(got[k - 1], 'tm', pairs)]
  transfers between devices with their start and end apart: 26 -> 26, of which waited for: 12 -> 10; matrix products, arithmetic and copies ran while one was open for 1% -> 1% of each run, Pallas kernels for 11% -> 14%
where the time goes in v5:
time: 120 us
  starting transfers between devices  44.7 us (37%)
  waiting for transfers between devices  38.3 us (32%)
  Pallas kernels  33.5 us (28%)
  local copies, waits for them, and re-layouts  1.29 us (1%)
  other arithmetic  1.24 us (1%)
    ppermute x13, waiting for transfers between devices, exchange_forward(): go = lambda a, pairs, x=0: lax.ppermute(a, 'vert', layers(pairs, x))  29.9 us
    pallas_call x1, Pallas kernels, temporal(): pl.pallas_call(functools.partial(temporal_kernel, sizes, count - 1), grid...  17.1 us
    ppermute x13, starting transfers between devices, exchange_forward(): go = lambda a, pairs, x=0: lax.ppermute(a, 'vert', layers(pairs, x))  15.3 us
    ppermute x3, starting transfers between devices, pass_on(): got[k] = lax.ppermute(got[k - 1], 'tm', pairs)  14 us
    ppermute x4, waiting for transfers between devices, send(): lax.ppermute(a, 'vert', [(v, v ^ k) for v in range(lax.axis_size('vert'))])  8.45 us
    pallas_call x3, Pallas kernels, spatial(): pl.pallas_call(functools.partial(spatial_kernel, start, [first for _, fir...  8.21 us
    ppermute x6, starting transfers between devices, gather_times(): got[k] = lax.ppermute(own, 'tm', pairs)  7.75 us
    ppermute x4, starting transfers between devices, send(): lax.ppermute(a, 'vert', [(v, v ^ k) for v in range(lax.axis_size('vert'))])  7.6 us
  transfers between devices with their start and end apart: 26, of which 10 were waited for; matrix products, arithmetic and copies ran while one was open for 1% of the time, Pallas kernels for 14%

profile of v5, /device:TPU:5, one launch (start us, length us, event | category | flops | bytes accessed | tf_op | source)
XLA Modules:
  0.0 119.6 jit_solution(16055105032488993852)
XLA Ops:
  0.7 3.8 %collective-permute-start = (bf16[8,4,128,128]{3,2,1,0:T(8,128)(2,1)}, bf16[8,4,128,128]{3,2,1,0:T(8,128)(2,1)S(1)}, u32[]{:S(2)}, u32[]{:S(2)}) collective-permute-start(bf16[8,4,128,128]{3,2,1,0:T(8,128)(2,1)} %bitcast.7), channel_id=1, source_target_pairs={{0,2},{1,3},{2,0},{3,1},{4,6},{5,7},{6,4},{7,5},{8,10},{9,11},{10,... | collective-permute-start | bytes 3145736 | tf_op jit(solution)/shard_map/ppermute | solution.py:411
  5.2 2.7 %lists.1 = (s32[8,1,16]{2,1,0:T(1,128)}, s32[8,4,8]{2,1,0:T(4,128)}) custom-call(s32[2]{0:T(128)} %pad_add_fusion.1.at_ref, s32[8,4,8]{2,1,0:T(4,128)} %cols_ref.1), custom_call_target="tpu_custom_call" | custom-call | flops 1150000000 | bytes 1024 | tf_op jit(solution)/shard_map/lists/pallas_call | solution.py:82
  9.0 1.8 %collective-permute-done.1.refs_0_ = s32[8,1,16]{2,1,0:T(1,128)S(1)} collective-permute-done((s32[8,1,16]{2,1,0:T(1,128)}, s32[8,1,16]{2,1,0:T(1,128)S(1)}, u32[]{:S(2)}, u32[]{:S(2)}) %collective-permute-start.1) | collective-permute-done | bytes 544 | tf_op jit(solution)/shard_map/ppermute | solution.py:411
  14.6 1.9 %collective-permute-start.2 = (s32[8,2,16]{2,1,0:T(2,128)S(1)}, s32[8,2,16]{2,1,0:T(2,128)S(1)}, u32[]{:S(2)}, u32[]{:S(2)}) collective-permute-start(s32[8,2,16]{2,1,0:T(2,128)S(1)} %pad_add_fusion), channel_id=1, source_target_pairs={{6,4},{7,5},{0,2},{1,3},{14,12},{15,13},{8,10},{9,11},{22,20},{23,... | collective-permute-start | bytes 3080 | tf_op jit(solution)/shard_map/ppermute | solution.py:431
  16.6 9.9 %collective-permute-done.2 = s32[8,2,16]{2,1,0:T(2,128)S(1)} collective-permute-done((s32[8,2,16]{2,1,0:T(2,128)S(1)}, s32[8,2,16]{2,1,0:T(2,128)S(1)}, u32[]{:S(2)}, u32[]{:S(2)}) %collective-permute-start.2) | collective-permute-done | bytes 1056 | tf_op jit(solution)/shard_map/ppermute | solution.py:431
  31.0 1.3 %collective-permute-start.9 = (bf16[8,2,128,128]{3,2,1,0:T(8,128)(2,1)S(1)}, bf16[8,2,128,128]{3,2,1,0:T(8,128)(2,1)S(1)}, u32[]{:S(2)}, u32[]{:S(2)}) collective-permute-start(bf16[8,2,128,128]{3,2,1,0:T(8,128)(2,1)S(1)} %get-tuple-element.55), channel_id=1, source_target_pairs={{4,6},{5,7},{2,0},{3,1},{12,14},{13,15},{10,8},{11,9},{20,22},{21,... | collective-permute-start | bytes 1572872 | tf_op jit(solution)/shard_map/ppermute | solution.py:431
  32.3 1.3 %collective-permute-start.10 = (bf16[8,2,128,128]{3,2,1,0:T(8,128)(2,1)S(1)}, bf16[8,2,128,128]{3,2,1,0:T(8,128)(2,1)S(1)}, u32[]{:S(2)}, u32[]{:S(2)}) collective-permute-start(bf16[8,2,128,128]{3,2,1,0:T(8,128)(2,1)S(1)} %get-tuple-element.56), channel_id=1, source_target_pairs={{4,7},{5,6},{2,1},{3,0},{12,15},{13,14},{10,9},{11,8},{20,23},{21,... | collective-permute-start | bytes 1572872 | tf_op jit(solution)/shard_map/ppermute | solution.py:431
  35.1 5.8 %collective-permute-done.6.refs_5_ = bf16[8,2,128,128]{3,2,1,0:T(8,128)(2,1)S(1)} collective-permute-done((bf16[8,2,128,128]{3,2,1,0:T(8,128)(2,1)S(1)}, bf16[8,2,128,128]{3,2,1,0:T(8,128)(2,1)S(1)}, u32[]{:S(2)}, u32[]{:S(2)}) %collective-permute-start.6) | collective-permute-done | bytes 524320 | tf_op jit(solution)/shard_map/ppermute | solution.py:411
  40.9 1.5 %collective-permute-start.11 = (bf16[2,2,128,128]{3,2,1,0:T(8,128)(2,1)S(1)}, bf16[2,2,128,128]{3,2,1,0:T(8,128)(2,1)S(1)}, u32[]{:S(2)}, u32[]{:S(2)}) collective-permute-start(bf16[2,2,128,128]{3,2,1,0:T(8,128)(2,1)S(1)} %get-tuple-element.57), channel_id=1, source_target_pairs={{4,6},{5,7},{2,0},{3,1},{12,14},{13,15},{10,8},{11,9},{20,22},{21,... | collective-permute-start | bytes 393224 | tf_op jit(solution)/shard_map/ppermute | solution.py:431
  44.7 1.4 %collective-permute-done.9.refs_8_ = bf16[8,2,128,128]{3,2,1,0:T(8,128)(2,1)S(1)} collective-permute-done((bf16[8,2,128,128]{3,2,1,0:T(8,128)(2,1)S(1)}, bf16[8,2,128,128]{3,2,1,0:T(8,128)(2,1)S(1)}, u32[]{:S(2)}, u32[]{:S(2)}) %collective-permute-start.9) | collective-permute-done | bytes 524320 | tf_op jit(solution)/shard_map/ppermute | solution.py:431
  47.4 10.7 %collective-permute-done.10.refs_9_ = bf16[8,2,128,128]{3,2,1,0:T(8,128)(2,1)S(1)} collective-permute-done((bf16[8,2,128,128]{3,2,1,0:T(8,128)(2,1)S(1)}, bf16[8,2,128,128]{3,2,1,0:T(8,128)(2,1)S(1)}, u32[]{:S(2)}, u32[]{:S(2)}) %collective-permute-start.10) | collective-permute-done | bytes 524320 | tf_op jit(solution)/shard_map/ppermute | solution.py:431
  59.4 2.3 %collective-permute-done.11.refs_10_ = bf16[2,2,128,128]{3,2,1,0:T(8,128)(2,1)S(1)} collective-permute-done((bf16[2,2,128,128]{3,2,1,0:T(8,128)(2,1)S(1)}, bf16[2,2,128,128]{3,2,1,0:T(8,128)(2,1)S(1)}, u32[]{:S(2)}, u32[]{:S(2)}) %collective-permute-start.11) | collective-permute-done | bytes 131104 | tf_op jit(solution)/shard_map/ppermute | solution.py:431
  61.7 2.3 %collective-permute-done.12.refs_11_ = bf16[2,2,128,128]{3,2,1,0:T(8,128)(2,1)S(1)} collective-permute-done((bf16[2,2,128,128]{3,2,1,0:T(8,128)(2,1)S(1)}, bf16[2,2,128,128]{3,2,1,0:T(8,128)(2,1)S(1)}, u32[]{:S(2)}, u32[]{:S(2)}) %collective-permute-start.12) | collective-permute-done | bytes 131104 | tf_op jit(solution)/shard_map/ppermute | solution.py:431
  64.0 2.2 %spatial.3.refs_0_ = bf16[4,2,128,128]{3,2,1,0:T(8,128)(2,1)S(1)} custom-call(s32[8,4,8]{2,1,0:T(4,128)S(1)} %copy-done.2, bf16[8,4,8,128,128]{4,3,2,1,0:T(8,128)(2,1)S(1)} %bitcast.5, bf16[128,128]{1,0:T(8,128)(2,1)S(1)} %get-tuple-element.45.weight_ref, f32[8,128]{1,0:T(8,128)S(1)} %get-tuple-element.46.pos_ref, bf16[8,4,128,128]{3,2,1,0:T(8,128)(2,1)S(1)} %bitcast.9, ...), custom_call_target="tpu_custom_call" | custom-call | flops 2300000000 | bytes 1024 | tf_op jit(solution)/shard_map/spatial/pallas_call | solution.py:226
  70.2 1.3 %collective-permute-start.21 = (bf16[3,2,128,128]{3,2,1,0:T(8,128)(2,1)S(1)}, bf16[3,2,128,128]{3,2,1,0:T(8,128)(2,1)S(1)}, u32[]{:S(2)}, u32[]{:S(2)}) collective-permute-start(bf16[3,2,128,128]{3,2,1,0:T(8,128)(2,1)S(1)} %get-tuple-element.67), channel_id=1, source_target_pairs={{4,7},{5,6},{2,1},{3,0},{12,15},{13,14},{10,9},{11,8},{20,23},{21,... | collective-permute-start | bytes 589832 | tf_op jit(solution)/shard_map/ppermute | solution.py:431
  72.4 3.0 %spatial.4.refs_1_.refs_4_ = bf16[4,3,128,128]{3,2,1,0:T(8,128)(2,1)S(1)} custom-call(s32[8,4,8]{2,1,0:T(4,128)S(1)} %copy-done.2, bf16[8,4,8,128,128]{4,3,2,1,0:T(8,128)(2,1)S(1)} %bitcast.5, bf16[128,128]{1,0:T(8,128)(2,1)S(1)} %get-tuple-element.45.weight_ref, f32[8,128]{1,0:T(8,128)S(1)} %get-tuple-element.46.pos_ref, ...), custom_call_target="tpu_custom_call" | custom-call | flops 3449999872 | bytes 1024 | tf_op jit(solution)/shard_map/spatial/pallas_call | solution.py:226
  75.4 1.3 %collective-permute-start.19 = (bf16[4,3,128,128]{3,2,1,0:T(8,128)(2,1)S(1)}, bf16[4,3,128,128]{3,2,1,0:T(8,128)(2,1)S(1)}, u32[]{:S(2)}, u32[]{:S(2)}) collective-permute-start(bf16[4,3,128,128]{3,2,1,0:T(8,128)(2,1)S(1)} %spatial.4.refs_1_.refs_4_), channel_id=1, source_target_pairs={{0,16},{8,24},{1,17},{9,25},{2,18},{10,26},{3,19},{11,27},{4,20},{... | collective-permute-start | bytes 1179656 | tf_op jit(solution)/shard_map/ppermute | solution.py:476
  76.7 2.3 %collective-permute-done.21.refs_11_ = bf16[3,2,128,128]{3,2,1,0:T(8,128)(2,1)S(1)} collective-permute-done((bf16[3,2,128,128]{3,2,1,0:T(8,128)(2,1)S(1)}, bf16[3,2,128,128]{3,2,1,0:T(8,128)(2,1)S(1)}, u32[]{:S(2)}, u32[]{:S(2)}) %collective-permute-start.21) | collective-permute-done | bytes 196640 | tf_op jit(solution)/shard_map/ppermute | solution.py:431
  79.0 3.0 %spatial.5.refs_2_.refs_8_ = bf16[4,3,128,128]{3,2,1,0:T(8,128)(2,1)S(1)} custom-call(s32[8,4,8]{2,1,0:T(4,128)S(1)} %copy-done.2, bf16[8,4,8,128,128]{4,3,2,1,0:T(8,128)(2,1)S(1)} %bitcast.5, bf16[128,128]{1,0:T(8,128)(2,1)S(1)} %get-tuple-element.45.weight_ref, f32[8,128]{1,0:T(8,128)S(1)} %get-tuple-element.46.pos_ref, ...), custom_call_target="tpu_custom_call" | custom-call | flops 3449999872 | bytes 1024 | tf_op jit(solution)/shard_map/spatial/pallas_call | solution.py:226
  85.9 7.6 %collective-permute-start.17 = (bf16[4,2,128,128]{3,2,1,0:T(8,128)(2,1)S(1)}, bf16[4,2,128,128]{3,2,1,0:T(8,128)(2,1)S(1)}, u32[]{:S(2)}, u32[]{:S(2)}) collective-permute-start(bf16[4,2,128,128]{3,2,1,0:T(8,128)(2,1)S(1)} %collective-permute-done.14.refs_2_), channel_id=1, source_target_pairs={{16,24},{24,16},{17,25},{25,17},{18,26},{26,18},{19,27},{27,19},{2... | collective-permute-start | bytes 786440 | tf_op jit(solution)/shard_map/ppermute | solution.py:486
  93.5 1.9 %collective-permute-start.22 = (bf16[4,3,128,128]{3,2,1,0:T(8,128)(2,1)S(1)}, bf16[4,3,128,128]{3,2,1,0:T(8,128)(2,1)S(1)}, u32[]{:S(2)}, u32[]{:S(2)}) collective-permute-start(bf16[4,3,128,128]{3,2,1,0:T(8,128)(2,1)S(1)} %collective-permute-done.19.refs_6_), channel_id=1, source_target_pairs={{16,24},{24,16},{17,25},{25,17},{18,26},{26,18},{19,27},{27,19},{2... | collective-permute-start | bytes 1179656 | tf_op jit(solution)/shard_map/ppermute | solution.py:486
  95.4 4.5 %collective-permute-start.25 = (bf16[4,3,128,128]{3,2,1,0:T(8,128)(2,1)S(1)}, bf16[4,3,128,128]{3,2,1,0:T(8,128)(2,1)S(1)}, u32[]{:S(2)}, u32[]{:S(2)}) collective-permute-start(bf16[4,3,128,128]{3,2,1,0:T(8,128)(2,1)S(1)} %collective-permute-done.24.refs_10_), channel_id=1, source_target_pairs={{16,24},{24,16},{17,25},{25,17},{18,26},{26,18},{19,27},{27,19},{2... | collective-permute-start | bytes 1179656 | tf_op jit(solution)/shard_map/ppermute | solution.py:486
  100.0 2.4 %temporal_own.1 = (bf16[4,8,128,128]{3,2,1,0:T(8,128)(2,1)S(1)}, f32[4,8,128,128]{3,2,1,0:T(8,128)S(1)}, f32[4,8,16,128]{3,2,1,0:T(8,128)S(1)}) custom-call(bf16[384,128]{1,0:T(8,128)(2,1)S(1)} %get-tuple-element.39.qkv_ref, bf16[4,2,128,128]{3,2,1,0:T(8,128)(2,1)S(1)} %spatial.3.refs_0_, bf16[4,3,128,128]{3,2,1,0:T(8,128)(2,1)S(1)} %spatial.4.refs_1_.refs_4_, ...), custom_call_target="tpu_custom_call" | custom-call | flops 6899999744 | bytes 1024 | tf_op jit(solution)/shard_map/temporal_own/pallas_call | solution.py:304
  102.4 17.1 %temporal.1 = bf16[8,512,128]{2,1,0:T(8,128)(2,1)} custom-call(s32[1]{0:T(128)} %bitcast.me_ref, bf16[384,128]{1,0:T(8,128)(2,1)S(1)} %get-tuple-element.39.qkv_ref, bf16[128,128]{1,0:T(8,128)(2,1)S(1)} %get-tuple-element.40.proj_ref, f32[128,128]{1,0:T(8,128)S(1)} %get-tuple-element.41.gain_ref, bf16[512,128]{1,0:T(8,128)(2,1)S(1)} %get-tuple-element.42.up_ref, ...), custom_call_target="tpu_custom_call" | custom-call | flops 11500000256 | bytes 1024 | tf_op jit(solution)/shard_map/temporal/pallas_call | solution.py:386
  (68 shorter events, 25.7 us)
Async XLA Ops:
  0.0 26.5 %collective-permute-start.4 = (bf16[8,4,128,128]{3,2,1,0:T(8,128)(2,1)}, bf16[8,4,128,128]{3,2,1,0:T(8,128)(2,1)S(1)}, u32[]{:S(2)}, u32[]{:S(2)}) collective-permute-start(bf16[8,4,128,128]{3,2,1,0:T(8,128)(2,1)} %bitcast.6), channel_id=1, source_target_pairs={{2,4},{3,5},{4,2},{5,3},{10,12},{11,13},{12,10},{13,11},{18,20},{1... | collective-permute-start | bytes 3145736 | tf_op jit(solution)/shard_map/ppermute | solution.py:431
  0.7 26.6 %collective-permute-start = (bf16[8,4,128,128]{3,2,1,0:T(8,128)(2,1)}, bf16[8,4,128,128]{3,2,1,0:T(8,128)(2,1)S(1)}, u32[]{:S(2)}, u32[]{:S(2)}) collective-permute-start(bf16[8,4,128,128]{3,2,1,0:T(8,128)(2,1)} %bitcast.7), channel_id=1, source_target_pairs={{0,2},{1,3},{2,0},{3,1},{4,6},{5,7},{6,4},{7,5},{8,10},{9,11},{10,... | collective-permute-start | bytes 3145736 | tf_op jit(solution)/shard_map/ppermute | solution.py:411
  12.7 13.8 %collective-permute-start.3 = (bf16[8,2,128,128]{3,2,1,0:T(8,128)(2,1)S(1)}, bf16[8,2,128,128]{3,2,1,0:T(8,128)(2,1)S(1)}, u32[]{:S(2)}, u32[]{:S(2)}) collective-permute-start(bf16[8,2,128,128]{3,2,1,0:T(8,128)(2,1)S(1)} %pick_blocks.3), channel_id=1, source_target_pairs={{0,1},{1,0},{2,3},{3,2},{4,5},{5,4},{6,7},{7,6},{8,9},{9,8},{10,11... | collective-permute-start | bytes 1572872 | tf_op jit(solution)/shard_map/ppermute | solution.py:411
  14.6 11.8 %collective-permute-start.2 = (s32[8,2,16]{2,1,0:T(2,128)S(1)}, s32[8,2,16]{2,1,0:T(2,128)S(1)}, u32[]{:S(2)}, u32[]{:S(2)}) collective-permute-start(s32[8,2,16]{2,1,0:T(2,128)S(1)} %pad_add_fusion), channel_id=1, source_target_pairs={{6,4},{7,5},{0,2},{1,3},{14,12},{15,13},{8,10},{9,11},{22,20},{23,... | collective-permute-start | bytes 3080 | tf_op jit(solution)/shard_map/ppermute | solution.py:431
  29.0 11.9 %collective-permute-start.6 = (bf16[8,2,128,128]{3,2,1,0:T(8,128)(2,1)S(1)}, bf16[8,2,128,128]{3,2,1,0:T(8,128)(2,1)S(1)}, u32[]{:S(2)}, u32[]{:S(2)}) collective-permute-start(bf16[8,2,128,128]{3,2,1,0:T(8,128)(2,1)S(1)} %get-tuple-element.52), channel_id=1, source_target_pairs={{0,1},{1,0},{2,3},{3,2},{4,5},{5,4},{6,7},{7,6},{8,9},{9,8},{10,11... | collective-permute-start | bytes 1572872 | tf_op jit(solution)/shard_map/ppermute | solution.py:411
  30.3 12.2 %collective-permute-start.7 = (bf16[8,2,128,128]{3,2,1,0:T(8,128)(2,1)S(1)}, bf16[8,2,128,128]{3,2,1,0:T(8,128)(2,1)S(1)}, u32[]{:S(2)}, u32[]{:S(2)}) collective-permute-start(bf16[8,2,128,128]{3,2,1,0:T(8,128)(2,1)S(1)} %get-tuple-element.53), channel_id=1, source_target_pairs={{2,3},{3,2},{4,5},{5,4},{10,11},{11,10},{12,13},{13,12},{18,19},{1... | collective-permute-start | bytes 1572872 | tf_op jit(solution)/shard_map/ppermute | solution.py:431
  31.0 15.1 %collective-permute-start.9 = (bf16[8,2,128,128]{3,2,1,0:T(8,128)(2,1)S(1)}, bf16[8,2,128,128]{3,2,1,0:T(8,128)(2,1)S(1)}, u32[]{:S(2)}, u32[]{:S(2)}) collective-permute-start(bf16[8,2,128,128]{3,2,1,0:T(8,128)(2,1)S(1)} %get-tuple-element.55), channel_id=1, source_target_pairs={{4,6},{5,7},{2,0},{3,1},{12,14},{13,15},{10,8},{11,9},{20,22},{21,... | collective-permute-start | bytes 1572872 | tf_op jit(solution)/shard_map/ppermute | solution.py:431
  32.3 25.8 %collective-permute-start.10 = (bf16[8,2,128,128]{3,2,1,0:T(8,128)(2,1)S(1)}, bf16[8,2,128,128]{3,2,1,0:T(8,128)(2,1)S(1)}, u32[]{:S(2)}, u32[]{:S(2)}) collective-permute-start(bf16[8,2,128,128]{3,2,1,0:T(8,128)(2,1)S(1)} %get-tuple-element.56), channel_id=1, source_target_pairs={{4,7},{5,6},{2,1},{3,0},{12,15},{13,14},{10,9},{11,8},{20,23},{21,... | collective-permute-start | bytes 1572872 | tf_op jit(solution)/shard_map/ppermute | solution.py:431
  34.4 29.6 %collective-permute-start.8 = (bf16[8,2,128,128]{3,2,1,0:T(8,128)(2,1)S(1)}, bf16[8,2,128,128]{3,2,1,0:T(8,128)(2,1)S(1)}, u32[]{:S(2)}, u32[]{:S(2)}) collective-permute-start(bf16[8,2,128,128]{3,2,1,0:T(8,128)(2,1)S(1)} %get-tuple-element.54), channel_id=1, source_target_pairs={{2,3},{3,2},{4,5},{5,4},{10,11},{11,10},{12,13},{13,12},{18,19},{1... | collective-permute-start | bytes 1572872 | tf_op jit(solution)/shard_map/ppermute | solution.py:431
  40.9 20.7 %collective-permute-start.11 = (bf16[2,2,128,128]{3,2,1,0:T(8,128)(2,1)S(1)}, bf16[2,2,128,128]{3,2,1,0:T(8,128)(2,1)S(1)}, u32[]{:S(2)}, u32[]{:S(2)}) collective-permute-start(bf16[2,2,128,128]{3,2,1,0:T(8,128)(2,1)S(1)} %get-tuple-element.57), channel_id=1, source_target_pairs={{4,6},{5,7},{2,0},{3,1},{12,14},{13,15},{10,8},{11,9},{20,22},{21,... | collective-permute-start | bytes 393224 | tf_op jit(solution)/shard_map/ppermute | solution.py:431
  42.5 21.5 %collective-permute-start.12 = (bf16[2,2,128,128]{3,2,1,0:T(8,128)(2,1)S(1)}, bf16[2,2,128,128]{3,2,1,0:T(8,128)(2,1)S(1)}, u32[]{:S(2)}, u32[]{:S(2)}) collective-permute-start(bf16[2,2,128,128]{3,2,1,0:T(8,128)(2,1)S(1)} %get-tuple-element.58), channel_id=1, source_target_pairs={{4,7},{5,6},{2,1},{3,0},{12,15},{13,14},{10,9},{11,8},{20,23},{21,... | collective-permute-start | bytes 393224 | tf_op jit(solution)/shard_map/ppermute | solution.py:431
  46.1 24.1 %collective-permute-start.15 = (bf16[3,2,128,128]{3,2,1,0:T(8,128)(2,1)S(1)}, bf16[3,2,128,128]{3,2,1,0:T(8,128)(2,1)S(1)}, u32[]{:S(2)}, u32[]{:S(2)}) collective-permute-start(bf16[3,2,128,128]{3,2,1,0:T(8,128)(2,1)S(1)} %get-tuple-element.60), channel_id=1, source_target_pairs={{4,6},{5,7},{2,0},{3,1},{12,14},{13,15},{10,8},{11,9},{20,22},{21,... | collective-permute-start | bytes 589832 | tf_op jit(solution)/shard_map/ppermute | solution.py:431
  58.1 14.3 %collective-permute-start.16 = (bf16[3,2,128,128]{3,2,1,0:T(8,128)(2,1)S(1)}, bf16[3,2,128,128]{3,2,1,0:T(8,128)(2,1)S(1)}, u32[]{:S(2)}, u32[]{:S(2)}) collective-permute-start(bf16[3,2,128,128]{3,2,1,0:T(8,128)(2,1)S(1)} %get-tuple-element.61), channel_id=1, source_target_pairs={{4,7},{5,6},{2,1},{3,0},{12,15},{13,14},{10,9},{11,8},{20,23},{21,... | collective-permute-start | bytes 589832 | tf_op jit(solution)/shard_map/ppermute | solution.py:431
  66.3 10.4 %collective-permute-start.14 = (bf16[4,2,128,128]{3,2,1,0:T(8,128)(2,1)S(1)}, bf16[4,2,128,128]{3,2,1,0:T(8,128)(2,1)S(1)}, u32[]{:S(2)}, u32[]{:S(2)}) collective-permute-start(bf16[4,2,128,128]{3,2,1,0:T(8,128)(2,1)S(1)} %spatial.3.refs_0_), channel_id=1, source_target_pairs={{0,16},{8,24},{1,17},{9,25},{2,18},{10,26},{3,19},{11,27},{4,20},{... | collective-permute-start | bytes 786440 | tf_op jit(solution)/shard_map/ppermute | solution.py:476
  67.6 9.1 %collective-permute-start.13 = (bf16[4,2,128,128]{3,2,1,0:T(8,128)(2,1)S(1)}, bf16[4,2,128,128]{3,2,1,0:T(8,128)(2,1)S(1)}, u32[]{:S(2)}, u32[]{:S(2)}) collective-permute-start(bf16[4,2,128,128]{3,2,1,0:T(8,128)(2,1)S(1)} %spatial.3.refs_0_), channel_id=1, source_target_pairs={{0,8},{16,24},{1,9},{17,25},{2,10},{18,26},{3,11},{19,27},{4,12},{... | collective-permute-start | bytes 786440 | tf_op jit(solution)/shard_map/ppermute | solution.py:476
  68.9 7.9 %collective-permute-start.20 = (bf16[3,2,128,128]{3,2,1,0:T(8,128)(2,1)S(1)}, bf16[3,2,128,128]{3,2,1,0:T(8,128)(2,1)S(1)}, u32[]{:S(2)}, u32[]{:S(2)}) collective-permute-start(bf16[3,2,128,128]{3,2,1,0:T(8,128)(2,1)S(1)} %get-tuple-element.66), channel_id=1, source_target_pairs={{4,6},{5,7},{2,0},{3,1},{12,14},{13,15},{10,8},{11,9},{20,22},{21,... | collective-permute-start | bytes 589832 | tf_op jit(solution)/shard_map/ppermute | solution.py:431
  70.2 8.8 %collective-permute-start.21 = (bf16[3,2,128,128]{3,2,1,0:T(8,128)(2,1)S(1)}, bf16[3,2,128,128]{3,2,1,0:T(8,128)(2,1)S(1)}, u32[]{:S(2)}, u32[]{:S(2)}) collective-permute-start(bf16[3,2,128,128]{3,2,1,0:T(8,128)(2,1)S(1)} %get-tuple-element.67), channel_id=1, source_target_pairs={{4,7},{5,6},{2,1},{3,0},{12,15},{13,14},{10,9},{11,8},{20,23},{21,... | collective-permute-start | bytes 589832 | tf_op jit(solution)/shard_map/ppermute | solution.py:431
  75.4 18.1 %collective-permute-start.19 = (bf16[4,3,128,128]{3,2,1,0:T(8,128)(2,1)S(1)}, bf16[4,3,128,128]{3,2,1,0:T(8,128)(2,1)S(1)}, u32[]{:S(2)}, u32[]{:S(2)}) collective-permute-start(bf16[4,3,128,128]{3,2,1,0:T(8,128)(2,1)S(1)} %spatial.4.refs_1_.refs_4_), channel_id=1, source_target_pairs={{0,16},{8,24},{1,17},{9,25},{2,18},{10,26},{3,19},{11,27},{4,20},{... | collective-permute-start | bytes 1179656 | tf_op jit(solution)/shard_map/ppermute | solution.py:476
  82.0 13.4 %collective-permute-start.24 = (bf16[4,3,128,128]{3,2,1,0:T(8,128)(2,1)S(1)}, bf16[4,3,128,128]{3,2,1,0:T(8,128)(2,1)S(1)}, u32[]{:S(2)}, u32[]{:S(2)}) collective-permute-start(bf16[4,3,128,128]{3,2,1,0:T(8,128)(2,1)S(1)} %spatial.5.refs_2_.refs_8_), channel_id=1, source_target_pairs={{0,16},{8,24},{1,17},{9,25},{2,18},{10,26},{3,19},{11,27},{4,20},{... | collective-permute-start | bytes 1179656 | tf_op jit(solution)/shard_map/ppermute | solution.py:476
  83.3 19.1 %collective-permute-start.18 = (bf16[4,3,128,128]{3,2,1,0:T(8,128)(2,1)S(1)}, bf16[4,3,128,128]{3,2,1,0:T(8,128)(2,1)S(1)}, u32[]{:S(2)}, u32[]{:S(2)}) collective-permute-start(bf16[4,3,128,128]{3,2,1,0:T(8,128)(2,1)S(1)} %spatial.4.refs_1_.refs_4_), channel_id=1, source_target_pairs={{0,8},{16,24},{1,9},{17,25},{2,10},{18,26},{3,11},{19,27},{4,12},{... | collective-permute-start | bytes 1179656 | tf_op jit(solution)/shard_map/ppermute | solution.py:476
  84.6 17.8 %collective-permute-start.23 = (bf16[4,3,128,128]{3,2,1,0:T(8,128)(2,1)S(1)}, bf16[4,3,128,128]{3,2,1,0:T(8,128)(2,1)S(1)}, u32[]{:S(2)}, u32[]{:S(2)}) collective-permute-start(bf16[4,3,128,128]{3,2,1,0:T(8,128)(2,1)S(1)} %spatial.5.refs_2_.refs_8_), channel_id=1, source_target_pairs={{0,8},{16,24},{1,9},{17,25},{2,10},{18,26},{3,11},{19,27},{4,12},{... | collective-permute-start | bytes 1179656 | tf_op jit(solution)/shard_map/ppermute | solution.py:476
  85.9 16.5 %collective-permute-start.17 = (bf16[4,2,128,128]{3,2,1,0:T(8,128)(2,1)S(1)}, bf16[4,2,128,128]{3,2,1,0:T(8,128)(2,1)S(1)}, u32[]{:S(2)}, u32[]{:S(2)}) collective-permute-start(bf16[4,2,128,128]{3,2,1,0:T(8,128)(2,1)S(1)} %collective-permute-done.14.refs_2_), channel_id=1, source_target_pairs={{16,24},{24,16},{17,25},{25,17},{18,26},{26,18},{19,27},{27,19},{2... | collective-permute-start | bytes 786440 | tf_op jit(solution)/shard_map/ppermute | solution.py:486
  93.5 8.9 %collective-permute-start.22 = (bf16[4,3,128,128]{3,2,1,0:T(8,128)(2,1)S(1)}, bf16[4,3,128,128]{3,2,1,0:T(8,128)(2,1)S(1)}, u32[]{:S(2)}, u32[]{:S(2)}) collective-permute-start(bf16[4,3,128,128]{3,2,1,0:T(8,128)(2,1)S(1)} %collective-permute-done.19.refs_6_), channel_id=1, source_target_pairs={{16,24},{24,16},{17,25},{25,17},{18,26},{26,18},{19,27},{27,19},{2... | collective-permute-start | bytes 1179656 | tf_op jit(solution)/shard_map/ppermute | solution.py:486
  95.4 7.0 %collective-permute-start.25 = (bf16[4,3,128,128]{3,2,1,0:T(8,128)(2,1)S(1)}, bf16[4,3,128,128]{3,2,1,0:T(8,128)(2,1)S(1)}, u32[]{:S(2)}, u32[]{:S(2)}) collective-permute-start(bf16[4,3,128,128]{3,2,1,0:T(8,128)(2,1)S(1)} %collective-permute-done.24.refs_10_), channel_id=1, source_target_pairs={{16,24},{24,16},{17,25},{25,17},{18,26},{26,18},{19,27},{27,19},{2... | collective-permute-start | bytes 1179656 | tf_op jit(solution)/shard_map/ppermute | solution.py:486
  (15 other events, 450.8 us)

commit v6 on v5

--- a/solution.py
+++ b/solution.py
@@ -425,7 +425,7 @@
     return [(0, snaps, lambda before: [(a, 0) for a in layer + arrived])]
 
 
-def exchange_forward(blocks, want):
+def exchange_forward(blocks, want, turned_weights):
     snaps = blocks.shape[0]
     layers = lambda pairs, x=0: [(a * 2 + i, b * 2 + (i ^ x)) for a, b in pairs for i in range(2)]
     go = lambda a, pairs, x=0: lax.ppermute(a, "vert", layers(pairs, x))
@@ -439,7 +439,7 @@
     (xo,) = pick([blocks], [0], wants[:1], [(0, [(0, 1)], 0, snaps)])
     xo = send(xo, 1)
     both = go(jnp.concatenate([want, wants[0]], axis=1), back)
-    beside, both, xo, p1 = after((beside, both, xo, p1))
+    beside, both, xo, p1, turned_weights = after((beside, both, xo, p1, turned_weights))
     wants[1:] = both[:, :1], both[:, 1:]
 
     p2 = go(beside, cross)
@@ -464,7 +464,7 @@
 
         return (*span, get)
 
-    return [part(span, a, b) for span, a, b in zip(spans, late[::2], late[1::2])]
+    return [part(span, a, b) for span, a, b in zip(spans, late[::2], late[1::2])], turned_weights
 
 
 def gather_times(own):
@@ -514,7 +514,10 @@
         at, snaps, positions, attn_proj, attn_out, norm_gain, mlp_up, mlp_down, space_weight
     )
     me = me_t.reshape(1)
-    parts = exchange_forward(blocks, want) if forward else exchange_direct(blocks, want, inner)
+    if forward:
+        parts, space_t = exchange_forward(blocks, want, space_t)
+    else:
+        parts = exchange_direct(blocks, want, inner)
 
     started, owns = [], []
     held = [get(None) for _, _, get in parts[:2]]

time: 120 us -> 120 us (level)
  no operation moved by 1% of the time
where the time goes in v6:
time: 120 us; the launch traced here: 119 us
  starting transfers between devices  44.3 us (37%)
  waiting for transfers between devices  38.6 us (32%)
  Pallas kernels  33.5 us (28%)
  local copies, waits for them, and re-layouts  1.29 us (1%)
  other arithmetic  1.24 us (1%)
    ppermute x13, waiting for transfers between devices, exchange_forward(): go = lambda a, pairs, x=0: lax.ppermute(a, 'vert', layers(pairs, x))  30.1 us
    pallas_call x1, Pallas kernels, temporal(): pl.pallas_call(functools.partial(temporal_kernel, sizes, count - 1), grid...  17.1 us
    ppermute x13, starting transfers between devices, exchange_forward(): go = lambda a, pairs, x=0: lax.ppermute(a, 'vert', layers(pairs, x))  15.2 us
    ppermute x3, starting transfers between devices, pass_on(): got[k] = lax.ppermute(got[k - 1], 'tm', pairs)  13.8 us
    ppermute x4, waiting for transfers between devices, send(): lax.ppermute(a, 'vert', [(v, v ^ k) for v in range(lax.axis_size('vert'))])  8.45 us
    pallas_call x3, Pallas kernels, spatial(): pl.pallas_call(functools.partial(spatial_kernel, start, [first for _, fir...  8.21 us
    ppermute x6, starting transfers between devices, gather_times(): got[k] = lax.ppermute(own, 'tm', pairs)  7.75 us
    ppermute x4, starting transfers between devices, send(): lax.ppermute(a, 'vert', [(v, v ^ k) for v in range(lax.axis_size('vert'))])  7.6 us
  transfers between devices with their start and end apart: 26, of which 10 were waited for; matrix products, arithmetic and copies ran while one was open for 1% of the time, Pallas kernels for 14%

profile of v6, /device:TPU:5, one launch (start us, length us, event | category | flops | bytes accessed | tf_op | source)
XLA Modules:
  0.0 119.5 jit_solution(15663796734226090186)
XLA Ops:
  0.9 3.8 %collective-permute-start = (bf16[8,4,128,128]{3,2,1,0:T(8,128)(2,1)}, bf16[8,4,128,128]{3,2,1,0:T(8,128)(2,1)S(1)}, u32[]{:S(2)}, u32[]{:S(2)}) collective-permute-start(bf16[8,4,128,128]{3,2,1,0:T(8,128)(2,1)} %bitcast.7), channel_id=1, source_target_pairs={{0,2},{1,3},{2,0},{3,1},{4,6},{5,7},{6,4},{7,5},{8,10},{9,11},{10,... | collective-permute-start | bytes 3145736 | tf_op jit(solution)/shard_map/ppermute | solution.py:411
  5.3 2.6 %lists.1 = (s32[8,1,16]{2,1,0:T(1,128)}, s32[8,4,8]{2,1,0:T(4,128)}) custom-call(s32[2]{0:T(128)} %pad_add_fusion.1.at_ref, s32[8,4,8]{2,1,0:T(4,128)} %cols_ref.1), custom_call_target="tpu_custom_call" | custom-call | flops 1150000000 | bytes 1024 | tf_op jit(solution)/shard_map/lists/pallas_call | solution.py:82
  9.2 1.8 %collective-permute-done.1.refs_0_ = s32[8,1,16]{2,1,0:T(1,128)S(1)} collective-permute-done((s32[8,1,16]{2,1,0:T(1,128)}, s32[8,1,16]{2,1,0:T(1,128)S(1)}, u32[]{:S(2)}, u32[]{:S(2)}) %collective-permute-start.1) | collective-permute-done | bytes 544 | tf_op jit(solution)/shard_map/ppermute | solution.py:411
  14.8 1.9 %collective-permute-start.2 = (s32[8,2,16]{2,1,0:T(2,128)S(1)}, s32[8,2,16]{2,1,0:T(2,128)S(1)}, u32[]{:S(2)}, u32[]{:S(2)}) collective-permute-start(s32[8,2,16]{2,1,0:T(2,128)S(1)} %pad_add_fusion), channel_id=1, source_target_pairs={{6,4},{7,5},{0,2},{1,3},{14,12},{15,13},{8,10},{9,11},{22,20},{23,... | collective-permute-start | bytes 3080 | tf_op jit(solution)/shard_map/ppermute | solution.py:431
  17.6 9.1 %collective-permute-done.2 = s32[8,2,16]{2,1,0:T(2,128)S(1)} collective-permute-done((s32[8,2,16]{2,1,0:T(2,128)S(1)}, s32[8,2,16]{2,1,0:T(2,128)S(1)}, u32[]{:S(2)}, u32[]{:S(2)}) %collective-permute-start.2) | collective-permute-done | bytes 1056 | tf_op jit(solution)/shard_map/ppermute | solution.py:431
  31.1 1.3 %collective-permute-start.9 = (bf16[8,2,128,128]{3,2,1,0:T(8,128)(2,1)S(1)}, bf16[8,2,128,128]{3,2,1,0:T(8,128)(2,1)S(1)}, u32[]{:S(2)}, u32[]{:S(2)}) collective-permute-start(bf16[8,2,128,128]{3,2,1,0:T(8,128)(2,1)S(1)} %get-tuple-element.57), channel_id=1, source_target_pairs={{4,6},{5,7},{2,0},{3,1},{12,14},{13,15},{10,8},{11,9},{20,22},{21,... | collective-permute-start | bytes 1572872 | tf_op jit(solution)/shard_map/ppermute | solution.py:431
  32.4 1.3 %collective-permute-start.10 = (bf16[8,2,128,128]{3,2,1,0:T(8,128)(2,1)S(1)}, bf16[8,2,128,128]{3,2,1,0:T(8,128)(2,1)S(1)}, u32[]{:S(2)}, u32[]{:S(2)}) collective-permute-start(bf16[8,2,128,128]{3,2,1,0:T(8,128)(2,1)S(1)} %get-tuple-element.58), channel_id=1, source_target_pairs={{4,7},{5,6},{2,1},{3,0},{12,15},{13,14},{10,9},{11,8},{20,23},{21,... | collective-permute-start | bytes 1572872 | tf_op jit(solution)/shard_map/ppermute | solution.py:431
  35.3 5.8 %collective-permute-done.6.refs_5_ = bf16[8,2,128,128]{3,2,1,0:T(8,128)(2,1)S(1)} collective-permute-done((bf16[8,2,128,128]{3,2,1,0:T(8,128)(2,1)S(1)}, bf16[8,2,128,128]{3,2,1,0:T(8,128)(2,1)S(1)}, u32[]{:S(2)}, u32[]{:S(2)}) %collective-permute-start.6) | collective-permute-done | bytes 524320 | tf_op jit(solution)/shard_map/ppermute | solution.py:411
  42.4 1.3 %collective-permute-start.12 = (bf16[2,2,128,128]{3,2,1,0:T(8,128)(2,1)S(1)}, bf16[2,2,128,128]{3,2,1,0:T(8,128)(2,1)S(1)}, u32[]{:S(2)}, u32[]{:S(2)}) collective-permute-start(bf16[2,2,128,128]{3,2,1,0:T(8,128)(2,1)S(1)} %get-tuple-element.60), channel_id=1, source_target_pairs={{4,7},{5,6},{2,1},{3,0},{12,15},{13,14},{10,9},{11,8},{20,23},{21,... | collective-permute-start | bytes 393224 | tf_op jit(solution)/shard_map/ppermute | solution.py:431
  43.7 2.7 %collective-permute-done.9.refs_8_ = bf16[8,2,128,128]{3,2,1,0:T(8,128)(2,1)S(1)} collective-permute-done((bf16[8,2,128,128]{3,2,1,0:T(8,128)(2,1)S(1)}, bf16[8,2,128,128]{3,2,1,0:T(8,128)(2,1)S(1)}, u32[]{:S(2)}, u32[]{:S(2)}) %collective-permute-start.9) | collective-permute-done | bytes 524320 | tf_op jit(solution)/shard_map/ppermute | solution.py:431
  47.7 10.6 %collective-permute-done.10.refs_9_ = bf16[8,2,128,128]{3,2,1,0:T(8,128)(2,1)S(1)} collective-permute-done((bf16[8,2,128,128]{3,2,1,0:T(8,128)(2,1)S(1)}, bf16[8,2,128,128]{3,2,1,0:T(8,128)(2,1)S(1)}, u32[]{:S(2)}, u32[]{:S(2)}) %collective-permute-start.10) | collective-permute-done | bytes 524320 | tf_op jit(solution)/shard_map/ppermute | solution.py:431
  59.6 2.3 %collective-permute-done.11.refs_10_ = bf16[2,2,128,128]{3,2,1,0:T(8,128)(2,1)S(1)} collective-permute-done((bf16[2,2,128,128]{3,2,1,0:T(8,128)(2,1)S(1)}, bf16[2,2,128,128]{3,2,1,0:T(8,128)(2,1)S(1)}, u32[]{:S(2)}, u32[]{:S(2)}) %collective-permute-start.11) | collective-permute-done | bytes 131104 | tf_op jit(solution)/shard_map/ppermute | solution.py:431
  61.8 2.6 %collective-permute-done.12.refs_11_ = bf16[2,2,128,128]{3,2,1,0:T(8,128)(2,1)S(1)} collective-permute-done((bf16[2,2,128,128]{3,2,1,0:T(8,128)(2,1)S(1)}, bf16[2,2,128,128]{3,2,1,0:T(8,128)(2,1)S(1)}, u32[]{:S(2)}, u32[]{:S(2)}) %collective-permute-start.12) | collective-permute-done | bytes 131104 | tf_op jit(solution)/shard_map/ppermute | solution.py:431
  64.5 2.2 %spatial.3.refs_0_ = bf16[4,2,128,128]{3,2,1,0:T(8,128)(2,1)S(1)} custom-call(s32[8,4,8]{2,1,0:T(4,128)S(1)} %copy-done.2, bf16[8,4,8,128,128]{4,3,2,1,0:T(8,128)(2,1)S(1)} %bitcast.5, bf16[128,128]{1,0:T(8,128)(2,1)S(1)} %get-tuple-element.48.weight_ref, f32[8,128]{1,0:T(8,128)S(1)} %get-tuple-element.49.pos_ref, bf16[8,4,128,128]{3,2,1,0:T(8,128)(2,1)S(1)} %bitcast.9, ...), custom_call_target="tpu_custom_call" | custom-call | flops 2300000000 | bytes 1024 | tf_op jit(solution)/shard_map/spatial/pallas_call | solution.py:226
  66.7 1.3 %collective-permute-start.14 = (bf16[4,2,128,128]{3,2,1,0:T(8,128)(2,1)S(1)}, bf16[4,2,128,128]{3,2,1,0:T(8,128)(2,1)S(1)}, u32[]{:S(2)}, u32[]{:S(2)}) collective-permute-start(bf16[4,2,128,128]{3,2,1,0:T(8,128)(2,1)S(1)} %spatial.3.refs_0_), channel_id=1, source_target_pairs={{0,16},{8,24},{1,17},{9,25},{2,18},{10,26},{3,19},{11,27},{4,20},{... | collective-permute-start | bytes 786440 | tf_op jit(solution)/shard_map/ppermute | solution.py:476
  70.6 1.3 %collective-permute-start.21 = (bf16[3,2,128,128]{3,2,1,0:T(8,128)(2,1)S(1)}, bf16[3,2,128,128]{3,2,1,0:T(8,128)(2,1)S(1)}, u32[]{:S(2)}, u32[]{:S(2)}) collective-permute-start(bf16[3,2,128,128]{3,2,1,0:T(8,128)(2,1)S(1)} %get-tuple-element.69), channel_id=1, source_target_pairs={{4,7},{5,6},{2,1},{3,0},{12,15},{13,14},{10,9},{11,8},{20,23},{21,... | collective-permute-start | bytes 589832 | tf_op jit(solution)/shard_map/ppermute | solution.py:431
  72.8 3.0 %spatial.4.refs_1_.refs_4_ = bf16[4,3,128,128]{3,2,1,0:T(8,128)(2,1)S(1)} custom-call(s32[8,4,8]{2,1,0:T(4,128)S(1)} %copy-done.2, bf16[8,4,8,128,128]{4,3,2,1,0:T(8,128)(2,1)S(1)} %bitcast.5, bf16[128,128]{1,0:T(8,128)(2,1)S(1)} %get-tuple-element.48.weight_ref, f32[8,128]{1,0:T(8,128)S(1)} %get-tuple-element.49.pos_ref, ...), custom_call_target="tpu_custom_call" | custom-call | flops 3449999872 | bytes 1024 | tf_op jit(solution)/shard_map/spatial/pallas_call | solution.py:226
  77.2 2.0 %collective-permute-done.21.refs_11_ = bf16[3,2,128,128]{3,2,1,0:T(8,128)(2,1)S(1)} collective-permute-done((bf16[3,2,128,128]{3,2,1,0:T(8,128)(2,1)S(1)}, bf16[3,2,128,128]{3,2,1,0:T(8,128)(2,1)S(1)}, u32[]{:S(2)}, u32[]{:S(2)}) %collective-permute-start.21) | collective-permute-done | bytes 196640 | tf_op jit(solution)/shard_map/ppermute | solution.py:431
  79.2 3.0 %spatial.5.refs_2_.refs_8_ = bf16[4,3,128,128]{3,2,1,0:T(8,128)(2,1)S(1)} custom-call(s32[8,4,8]{2,1,0:T(4,128)S(1)} %copy-done.2, bf16[8,4,8,128,128]{4,3,2,1,0:T(8,128)(2,1)S(1)} %bitcast.5, bf16[128,128]{1,0:T(8,128)(2,1)S(1)} %get-tuple-element.48.weight_ref, f32[8,128]{1,0:T(8,128)S(1)} %get-tuple-element.49.pos_ref, ...), custom_call_target="tpu_custom_call" | custom-call | flops 3449999872 | bytes 1024 | tf_op jit(solution)/shard_map/spatial/pallas_call | solution.py:226
  86.1 7.6 %collective-permute-start.17 = (bf16[4,2,128,128]{3,2,1,0:T(8,128)(2,1)S(1)}, bf16[4,2,128,128]{3,2,1,0:T(8,128)(2,1)S(1)}, u32[]{:S(2)}, u32[]{:S(2)}) collective-permute-start(bf16[4,2,128,128]{3,2,1,0:T(8,128)(2,1)S(1)} %collective-permute-done.14.refs_2_), channel_id=1, source_target_pairs={{16,24},{24,16},{17,25},{25,17},{18,26},{26,18},{19,27},{27,19},{2... | collective-permute-start | bytes 786440 | tf_op jit(solution)/shard_map/ppermute | solution.py:486
  93.7 1.9 %collective-permute-start.22 = (bf16[4,3,128,128]{3,2,1,0:T(8,128)(2,1)S(1)}, bf16[4,3,128,128]{3,2,1,0:T(8,128)(2,1)S(1)}, u32[]{:S(2)}, u32[]{:S(2)}) collective-permute-start(bf16[4,3,128,128]{3,2,1,0:T(8,128)(2,1)S(1)} %collective-permute-done.19.refs_6_), channel_id=1, source_target_pairs={{16,24},{24,16},{17,25},{25,17},{18,26},{26,18},{19,27},{27,19},{2... | collective-permute-start | bytes 1179656 | tf_op jit(solution)/shard_map/ppermute | solution.py:486
  95.6 4.2 %collective-permute-start.25 = (bf16[4,3,128,128]{3,2,1,0:T(8,128)(2,1)S(1)}, bf16[4,3,128,128]{3,2,1,0:T(8,128)(2,1)S(1)}, u32[]{:S(2)}, u32[]{:S(2)}) collective-permute-start(bf16[4,3,128,128]{3,2,1,0:T(8,128)(2,1)S(1)} %collective-permute-done.24.refs_10_), channel_id=1, source_target_pairs={{16,24},{24,16},{17,25},{25,17},{18,26},{26,18},{19,27},{27,19},{2... | collective-permute-start | bytes 1179656 | tf_op jit(solution)/shard_map/ppermute | solution.py:486
  99.9 2.4 %temporal_own.1 = (bf16[4,8,128,128]{3,2,1,0:T(8,128)(2,1)S(1)}, f32[4,8,128,128]{3,2,1,0:T(8,128)S(1)}, f32[4,8,16,128]{3,2,1,0:T(8,128)S(1)}) custom-call(bf16[384,128]{1,0:T(8,128)(2,1)S(1)} %get-tuple-element.40.qkv_ref, bf16[4,2,128,128]{3,2,1,0:T(8,128)(2,1)S(1)} %spatial.3.refs_0_, bf16[4,3,128,128]{3,2,1,0:T(8,128)(2,1)S(1)} %spatial.4.refs_1_.refs_4_, ...), custom_call_target="tpu_custom_call" | custom-call | flops 6899999744 | bytes 1024 | tf_op jit(solution)/shard_map/temporal_own/pallas_call | solution.py:304
  102.4 17.1 %temporal.1 = bf16[8,512,128]{2,1,0:T(8,128)(2,1)} custom-call(s32[1]{0:T(128)} %bitcast.me_ref, bf16[384,128]{1,0:T(8,128)(2,1)S(1)} %get-tuple-element.40.qkv_ref, bf16[128,128]{1,0:T(8,128)(2,1)S(1)} %get-tuple-element.41.proj_ref, f32[128,128]{1,0:T(8,128)S(1)} %get-tuple-element.42.gain_ref, bf16[512,128]{1,0:T(8,128)(2,1)S(1)} %get-tuple-element.43.up_ref, ...), custom_call_target="tpu_custom_call" | custom-call | flops 11500000256 | bytes 1024 | tf_op jit(solution)/shard_map/temporal/pallas_call | solution.py:386
  (68 shorter events, 25.8 us)
Async XLA Ops:
  0.0 26.6 %collective-permute-start.4 = (bf16[8,4,128,128]{3,2,1,0:T(8,128)(2,1)}, bf16[8,4,128,128]{3,2,1,0:T(8,128)(2,1)S(1)}, u32[]{:S(2)}, u32[]{:S(2)}) collective-permute-start(bf16[8,4,128,128]{3,2,1,0:T(8,128)(2,1)} %bitcast.6), channel_id=1, source_target_pairs={{2,4},{3,5},{4,2},{5,3},{10,12},{11,13},{12,10},{13,11},{18,20},{1... | collective-permute-start | bytes 3145736 | tf_op jit(solution)/shard_map/ppermute | solution.py:431
  0.9 26.6 %collective-permute-start = (bf16[8,4,128,128]{3,2,1,0:T(8,128)(2,1)}, bf16[8,4,128,128]{3,2,1,0:T(8,128)(2,1)S(1)}, u32[]{:S(2)}, u32[]{:S(2)}) collective-permute-start(bf16[8,4,128,128]{3,2,1,0:T(8,128)(2,1)} %bitcast.7), channel_id=1, source_target_pairs={{0,2},{1,3},{2,0},{3,1},{4,6},{5,7},{6,4},{7,5},{8,10},{9,11},{10,... | collective-permute-start | bytes 3145736 | tf_op jit(solution)/shard_map/ppermute | solution.py:411
  12.8 13.9 %collective-permute-start.3 = (bf16[8,2,128,128]{3,2,1,0:T(8,128)(2,1)S(1)}, bf16[8,2,128,128]{3,2,1,0:T(8,128)(2,1)S(1)}, u32[]{:S(2)}, u32[]{:S(2)}) collective-permute-start(bf16[8,2,128,128]{3,2,1,0:T(8,128)(2,1)S(1)} %pick_blocks.3), channel_id=1, source_target_pairs={{0,1},{1,0},{2,3},{3,2},{4,5},{5,4},{6,7},{7,6},{8,9},{9,8},{10,11... | collective-permute-start | bytes 1572872 | tf_op jit(solution)/shard_map/ppermute | solution.py:411
  14.8 11.9 %collective-permute-start.2 = (s32[8,2,16]{2,1,0:T(2,128)S(1)}, s32[8,2,16]{2,1,0:T(2,128)S(1)}, u32[]{:S(2)}, u32[]{:S(2)}) collective-permute-start(s32[8,2,16]{2,1,0:T(2,128)S(1)} %pad_add_fusion), channel_id=1, source_target_pairs={{6,4},{7,5},{0,2},{1,3},{14,12},{15,13},{8,10},{9,11},{22,20},{23,... | collective-permute-start | bytes 3080 | tf_op jit(solution)/shard_map/ppermute | solution.py:431
  29.2 11.9 %collective-permute-start.6 = (bf16[8,2,128,128]{3,2,1,0:T(8,128)(2,1)S(1)}, bf16[8,2,128,128]{3,2,1,0:T(8,128)(2,1)S(1)}, u32[]{:S(2)}, u32[]{:S(2)}) collective-permute-start(bf16[8,2,128,128]{3,2,1,0:T(8,128)(2,1)S(1)} %get-tuple-element.54), channel_id=1, source_target_pairs={{0,1},{1,0},{2,3},{3,2},{4,5},{5,4},{6,7},{7,6},{8,9},{9,8},{10,11... | collective-permute-start | bytes 1572872 | tf_op jit(solution)/shard_map/ppermute | solution.py:411
  30.4 12.0 %collective-permute-start.7 = (bf16[8,2,128,128]{3,2,1,0:T(8,128)(2,1)S(1)}, bf16[8,2,128,128]{3,2,1,0:T(8,128)(2,1)S(1)}, u32[]{:S(2)}, u32[]{:S(2)}) collective-permute-start(bf16[8,2,128,128]{3,2,1,0:T(8,128)(2,1)S(1)} %get-tuple-element.55), channel_id=1, source_target_pairs={{2,3},{3,2},{4,5},{5,4},{10,11},{11,10},{12,13},{13,12},{18,19},{1... | collective-permute-start | bytes 1572872 | tf_op jit(solution)/shard_map/ppermute | solution.py:431
  31.1 15.2 %collective-permute-start.9 = (bf16[8,2,128,128]{3,2,1,0:T(8,128)(2,1)S(1)}, bf16[8,2,128,128]{3,2,1,0:T(8,128)(2,1)S(1)}, u32[]{:S(2)}, u32[]{:S(2)}) collective-permute-start(bf16[8,2,128,128]{3,2,1,0:T(8,128)(2,1)S(1)} %get-tuple-element.57), channel_id=1, source_target_pairs={{4,6},{5,7},{2,0},{3,1},{12,14},{13,15},{10,8},{11,9},{20,22},{21,... | collective-permute-start | bytes 1572872 | tf_op jit(solution)/shard_map/ppermute | solution.py:431
  32.4 25.8 %collective-permute-start.10 = (bf16[8,2,128,128]{3,2,1,0:T(8,128)(2,1)S(1)}, bf16[8,2,128,128]{3,2,1,0:T(8,128)(2,1)S(1)}, u32[]{:S(2)}, u32[]{:S(2)}) collective-permute-start(bf16[8,2,128,128]{3,2,1,0:T(8,128)(2,1)S(1)} %get-tuple-element.58), channel_id=1, source_target_pairs={{4,7},{5,6},{2,1},{3,0},{12,15},{13,14},{10,9},{11,8},{20,23},{21,... | collective-permute-start | bytes 1572872 | tf_op jit(solution)/shard_map/ppermute | solution.py:431
  34.6 29.8 %collective-permute-start.8 = (bf16[8,2,128,128]{3,2,1,0:T(8,128)(2,1)S(1)}, bf16[8,2,128,128]{3,2,1,0:T(8,128)(2,1)S(1)}, u32[]{:S(2)}, u32[]{:S(2)}) collective-permute-start(bf16[8,2,128,128]{3,2,1,0:T(8,128)(2,1)S(1)} %get-tuple-element.56), channel_id=1, source_target_pairs={{2,3},{3,2},{4,5},{5,4},{10,11},{11,10},{12,13},{13,12},{18,19},{1... | collective-permute-start | bytes 1572872 | tf_op jit(solution)/shard_map/ppermute | solution.py:431
  41.1 20.7 %collective-permute-start.11 = (bf16[2,2,128,128]{3,2,1,0:T(8,128)(2,1)S(1)}, bf16[2,2,128,128]{3,2,1,0:T(8,128)(2,1)S(1)}, u32[]{:S(2)}, u32[]{:S(2)}) collective-permute-start(bf16[2,2,128,128]{3,2,1,0:T(8,128)(2,1)S(1)} %get-tuple-element.59), channel_id=1, source_target_pairs={{4,6},{5,7},{2,0},{3,1},{12,14},{13,15},{10,8},{11,9},{20,22},{21,... | collective-permute-start | bytes 393224 | tf_op jit(solution)/shard_map/ppermute | solution.py:431
  42.4 22.0 %collective-permute-start.12 = (bf16[2,2,128,128]{3,2,1,0:T(8,128)(2,1)S(1)}, bf16[2,2,128,128]{3,2,1,0:T(8,128)(2,1)S(1)}, u32[]{:S(2)}, u32[]{:S(2)}) collective-permute-start(bf16[2,2,128,128]{3,2,1,0:T(8,128)(2,1)S(1)} %get-tuple-element.60), channel_id=1, source_target_pairs={{4,7},{5,6},{2,1},{3,0},{12,15},{13,14},{10,9},{11,8},{20,23},{21,... | collective-permute-start | bytes 393224 | tf_op jit(solution)/shard_map/ppermute | solution.py:431
  46.4 24.2 %collective-permute-start.15 = (bf16[3,2,128,128]{3,2,1,0:T(8,128)(2,1)S(1)}, bf16[3,2,128,128]{3,2,1,0:T(8,128)(2,1)S(1)}, u32[]{:S(2)}, u32[]{:S(2)}) collective-permute-start(bf16[3,2,128,128]{3,2,1,0:T(8,128)(2,1)S(1)} %get-tuple-element.62), channel_id=1, source_target_pairs={{4,6},{5,7},{2,0},{3,1},{12,14},{13,15},{10,8},{11,9},{20,22},{21,... | collective-permute-start | bytes 589832 | tf_op jit(solution)/shard_map/ppermute | solution.py:431
  58.3 14.6 %collective-permute-start.16 = (bf16[3,2,128,128]{3,2,1,0:T(8,128)(2,1)S(1)}, bf16[3,2,128,128]{3,2,1,0:T(8,128)(2,1)S(1)}, u32[]{:S(2)}, u32[]{:S(2)}) collective-permute-start(bf16[3,2,128,128]{3,2,1,0:T(8,128)(2,1)S(1)} %get-tuple-element.63), channel_id=1, source_target_pairs={{4,7},{5,6},{2,1},{3,0},{12,15},{13,14},{10,9},{11,8},{20,23},{21,... | collective-permute-start | bytes 589832 | tf_op jit(solution)/shard_map/ppermute | solution.py:431
  66.7 10.4 %collective-permute-start.14 = (bf16[4,2,128,128]{3,2,1,0:T(8,128)(2,1)S(1)}, bf16[4,2,128,128]{3,2,1,0:T(8,128)(2,1)S(1)}, u32[]{:S(2)}, u32[]{:S(2)}) collective-permute-start(bf16[4,2,128,128]{3,2,1,0:T(8,128)(2,1)S(1)} %spatial.3.refs_0_), channel_id=1, source_target_pairs={{0,16},{8,24},{1,17},{9,25},{2,18},{10,26},{3,19},{11,27},{4,20},{... | collective-permute-start | bytes 786440 | tf_op jit(solution)/shard_map/ppermute | solution.py:476
  68.0 9.1 %collective-permute-start.13 = (bf16[4,2,128,128]{3,2,1,0:T(8,128)(2,1)S(1)}, bf16[4,2,128,128]{3,2,1,0:T(8,128)(2,1)S(1)}, u32[]{:S(2)}, u32[]{:S(2)}) collective-permute-start(bf16[4,2,128,128]{3,2,1,0:T(8,128)(2,1)S(1)} %spatial.3.refs_0_), channel_id=1, source_target_pairs={{0,8},{16,24},{1,9},{17,25},{2,10},{18,26},{3,11},{19,27},{4,12},{... | collective-permute-start | bytes 786440 | tf_op jit(solution)/shard_map/ppermute | solution.py:476
  69.3 7.9 %collective-permute-start.20 = (bf16[3,2,128,128]{3,2,1,0:T(8,128)(2,1)S(1)}, bf16[3,2,128,128]{3,2,1,0:T(8,128)(2,1)S(1)}, u32[]{:S(2)}, u32[]{:S(2)}) collective-permute-start(bf16[3,2,128,128]{3,2,1,0:T(8,128)(2,1)S(1)} %get-tuple-element.68), channel_id=1, source_target_pairs={{4,6},{5,7},{2,0},{3,1},{12,14},{13,15},{10,8},{11,9},{20,22},{21,... | collective-permute-start | bytes 589832 | tf_op jit(solution)/shard_map/ppermute | solution.py:431
  70.6 8.6 %collective-permute-start.21 = (bf16[3,2,128,128]{3,2,1,0:T(8,128)(2,1)S(1)}, bf16[3,2,128,128]{3,2,1,0:T(8,128)(2,1)S(1)}, u32[]{:S(2)}, u32[]{:S(2)}) collective-permute-start(bf16[3,2,128,128]{3,2,1,0:T(8,128)(2,1)S(1)} %get-tuple-element.69), channel_id=1, source_target_pairs={{4,7},{5,6},{2,1},{3,0},{12,15},{13,14},{10,9},{11,8},{20,23},{21,... | collective-permute-start | bytes 589832 | tf_op jit(solution)/shard_map/ppermute | solution.py:431
  75.8 17.9 %collective-permute-start.19 = (bf16[4,3,128,128]{3,2,1,0:T(8,128)(2,1)S(1)}, bf16[4,3,128,128]{3,2,1,0:T(8,128)(2,1)S(1)}, u32[]{:S(2)}, u32[]{:S(2)}) collective-permute-start(bf16[4,3,128,128]{3,2,1,0:T(8,128)(2,1)S(1)} %spatial.4.refs_1_.refs_4_), channel_id=1, source_target_pairs={{0,16},{8,24},{1,17},{9,25},{2,18},{10,26},{3,19},{11,27},{4,20},{... | collective-permute-start | bytes 1179656 | tf_op jit(solution)/shard_map/ppermute | solution.py:476
  82.2 13.5 %collective-permute-start.24 = (bf16[4,3,128,128]{3,2,1,0:T(8,128)(2,1)S(1)}, bf16[4,3,128,128]{3,2,1,0:T(8,128)(2,1)S(1)}, u32[]{:S(2)}, u32[]{:S(2)}) collective-permute-start(bf16[4,3,128,128]{3,2,1,0:T(8,128)(2,1)S(1)} %spatial.5.refs_2_.refs_8_), channel_id=1, source_target_pairs={{0,16},{8,24},{1,17},{9,25},{2,18},{10,26},{3,19},{11,27},{4,20},{... | collective-permute-start | bytes 1179656 | tf_op jit(solution)/shard_map/ppermute | solution.py:476
  83.5 18.8 %collective-permute-start.18 = (bf16[4,3,128,128]{3,2,1,0:T(8,128)(2,1)S(1)}, bf16[4,3,128,128]{3,2,1,0:T(8,128)(2,1)S(1)}, u32[]{:S(2)}, u32[]{:S(2)}) collective-permute-start(bf16[4,3,128,128]{3,2,1,0:T(8,128)(2,1)S(1)} %spatial.4.refs_1_.refs_4_), channel_id=1, source_target_pairs={{0,8},{16,24},{1,9},{17,25},{2,10},{18,26},{3,11},{19,27},{4,12},{... | collective-permute-start | bytes 1179656 | tf_op jit(solution)/shard_map/ppermute | solution.py:476
  84.8 17.6 %collective-permute-start.23 = (bf16[4,3,128,128]{3,2,1,0:T(8,128)(2,1)S(1)}, bf16[4,3,128,128]{3,2,1,0:T(8,128)(2,1)S(1)}, u32[]{:S(2)}, u32[]{:S(2)}) collective-permute-start(bf16[4,3,128,128]{3,2,1,0:T(8,128)(2,1)S(1)} %spatial.5.refs_2_.refs_8_), channel_id=1, source_target_pairs={{0,8},{16,24},{1,9},{17,25},{2,10},{18,26},{3,11},{19,27},{4,12},{... | collective-permute-start | bytes 1179656 | tf_op jit(solution)/shard_map/ppermute | solution.py:476
  86.1 16.2 %collective-permute-start.17 = (bf16[4,2,128,128]{3,2,1,0:T(8,128)(2,1)S(1)}, bf16[4,2,128,128]{3,2,1,0:T(8,128)(2,1)S(1)}, u32[]{:S(2)}, u32[]{:S(2)}) collective-permute-start(bf16[4,2,128,128]{3,2,1,0:T(8,128)(2,1)S(1)} %collective-permute-done.14.refs_2_), channel_id=1, source_target_pairs={{16,24},{24,16},{17,25},{25,17},{18,26},{26,18},{19,27},{27,19},{2... | collective-permute-start | bytes 786440 | tf_op jit(solution)/shard_map/ppermute | solution.py:486
  93.7 8.6 %collective-permute-start.22 = (bf16[4,3,128,128]{3,2,1,0:T(8,128)(2,1)S(1)}, bf16[4,3,128,128]{3,2,1,0:T(8,128)(2,1)S(1)}, u32[]{:S(2)}, u32[]{:S(2)}) collective-permute-start(bf16[4,3,128,128]{3,2,1,0:T(8,128)(2,1)S(1)} %collective-permute-done.19.refs_6_), channel_id=1, source_target_pairs={{16,24},{24,16},{17,25},{25,17},{18,26},{26,18},{19,27},{27,19},{2... | collective-permute-start | bytes 1179656 | tf_op jit(solution)/shard_map/ppermute | solution.py:486
  95.6 6.7 %collective-permute-start.25 = (bf16[4,3,128,128]{3,2,1,0:T(8,128)(2,1)S(1)}, bf16[4,3,128,128]{3,2,1,0:T(8,128)(2,1)S(1)}, u32[]{:S(2)}, u32[]{:S(2)}) collective-permute-start(bf16[4,3,128,128]{3,2,1,0:T(8,128)(2,1)S(1)} %collective-permute-done.24.refs_10_), channel_id=1, source_target_pairs={{16,24},{24,16},{17,25},{25,17},{18,26},{26,18},{19,27},{27,19},{2... | collective-permute-start | bytes 1179656 | tf_op jit(solution)/shard_map/ppermute | solution.py:486
  (15 other events, 317.9 us)

commit v7 on v5

--- a/solution.py
+++ b/solution.py
@@ -255,12 +255,13 @@
     spans = [slice(d, d + HEADS) for d in range(0, width, HEADS)]
     steep = scales(width)[1]
     q = [q_ref[at, span] for span in spans]
+    scale = scales(width)[0]
     total, acc = sums if sums else (None, None)
     for u in keys:
         raw = q[0] * k_ref[u, spans[0]]
         for d in range(1, len(spans)):
             raw = raw + q[d] * k_ref[u, spans[d]]
-        e = jnp.exp2(steep * jnp.tanh(raw))
+        e = jnp.exp2(steep * jnp.tanh(raw.astype(F32) * scale))
         values = [e * v_ref[u, span] for span in spans]
         total = e if total is None else total + e
         acc = values if acc is None else [one + more for one, more in zip(acc, values)]
@@ -273,7 +274,6 @@
     snaps = sum(sizes)
     g = pl.program_id(0)
     width, lanes = arrays[0].shape[2:]
-    scale = scales(width)[0]
     found = [a[g, s] for a, n in zip(arrays, sizes) for s in range(n)]
     for first in range(0, snaps, 4):
         some = found[first : first + 4]
@@ -281,8 +281,8 @@
         for j in range(len(some)):
             part = got[:, j * lanes : (j + 1) * lanes]
             q_out[0, first + j] = part[:width]
-            q_s[first + j] = part[:width].astype(F32) * scale
-            k_s[first + j] = part[width : 2 * width].astype(F32)
+            q_s[first + j] = part[:width]
+            k_s[first + j] = part[width : 2 * width]
             v_s[first + j] = part[2 * width :].astype(F32)
     for s in range(snaps):
         total, acc = attend(q_s, k_s, v_s, s, range(s + 1), None)
@@ -306,7 +306,7 @@
         grid=(groups,),
         in_specs=[whole(qkv_t)] + [pl.BlockSpec(memory_space=pltpu.VMEM)] * len(arrays),
         out_specs=[pl.BlockSpec((1,) + a.shape[1:], lambda g: (g, 0, 0, 0)) for a in outs],
-        scratch_shapes=[pltpu.VMEM((snaps, width, lanes), F32)] * 3,
+        scratch_shapes=[pltpu.VMEM((snaps, width, lanes), t) for t in (BF16, BF16, F32)],
         out_shape=outs,
         compiler_params=pltpu.CompilerParams(vmem_limit_bytes=VMEM),
         cost_estimate=cost(6),
@@ -321,7 +321,6 @@
     snaps = sum(sizes)
     width, lanes = arrays[0].shape[2:]
     me, g = me_ref[0], pl.program_id(0)
-    scale = scales(width)[0]
     spans = [slice(d, d + HEADS) for d in range(0, width, HEADS)]
 
     def held(i):
@@ -335,13 +334,13 @@
             got = dot(qkv_ref[width:, :], jnp.concatenate(some, axis=1)).astype(BF16).astype(F32)
             for j in range(len(some)):
                 part = got[:, j * lanes : (j + 1) * lanes]
-                k_s[base + first + j] = part[:width]
+                k_s[base + first + j] = part[:width].astype(BF16)
                 v_s[base + first + j] = part[width:]
 
     for i in range(1, count):
         pl.when((me ^ i) < me)(functools.partial(project, i))
     for at in range(snaps):
-        q_s[at] = q_ref[g, at].astype(F32) * scale
+        q_s[at] = q_ref[g, at]
         acc_s[at] = acc_ref[g, at]
         total_s[at] = total_ref[g, at]
 
@@ -392,9 +391,9 @@
             + [pl.BlockSpec(memory_space=pltpu.VMEM)] * len(parts),
             out_specs=pl.BlockSpec((snaps, lanes, width), lambda g, i: (0, g, 0)),
             scratch_shapes=[
+                pltpu.VMEM((snaps * count, width, lanes), BF16),
                 pltpu.VMEM((snaps * count, width, lanes), F32),
-                pltpu.VMEM((snaps * count, width, lanes), F32),
-                pltpu.VMEM((snaps, width, lanes), F32),
+                pltpu.VMEM((snaps, width, lanes), BF16),
                 pltpu.VMEM((snaps, width, lanes), F32),
                 pltpu.VMEM((snaps, HEADS, lanes), F32),
                 pltpu.VMEM((width, snaps * lanes), BF16),

time: 120 us -> 121 us (level)
  no operation moved by 1% of the time
where the time goes in v7:
time: 121 us; the launch traced here: 120 us
  starting transfers between devices  44.7 us (37%)
  waiting for transfers between devices  38.3 us (32%)
  Pallas kernels  34 us (28%)
  local copies, waits for them, and re-layouts  1.29 us (1%)
  other arithmetic  1.24 us (1%)
    ppermute x13, waiting for transfers between devices, exchange_forward(): go = lambda a, pairs, x=0: lax.ppermute(a, 'vert', layers(pairs, x))  29.9 us
    pallas_call x1, Pallas kernels, temporal(): pl.pallas_call(functools.partial(temporal_kernel, sizes, count - 1), grid...  17.4 us
    ppermute x13, starting transfers between devices, exchange_forward(): go = lambda a, pairs, x=0: lax.ppermute(a, 'vert', layers(pairs, x))  15.3 us
    ppermute x3, starting transfers between devices, pass_on(): got[k] = lax.ppermute(got[k - 1], 'tm', pairs)  14 us
    ppermute x4, waiting for transfers between devices, send(): lax.ppermute(a, 'vert', [(v, v ^ k) for v in range(lax.axis_size('vert'))])  8.45 us
    pallas_call x3, Pallas kernels, spatial(): pl.pallas_call(functools.partial(spatial_kernel, start, [first for _, fir...  8.21 us
    ppermute x6, starting transfers between devices, gather_times(): got[k] = lax.ppermute(own, 'tm', pairs)  7.75 us
    ppermute x4, starting transfers between devices, send(): lax.ppermute(a, 'vert', [(v, v ^ k) for v in range(lax.axis_size('vert'))])  7.6 us
  transfers between devices with their start and end apart: 26, of which 10 were waited for; matrix products, arithmetic and copies ran while one was open for 1% of the time, Pallas kernels for 14%

profile of v7, /device:TPU:5, one launch (start us, length us, event | category | flops | bytes accessed | tf_op | source)
XLA Modules:
  0.0 120.0 jit_solution(9376108922749684305)
XLA Ops:
  0.7 3.8 %collective-permute-start = (bf16[8,4,128,128]{3,2,1,0:T(8,128)(2,1)}, bf16[8,4,128,128]{3,2,1,0:T(8,128)(2,1)S(1)}, u32[]{:S(2)}, u32[]{:S(2)}) collective-permute-start(bf16[8,4,128,128]{3,2,1,0:T(8,128)(2,1)} %bitcast.7), channel_id=1, source_target_pairs={{0,2},{1,3},{2,0},{3,1},{4,6},{5,7},{6,4},{7,5},{8,10},{9,11},{10,... | collective-permute-start | bytes 3145736 | tf_op jit(solution)/shard_map/ppermute | solution.py:410
  5.2 2.7 %lists.1 = (s32[8,1,16]{2,1,0:T(1,128)}, s32[8,4,8]{2,1,0:T(4,128)}) custom-call(s32[2]{0:T(128)} %pad_add_fusion.1.at_ref, s32[8,4,8]{2,1,0:T(4,128)} %cols_ref.1), custom_call_target="tpu_custom_call" | custom-call | flops 1150000000 | bytes 1024 | tf_op jit(solution)/shard_map/lists/pallas_call | solution.py:82
  9.0 1.8 %collective-permute-done.1.refs_0_ = s32[8,1,16]{2,1,0:T(1,128)S(1)} collective-permute-done((s32[8,1,16]{2,1,0:T(1,128)}, s32[8,1,16]{2,1,0:T(1,128)S(1)}, u32[]{:S(2)}, u32[]{:S(2)}) %collective-permute-start.1) | collective-permute-done | bytes 544 | tf_op jit(solution)/shard_map/ppermute | solution.py:410
  14.6 1.9 %collective-permute-start.2 = (s32[8,2,16]{2,1,0:T(2,128)S(1)}, s32[8,2,16]{2,1,0:T(2,128)S(1)}, u32[]{:S(2)}, u32[]{:S(2)}) collective-permute-start(s32[8,2,16]{2,1,0:T(2,128)S(1)} %pad_add_fusion), channel_id=1, source_target_pairs={{6,4},{7,5},{0,2},{1,3},{14,12},{15,13},{8,10},{9,11},{22,20},{23,... | collective-permute-start | bytes 3080 | tf_op jit(solution)/shard_map/ppermute | solution.py:430
  16.6 9.9 %collective-permute-done.2 = s32[8,2,16]{2,1,0:T(2,128)S(1)} collective-permute-done((s32[8,2,16]{2,1,0:T(2,128)S(1)}, s32[8,2,16]{2,1,0:T(2,128)S(1)}, u32[]{:S(2)}, u32[]{:S(2)}) %collective-permute-start.2) | collective-permute-done | bytes 1056 | tf_op jit(solution)/shard_map/ppermute | solution.py:430
  31.0 1.3 %collective-permute-start.9 = (bf16[8,2,128,128]{3,2,1,0:T(8,128)(2,1)S(1)}, bf16[8,2,128,128]{3,2,1,0:T(8,128)(2,1)S(1)}, u32[]{:S(2)}, u32[]{:S(2)}) collective-permute-start(bf16[8,2,128,128]{3,2,1,0:T(8,128)(2,1)S(1)} %get-tuple-element.55), channel_id=1, source_target_pairs={{4,6},{5,7},{2,0},{3,1},{12,14},{13,15},{10,8},{11,9},{20,22},{21,... | collective-permute-start | bytes 1572872 | tf_op jit(solution)/shard_map/ppermute | solution.py:430
  32.3 1.3 %collective-permute-start.10 = (bf16[8,2,128,128]{3,2,1,0:T(8,128)(2,1)S(1)}, bf16[8,2,128,128]{3,2,1,0:T(8,128)(2,1)S(1)}, u32[]{:S(2)}, u32[]{:S(2)}) collective-permute-start(bf16[8,2,128,128]{3,2,1,0:T(8,128)(2,1)S(1)} %get-tuple-element.56), channel_id=1, source_target_pairs={{4,7},{5,6},{2,1},{3,0},{12,15},{13,14},{10,9},{11,8},{20,23},{21,... | collective-permute-start | bytes 1572872 | tf_op jit(solution)/shard_map/ppermute | solution.py:430
  35.1 5.8 %collective-permute-done.6.refs_5_ = bf16[8,2,128,128]{3,2,1,0:T(8,128)(2,1)S(1)} collective-permute-done((bf16[8,2,128,128]{3,2,1,0:T(8,128)(2,1)S(1)}, bf16[8,2,128,128]{3,2,1,0:T(8,128)(2,1)S(1)}, u32[]{:S(2)}, u32[]{:S(2)}) %collective-permute-start.6) | collective-permute-done | bytes 524320 | tf_op jit(solution)/shard_map/ppermute | solution.py:410
  40.9 1.5 %collective-permute-start.11 = (bf16[2,2,128,128]{3,2,1,0:T(8,128)(2,1)S(1)}, bf16[2,2,128,128]{3,2,1,0:T(8,128)(2,1)S(1)}, u32[]{:S(2)}, u32[]{:S(2)}) collective-permute-start(bf16[2,2,128,128]{3,2,1,0:T(8,128)(2,1)S(1)} %get-tuple-element.57), channel_id=1, source_target_pairs={{4,6},{5,7},{2,0},{3,1},{12,14},{13,15},{10,8},{11,9},{20,22},{21,... | collective-permute-start | bytes 393224 | tf_op jit(solution)/shard_map/ppermute | solution.py:430
  42.5 1.3 %collective-permute-start.12 = (bf16[2,2,128,128]{3,2,1,0:T(8,128)(2,1)S(1)}, bf16[2,2,128,128]{3,2,1,0:T(8,128)(2,1)S(1)}, u32[]{:S(2)}, u32[]{:S(2)}) collective-permute-start(bf16[2,2,128,128]{3,2,1,0:T(8,128)(2,1)S(1)} %get-tuple-element.58), channel_id=1, source_target_pairs={{4,7},{5,6},{2,1},{3,0},{12,15},{13,14},{10,9},{11,8},{20,23},{21,... | collective-permute-start | bytes 393224 | tf_op jit(solution)/shard_map/ppermute | solution.py:430
  44.7 1.4 %collective-permute-done.9.refs_8_ = bf16[8,2,128,128]{3,2,1,0:T(8,128)(2,1)S(1)} collective-permute-done((bf16[8,2,128,128]{3,2,1,0:T(8,128)(2,1)S(1)}, bf16[8,2,128,128]{3,2,1,0:T(8,128)(2,1)S(1)}, u32[]{:S(2)}, u32[]{:S(2)}) %collective-permute-start.9) | collective-permute-done | bytes 524320 | tf_op jit(solution)/shard_map/ppermute | solution.py:430
  47.4 10.7 %collective-permute-done.10.refs_9_ = bf16[8,2,128,128]{3,2,1,0:T(8,128)(2,1)S(1)} collective-permute-done((bf16[8,2,128,128]{3,2,1,0:T(8,128)(2,1)S(1)}, bf16[8,2,128,128]{3,2,1,0:T(8,128)(2,1)S(1)}, u32[]{:S(2)}, u32[]{:S(2)}) %collective-permute-start.10) | collective-permute-done | bytes 524320 | tf_op jit(solution)/shard_map/ppermute | solution.py:430
  59.4 2.3 %collective-permute-done.11.refs_10_ = bf16[2,2,128,128]{3,2,1,0:T(8,128)(2,1)S(1)} collective-permute-done((bf16[2,2,128,128]{3,2,1,0:T(8,128)(2,1)S(1)}, bf16[2,2,128,128]{3,2,1,0:T(8,128)(2,1)S(1)}, u32[]{:S(2)}, u32[]{:S(2)}) %collective-permute-start.11) | collective-permute-done | bytes 131104 | tf_op jit(solution)/shard_map/ppermute | solution.py:430
  61.7 2.3 %collective-permute-done.12.refs_11_ = bf16[2,2,128,128]{3,2,1,0:T(8,128)(2,1)S(1)} collective-permute-done((bf16[2,2,128,128]{3,2,1,0:T(8,128)(2,1)S(1)}, bf16[2,2,128,128]{3,2,1,0:T(8,128)(2,1)S(1)}, u32[]{:S(2)}, u32[]{:S(2)}) %collective-permute-start.12) | collective-permute-done | bytes 131104 | tf_op jit(solution)/shard_map/ppermute | solution.py:430
  64.0 2.2 %spatial.3.refs_0_ = bf16[4,2,128,128]{3,2,1,0:T(8,128)(2,1)S(1)} custom-call(s32[8,4,8]{2,1,0:T(4,128)S(1)} %copy-done.2, bf16[8,4,8,128,128]{4,3,2,1,0:T(8,128)(2,1)S(1)} %bitcast.5, bf16[128,128]{1,0:T(8,128)(2,1)S(1)} %get-tuple-element.45.weight_ref, f32[8,128]{1,0:T(8,128)S(1)} %get-tuple-element.46.pos_ref, bf16[8,4,128,128]{3,2,1,0:T(8,128)(2,1)S(1)} %bitcast.9, ...), custom_call_target="tpu_custom_call" | custom-call | flops 2300000000 | bytes 1024 | tf_op jit(solution)/shard_map/spatial/pallas_call | solution.py:226
  70.2 1.3 %collective-permute-start.21 = (bf16[3,2,128,128]{3,2,1,0:T(8,128)(2,1)S(1)}, bf16[3,2,128,128]{3,2,1,0:T(8,128)(2,1)S(1)}, u32[]{:S(2)}, u32[]{:S(2)}) collective-permute-start(bf16[3,2,128,128]{3,2,1,0:T(8,128)(2,1)S(1)} %get-tuple-element.67), channel_id=1, source_target_pairs={{4,7},{5,6},{2,1},{3,0},{12,15},{13,14},{10,9},{11,8},{20,23},{21,... | collective-permute-start | bytes 589832 | tf_op jit(solution)/shard_map/ppermute | solution.py:430
  72.4 3.0 %spatial.4.refs_1_.refs_4_ = bf16[4,3,128,128]{3,2,1,0:T(8,128)(2,1)S(1)} custom-call(s32[8,4,8]{2,1,0:T(4,128)S(1)} %copy-done.2, bf16[8,4,8,128,128]{4,3,2,1,0:T(8,128)(2,1)S(1)} %bitcast.5, bf16[128,128]{1,0:T(8,128)(2,1)S(1)} %get-tuple-element.45.weight_ref, f32[8,128]{1,0:T(8,128)S(1)} %get-tuple-element.46.pos_ref, ...), custom_call_target="tpu_custom_call" | custom-call | flops 3449999872 | bytes 1024 | tf_op jit(solution)/shard_map/spatial/pallas_call | solution.py:226
  76.7 2.3 %collective-permute-done.21.refs_11_ = bf16[3,2,128,128]{3,2,1,0:T(8,128)(2,1)S(1)} collective-permute-done((bf16[3,2,128,128]{3,2,1,0:T(8,128)(2,1)S(1)}, bf16[3,2,128,128]{3,2,1,0:T(8,128)(2,1)S(1)}, u32[]{:S(2)}, u32[]{:S(2)}) %collective-permute-start.21) | collective-permute-done | bytes 196640 | tf_op jit(solution)/shard_map/ppermute | solution.py:430
  79.0 3.0 %spatial.5.refs_2_.refs_8_ = bf16[4,3,128,128]{3,2,1,0:T(8,128)(2,1)S(1)} custom-call(s32[8,4,8]{2,1,0:T(4,128)S(1)} %copy-done.2, bf16[8,4,8,128,128]{4,3,2,1,0:T(8,128)(2,1)S(1)} %bitcast.5, bf16[128,128]{1,0:T(8,128)(2,1)S(1)} %get-tuple-element.45.weight_ref, f32[8,128]{1,0:T(8,128)S(1)} %get-tuple-element.46.pos_ref, ...), custom_call_target="tpu_custom_call" | custom-call | flops 3449999872 | bytes 1024 | tf_op jit(solution)/shard_map/spatial/pallas_call | solution.py:226
  85.9 7.6 %collective-permute-start.17 = (bf16[4,2,128,128]{3,2,1,0:T(8,128)(2,1)S(1)}, bf16[4,2,128,128]{3,2,1,0:T(8,128)(2,1)S(1)}, u32[]{:S(2)}, u32[]{:S(2)}) collective-permute-start(bf16[4,2,128,128]{3,2,1,0:T(8,128)(2,1)S(1)} %collective-permute-done.14.refs_2_), channel_id=1, source_target_pairs={{16,24},{24,16},{17,25},{25,17},{18,26},{26,18},{19,27},{27,19},{2... | collective-permute-start | bytes 786440 | tf_op jit(solution)/shard_map/ppermute | solution.py:485
  93.5 1.9 %collective-permute-start.22 = (bf16[4,3,128,128]{3,2,1,0:T(8,128)(2,1)S(1)}, bf16[4,3,128,128]{3,2,1,0:T(8,128)(2,1)S(1)}, u32[]{:S(2)}, u32[]{:S(2)}) collective-permute-start(bf16[4,3,128,128]{3,2,1,0:T(8,128)(2,1)S(1)} %collective-permute-done.19.refs_6_), channel_id=1, source_target_pairs={{16,24},{24,16},{17,25},{25,17},{18,26},{26,18},{19,27},{27,19},{2... | collective-permute-start | bytes 1179656 | tf_op jit(solution)/shard_map/ppermute | solution.py:485
  95.4 4.5 %collective-permute-start.25 = (bf16[4,3,128,128]{3,2,1,0:T(8,128)(2,1)S(1)}, bf16[4,3,128,128]{3,2,1,0:T(8,128)(2,1)S(1)}, u32[]{:S(2)}, u32[]{:S(2)}) collective-permute-start(bf16[4,3,128,128]{3,2,1,0:T(8,128)(2,1)S(1)} %collective-permute-done.24.refs_10_), channel_id=1, source_target_pairs={{16,24},{24,16},{17,25},{25,17},{18,26},{26,18},{19,27},{27,19},{2... | collective-permute-start | bytes 1179656 | tf_op jit(solution)/shard_map/ppermute | solution.py:485
  100.0 2.5 %temporal_own.1 = (bf16[4,8,128,128]{3,2,1,0:T(8,128)(2,1)S(1)}, f32[4,8,128,128]{3,2,1,0:T(8,128)S(1)}, f32[4,8,16,128]{3,2,1,0:T(8,128)S(1)}) custom-call(bf16[384,128]{1,0:T(8,128)(2,1)S(1)} %get-tuple-element.39.qkv_ref, bf16[4,2,128,128]{3,2,1,0:T(8,128)(2,1)S(1)} %spatial.3.refs_0_, bf16[4,3,128,128]{3,2,1,0:T(8,128)(2,1)S(1)} %spatial.4.refs_1_.refs_4_, ...), custom_call_target="tpu_custom_call" | custom-call | flops 6899999744 | bytes 1024 | tf_op jit(solution)/shard_map/temporal_own/pallas_call | solution.py:304
  102.6 17.4 %temporal.1 = bf16[8,512,128]{2,1,0:T(8,128)(2,1)} custom-call(s32[1]{0:T(128)} %bitcast.me_ref, bf16[384,128]{1,0:T(8,128)(2,1)S(1)} %get-tuple-element.39.qkv_ref, bf16[128,128]{1,0:T(8,128)(2,1)S(1)} %get-tuple-element.40.proj_ref, f32[128,128]{1,0:T(8,128)S(1)} %get-tuple-element.41.gain_ref, bf16[512,128]{1,0:T(8,128)(2,1)S(1)} %get-tuple-element.42.up_ref, ...), custom_call_target="tpu_custom_call" | custom-call | flops 11500000256 | bytes 1024 | tf_op jit(solution)/shard_map/temporal/pallas_call | solution.py:385
  (68 shorter events, 25.7 us)
Async XLA Ops:
  0.0 26.5 %collective-permute-start.4 = (bf16[8,4,128,128]{3,2,1,0:T(8,128)(2,1)}, bf16[8,4,128,128]{3,2,1,0:T(8,128)(2,1)S(1)}, u32[]{:S(2)}, u32[]{:S(2)}) collective-permute-start(bf16[8,4,128,128]{3,2,1,0:T(8,128)(2,1)} %bitcast.6), channel_id=1, source_target_pairs={{2,4},{3,5},{4,2},{5,3},{10,12},{11,13},{12,10},{13,11},{18,20},{1... | collective-permute-start | bytes 3145736 | tf_op jit(solution)/shard_map/ppermute | solution.py:430
  0.7 26.6 %collective-permute-start = (bf16[8,4,128,128]{3,2,1,0:T(8,128)(2,1)}, bf16[8,4,128,128]{3,2,1,0:T(8,128)(2,1)S(1)}, u32[]{:S(2)}, u32[]{:S(2)}) collective-permute-start(bf16[8,4,128,128]{3,2,1,0:T(8,128)(2,1)} %bitcast.7), channel_id=1, source_target_pairs={{0,2},{1,3},{2,0},{3,1},{4,6},{5,7},{6,4},{7,5},{8,10},{9,11},{10,... | collective-permute-start | bytes 3145736 | tf_op jit(solution)/shard_map/ppermute | solution.py:410
  12.7 13.8 %collective-permute-start.3 = (bf16[8,2,128,128]{3,2,1,0:T(8,128)(2,1)S(1)}, bf16[8,2,128,128]{3,2,1,0:T(8,128)(2,1)S(1)}, u32[]{:S(2)}, u32[]{:S(2)}) collective-permute-start(bf16[8,2,128,128]{3,2,1,0:T(8,128)(2,1)S(1)} %pick_blocks.3), channel_id=1, source_target_pairs={{0,1},{1,0},{2,3},{3,2},{4,5},{5,4},{6,7},{7,6},{8,9},{9,8},{10,11... | collective-permute-start | bytes 1572872 | tf_op jit(solution)/shard_map/ppermute | solution.py:410
  14.6 11.8 %collective-permute-start.2 = (s32[8,2,16]{2,1,0:T(2,128)S(1)}, s32[8,2,16]{2,1,0:T(2,128)S(1)}, u32[]{:S(2)}, u32[]{:S(2)}) collective-permute-start(s32[8,2,16]{2,1,0:T(2,128)S(1)} %pad_add_fusion), channel_id=1, source_target_pairs={{6,4},{7,5},{0,2},{1,3},{14,12},{15,13},{8,10},{9,11},{22,20},{23,... | collective-permute-start | bytes 3080 | tf_op jit(solution)/shard_map/ppermute | solution.py:430
  29.0 11.9 %collective-permute-start.6 = (bf16[8,2,128,128]{3,2,1,0:T(8,128)(2,1)S(1)}, bf16[8,2,128,128]{3,2,1,0:T(8,128)(2,1)S(1)}, u32[]{:S(2)}, u32[]{:S(2)}) collective-permute-start(bf16[8,2,128,128]{3,2,1,0:T(8,128)(2,1)S(1)} %get-tuple-element.52), channel_id=1, source_target_pairs={{0,1},{1,0},{2,3},{3,2},{4,5},{5,4},{6,7},{7,6},{8,9},{9,8},{10,11... | collective-permute-start | bytes 1572872 | tf_op jit(solution)/shard_map/ppermute | solution.py:410
  30.3 12.2 %collective-permute-start.7 = (bf16[8,2,128,128]{3,2,1,0:T(8,128)(2,1)S(1)}, bf16[8,2,128,128]{3,2,1,0:T(8,128)(2,1)S(1)}, u32[]{:S(2)}, u32[]{:S(2)}) collective-permute-start(bf16[8,2,128,128]{3,2,1,0:T(8,128)(2,1)S(1)} %get-tuple-element.53), channel_id=1, source_target_pairs={{2,3},{3,2},{4,5},{5,4},{10,11},{11,10},{12,13},{13,12},{18,19},{1... | collective-permute-start | bytes 1572872 | tf_op jit(solution)/shard_map/ppermute | solution.py:430
  31.0 15.1 %collective-permute-start.9 = (bf16[8,2,128,128]{3,2,1,0:T(8,128)(2,1)S(1)}, bf16[8,2,128,128]{3,2,1,0:T(8,128)(2,1)S(1)}, u32[]{:S(2)}, u32[]{:S(2)}) collective-permute-start(bf16[8,2,128,128]{3,2,1,0:T(8,128)(2,1)S(1)} %get-tuple-element.55), channel_id=1, source_target_pairs={{4,6},{5,7},{2,0},{3,1},{12,14},{13,15},{10,8},{11,9},{20,22},{21,... | collective-permute-start | bytes 1572872 | tf_op jit(solution)/shard_map/ppermute | solution.py:430
  32.3 25.8 %collective-permute-start.10 = (bf16[8,2,128,128]{3,2,1,0:T(8,128)(2,1)S(1)}, bf16[8,2,128,128]{3,2,1,0:T(8,128)(2,1)S(1)}, u32[]{:S(2)}, u32[]{:S(2)}) collective-permute-start(bf16[8,2,128,128]{3,2,1,0:T(8,128)(2,1)S(1)} %get-tuple-element.56), channel_id=1, source_target_pairs={{4,7},{5,6},{2,1},{3,0},{12,15},{13,14},{10,9},{11,8},{20,23},{21,... | collective-permute-start | bytes 1572872 | tf_op jit(solution)/shard_map/ppermute | solution.py:430
  34.4 29.6 %collective-permute-start.8 = (bf16[8,2,128,128]{3,2,1,0:T(8,128)(2,1)S(1)}, bf16[8,2,128,128]{3,2,1,0:T(8,128)(2,1)S(1)}, u32[]{:S(2)}, u32[]{:S(2)}) collective-permute-start(bf16[8,2,128,128]{3,2,1,0:T(8,128)(2,1)S(1)} %get-tuple-element.54), channel_id=1, source_target_pairs={{2,3},{3,2},{4,5},{5,4},{10,11},{11,10},{12,13},{13,12},{18,19},{1... | collective-permute-start | bytes 1572872 | tf_op jit(solution)/shard_map/ppermute | solution.py:430
  40.9 20.7 %collective-permute-start.11 = (bf16[2,2,128,128]{3,2,1,0:T(8,128)(2,1)S(1)}, bf16[2,2,128,128]{3,2,1,0:T(8,128)(2,1)S(1)}, u32[]{:S(2)}, u32[]{:S(2)}) collective-permute-start(bf16[2,2,128,128]{3,2,1,0:T(8,128)(2,1)S(1)} %get-tuple-element.57), channel_id=1, source_target_pairs={{4,6},{5,7},{2,0},{3,1},{12,14},{13,15},{10,8},{11,9},{20,22},{21,... | collective-permute-start | bytes 393224 | tf_op jit(solution)/shard_map/ppermute | solution.py:430
  42.5 21.5 %collective-permute-start.12 = (bf16[2,2,128,128]{3,2,1,0:T(8,128)(2,1)S(1)}, bf16[2,2,128,128]{3,2,1,0:T(8,128)(2,1)S(1)}, u32[]{:S(2)}, u32[]{:S(2)}) collective-permute-start(bf16[2,2,128,128]{3,2,1,0:T(8,128)(2,1)S(1)} %get-tuple-element.58), channel_id=1, source_target_pairs={{4,7},{5,6},{2,1},{3,0},{12,15},{13,14},{10,9},{11,8},{20,23},{21,... | collective-permute-start | bytes 393224 | tf_op jit(solution)/shard_map/ppermute | solution.py:430
  46.1 24.1 %collective-permute-start.15 = (bf16[3,2,128,128]{3,2,1,0:T(8,128)(2,1)S(1)}, bf16[3,2,128,128]{3,2,1,0:T(8,128)(2,1)S(1)}, u32[]{:S(2)}, u32[]{:S(2)}) collective-permute-start(bf16[3,2,128,128]{3,2,1,0:T(8,128)(2,1)S(1)} %get-tuple-element.60), channel_id=1, source_target_pairs={{4,6},{5,7},{2,0},{3,1},{12,14},{13,15},{10,8},{11,9},{20,22},{21,... | collective-permute-start | bytes 589832 | tf_op jit(solution)/shard_map/ppermute | solution.py:430
  58.1 14.3 %collective-permute-start.16 = (bf16[3,2,128,128]{3,2,1,0:T(8,128)(2,1)S(1)}, bf16[3,2,128,128]{3,2,1,0:T(8,128)(2,1)S(1)}, u32[]{:S(2)}, u32[]{:S(2)}) collective-permute-start(bf16[3,2,128,128]{3,2,1,0:T(8,128)(2,1)S(1)} %get-tuple-element.61), channel_id=1, source_target_pairs={{4,7},{5,6},{2,1},{3,0},{12,15},{13,14},{10,9},{11,8},{20,23},{21,... | collective-permute-start | bytes 589832 | tf_op jit(solution)/shard_map/ppermute | solution.py:430
  66.3 10.4 %collective-permute-start.14 = (bf16[4,2,128,128]{3,2,1,0:T(8,128)(2,1)S(1)}, bf16[4,2,128,128]{3,2,1,0:T(8,128)(2,1)S(1)}, u32[]{:S(2)}, u32[]{:S(2)}) collective-permute-start(bf16[4,2,128,128]{3,2,1,0:T(8,128)(2,1)S(1)} %spatial.3.refs_0_), channel_id=1, source_target_pairs={{0,16},{8,24},{1,17},{9,25},{2,18},{10,26},{3,19},{11,27},{4,20},{... | collective-permute-start | bytes 786440 | tf_op jit(solution)/shard_map/ppermute | solution.py:475
  67.6 9.1 %collective-permute-start.13 = (bf16[4,2,128,128]{3,2,1,0:T(8,128)(2,1)S(1)}, bf16[4,2,128,128]{3,2,1,0:T(8,128)(2,1)S(1)}, u32[]{:S(2)}, u32[]{:S(2)}) collective-permute-start(bf16[4,2,128,128]{3,2,1,0:T(8,128)(2,1)S(1)} %spatial.3.refs_0_), channel_id=1, source_target_pairs={{0,8},{16,24},{1,9},{17,25},{2,10},{18,26},{3,11},{19,27},{4,12},{... | collective-permute-start | bytes 786440 | tf_op jit(solution)/shard_map/ppermute | solution.py:475
  68.9 7.9 %collective-permute-start.20 = (bf16[3,2,128,128]{3,2,1,0:T(8,128)(2,1)S(1)}, bf16[3,2,128,128]{3,2,1,0:T(8,128)(2,1)S(1)}, u32[]{:S(2)}, u32[]{:S(2)}) collective-permute-start(bf16[3,2,128,128]{3,2,1,0:T(8,128)(2,1)S(1)} %get-tuple-element.66), channel_id=1, source_target_pairs={{4,6},{5,7},{2,0},{3,1},{12,14},{13,15},{10,8},{11,9},{20,22},{21,... | collective-permute-start | bytes 589832 | tf_op jit(solution)/shard_map/ppermute | solution.py:430
  70.2 8.8 %collective-permute-start.21 = (bf16[3,2,128,128]{3,2,1,0:T(8,128)(2,1)S(1)}, bf16[3,2,128,128]{3,2,1,0:T(8,128)(2,1)S(1)}, u32[]{:S(2)}, u32[]{:S(2)}) collective-permute-start(bf16[3,2,128,128]{3,2,1,0:T(8,128)(2,1)S(1)} %get-tuple-element.67), channel_id=1, source_target_pairs={{4,7},{5,6},{2,1},{3,0},{12,15},{13,14},{10,9},{11,8},{20,23},{21,... | collective-permute-start | bytes 589832 | tf_op jit(solution)/shard_map/ppermute | solution.py:430
  75.4 18.1 %collective-permute-start.19 = (bf16[4,3,128,128]{3,2,1,0:T(8,128)(2,1)S(1)}, bf16[4,3,128,128]{3,2,1,0:T(8,128)(2,1)S(1)}, u32[]{:S(2)}, u32[]{:S(2)}) collective-permute-start(bf16[4,3,128,128]{3,2,1,0:T(8,128)(2,1)S(1)} %spatial.4.refs_1_.refs_4_), channel_id=1, source_target_pairs={{0,16},{8,24},{1,17},{9,25},{2,18},{10,26},{3,19},{11,27},{4,20},{... | collective-permute-start | bytes 1179656 | tf_op jit(solution)/shard_map/ppermute | solution.py:475
  82.0 13.4 %collective-permute-start.24 = (bf16[4,3,128,128]{3,2,1,0:T(8,128)(2,1)S(1)}, bf16[4,3,128,128]{3,2,1,0:T(8,128)(2,1)S(1)}, u32[]{:S(2)}, u32[]{:S(2)}) collective-permute-start(bf16[4,3,128,128]{3,2,1,0:T(8,128)(2,1)S(1)} %spatial.5.refs_2_.refs_8_), channel_id=1, source_target_pairs={{0,16},{8,24},{1,17},{9,25},{2,18},{10,26},{3,19},{11,27},{4,20},{... | collective-permute-start | bytes 1179656 | tf_op jit(solution)/shard_map/ppermute | solution.py:475
  83.3 19.2 %collective-permute-start.18 = (bf16[4,3,128,128]{3,2,1,0:T(8,128)(2,1)S(1)}, bf16[4,3,128,128]{3,2,1,0:T(8,128)(2,1)S(1)}, u32[]{:S(2)}, u32[]{:S(2)}) collective-permute-start(bf16[4,3,128,128]{3,2,1,0:T(8,128)(2,1)S(1)} %spatial.4.refs_1_.refs_4_), channel_id=1, source_target_pairs={{0,8},{16,24},{1,9},{17,25},{2,10},{18,26},{3,11},{19,27},{4,12},{... | collective-permute-start | bytes 1179656 | tf_op jit(solution)/shard_map/ppermute | solution.py:475
  84.6 17.9 %collective-permute-start.23 = (bf16[4,3,128,128]{3,2,1,0:T(8,128)(2,1)S(1)}, bf16[4,3,128,128]{3,2,1,0:T(8,128)(2,1)S(1)}, u32[]{:S(2)}, u32[]{:S(2)}) collective-permute-start(bf16[4,3,128,128]{3,2,1,0:T(8,128)(2,1)S(1)} %spatial.5.refs_2_.refs_8_), channel_id=1, source_target_pairs={{0,8},{16,24},{1,9},{17,25},{2,10},{18,26},{3,11},{19,27},{4,12},{... | collective-permute-start | bytes 1179656 | tf_op jit(solution)/shard_map/ppermute | solution.py:475
  85.9 16.6 %collective-permute-start.17 = (bf16[4,2,128,128]{3,2,1,0:T(8,128)(2,1)S(1)}, bf16[4,2,128,128]{3,2,1,0:T(8,128)(2,1)S(1)}, u32[]{:S(2)}, u32[]{:S(2)}) collective-permute-start(bf16[4,2,128,128]{3,2,1,0:T(8,128)(2,1)S(1)} %collective-permute-done.14.refs_2_), channel_id=1, source_target_pairs={{16,24},{24,16},{17,25},{25,17},{18,26},{26,18},{19,27},{27,19},{2... | collective-permute-start | bytes 786440 | tf_op jit(solution)/shard_map/ppermute | solution.py:485
  93.5 9.1 %collective-permute-start.22 = (bf16[4,3,128,128]{3,2,1,0:T(8,128)(2,1)S(1)}, bf16[4,3,128,128]{3,2,1,0:T(8,128)(2,1)S(1)}, u32[]{:S(2)}, u32[]{:S(2)}) collective-permute-start(bf16[4,3,128,128]{3,2,1,0:T(8,128)(2,1)S(1)} %collective-permute-done.19.refs_6_), channel_id=1, source_target_pairs={{16,24},{24,16},{17,25},{25,17},{18,26},{26,18},{19,27},{27,19},{2... | collective-permute-start | bytes 1179656 | tf_op jit(solution)/shard_map/ppermute | solution.py:485
  95.4 7.1 %collective-permute-start.25 = (bf16[4,3,128,128]{3,2,1,0:T(8,128)(2,1)S(1)}, bf16[4,3,128,128]{3,2,1,0:T(8,128)(2,1)S(1)}, u32[]{:S(2)}, u32[]{:S(2)}) collective-permute-start(bf16[4,3,128,128]{3,2,1,0:T(8,128)(2,1)S(1)} %collective-permute-done.24.refs_10_), channel_id=1, source_target_pairs={{16,24},{24,16},{17,25},{25,17},{18,26},{26,18},{19,27},{27,19},{2... | collective-permute-start | bytes 1179656 | tf_op jit(solution)/shard_map/ppermute | solution.py:485
  (15 other events, 450.8 us)
